TPU v7x, 32 devices: a whole 2x2x4 slice. The times are simulated.
32 devices in a mesh: bulk: 16 (over z, x, core), span: 2 (over y).
Axes of the slice: x: 2, y: 2, z: 4, core: 2. Of those that a mesh axis runs over, the one named last changes fastest.
Arguments:
- snapshots: float32 [65536, 128], P(('span', 'bulk'))
- jac_blocks: bfloat16 [512, 4, 128, 128], P(('span', 'bulk'))
- jac_cols: int32 [512, 4], P(('span', 'bulk')), may hold values from 0 to 511, as said below
Outputs:
- modes: float32 [65536, 128], P(('span', 'bulk'))
- factor: float32 [128, 128], replicated
- jac_modes: bfloat16 [65536, 128], P(('span', 'bulk'))
- reduced: float32 [128, 128], replicated
Inputs may be any that keep to these rules, and one draw needn't show every extreme that they name: jac_cols[r, 0] = r. Every column block lies in the die region of r (aligned runs of 256 block rows) and within 16 block rows of the shard of 16 block rows that holds r.
All inputs are finite; a program needn't handle non-finite values.
Results may differ from a plain program's by a relative error of at most 0.0029.
The roundings to bfloat16 on the way count: a program that leaves them out, or rounds other values in their place, can miss the bound.
Values may be sent and summed in bfloat16 or wider, within the bound.
No kernel may reach another device: no remote copies, remote signals or barrier semaphores. Data moves between devices by JAX's collectives and lax.ppermute only.
A program may use at most 64 MiB of HBM per device.

v0:
```python
import jax
import jax.numpy as jnp
from jax import lax
from jax.sharding import PartitionSpec as P


def with_halo(array, sides, width):
    for axis, dim in sides:
        size, length = (lax.axis_size(axis), array.shape[dim])
        up = [(i, (i + 1) % size) for i in range(size - 1)]
        down = [(j, i) for i, j in up]
        last = lax.slice_in_dim(array, length - width, length, axis=dim)
        initial = lax.slice_in_dim(array, 0, width, axis=dim)
        before = lax.ppermute(last, axis, up)
        after = lax.ppermute(initial, axis, down)
        array = jnp.concatenate([before, array, after], axis=dim)
    return array


def total_gram(partial_value):
    return lax.psum(partial_value, ("bulk", "span"))


def cholesky_step(data, row_count):
    high = lax.Precision.HIGHEST
    width = data.shape[1]
    partial_value = lax.dot_general(
        data, data, (((0,), (0,)), ((), ())), precision=high, preferred_element_type=jnp.float32
    )
    gram = total_gram(partial_value) / row_count
    lower = jnp.linalg.cholesky(gram)
    inverse = lax.linalg.triangular_solve(
        lower, jnp.eye(width, dtype=jnp.float32), left_side=True, lower=True
    )
    result = jnp.dot(data, inverse.T, precision=high, preferred_element_type=jnp.float32)
    return (result, lower)


def shards(snapshots, jac_blocks, jac_cols):
    high = lax.Precision.HIGHEST
    local_rows, width = snapshots.shape
    block_rows = jac_cols.shape[0]
    blk = jac_blocks.shape[2]
    row_count = local_rows * lax.axis_size(("bulk", "span"))
    first, lower1 = cholesky_step(snapshots, row_count)
    modes, lower2 = cholesky_step(first, row_count)
    factor = jnp.dot(lower2.T, lower1.T, precision=high, preferred_element_type=jnp.float32)
    modes_b = modes.astype(jnp.bfloat16)
    shard_start = (
        lax.axis_index("span") * lax.axis_size("bulk") + lax.axis_index("bulk")
    ) * block_rows
    relative = jac_cols - shard_start
    extended = with_halo(modes_b, (("bulk", 0),), local_rows)
    ext_blocks = extended.reshape(3 * block_rows, blk, width)
    picked = jnp.take(ext_blocks, relative + block_rows, axis=0)
    product = jnp.einsum("rnij,rnjk->rik", jac_blocks, picked, preferred_element_type=jnp.float32)
    jac_modes = product.astype(jnp.bfloat16).reshape(local_rows, width)
    partial_value = lax.dot_general(
        modes,
        jac_modes.astype(jnp.float32),
        (((0,), (0,)), ((), ())),
        precision=high,
        preferred_element_type=jnp.float32,
    )
    reduced = lax.psum(partial_value, ("bulk", "span")) / row_count
    return (modes, factor, jac_modes, reduced)


def solution(mesh):
    return jax.shard_map(
        shards,
        mesh=mesh,
        in_specs=(
            P(("span", "bulk"), None),
            P(("span", "bulk"), None, None, None),
            P(("span", "bulk"), None),
        ),
        out_specs=(P(("span", "bulk"), None), P(), P(("span", "bulk"), None), P()),
        check_vma=False,
    )
```

profile of v0, /device:TPU:0, one launch (start us, length us, event | category | flops | bytes accessed | tf_op | source)
XLA Modules:
  0.0 462.0 jit_solution(13357699271137728843)
XLA Ops:
  7.2 0.0 copy-start
  7.2 0.0 all-reduce.4.cloned.1.call-start
  7.2 4.1 fusion.29
  11.4 0.0 all-reduce.4.cloned.1.call-update
  11.4 0.0 all-reduce.6.cloned.1.call-start
  11.4 123.0 %all-reduce.4.cloned.1.call-done = f32[128,128]{0,1:T(8,128)} async-done(((f32[128,128]{0,1:T(8,128)}), f32[128,128]{0,1:T(8,128)}) %all-reduce.4.cloned.1.call-update) | async-done | bytes 65552 | tf_op jit(solution)/shard_map/psum | solution.py:21
  134.4 0.8 broadcast_multiply_fusion.2
  135.3 0.1 copy.16
  135.4 0.9 fusion.17
  136.2 11.7 %cholesky.44 = f32[128,128]{1,0:T(8,128)S(1)} custom-call(f32[128,128]{1,0:T(8,128)S(1)} %fusion.17), custom_call_target="Cholesky" | custom-call | tf_op jit(solution)/shard_map/jit(cholesky)/cholesky | solution.py:31
  148.0 0.6 compare_reduce_fusion.1
  148.6 0.6 select_bitcast_fusion.1
  149.2 9.8 %custom-call.6 = f32[1,128,128]{1,2,0:T(8,128)S(1)} custom-call(f32[1,128,128]{2,1,0:T(8,128)S(1)} %select_bitcast_fusion.1), custom_call_target="InvertDiagBlocksLowerTriangular" | custom-call | tf_op jit(solution)/shard_map/triangular_solve/custom-call.0 | solution.py:32
  159.0 0.3 fusion.12
  159.3 2.2 fusion.30
  161.5 1.6 fusion.31
  163.2 0.0 all-reduce.6.cloned.1.call-update
  163.2 0.2 all-reduce.8.cloned.1.call-start
  163.4 118.2 %all-reduce.6.cloned.1.call-done = f32[128,128]{0,1:T(8,128)} async-done(((f32[128,128]{0,1:T(8,128)}), f32[128,128]{0,1:T(8,128)}) %all-reduce.6.cloned.1.call-update) | async-done | bytes 65552 | tf_op jit(solution)/shard_map/psum | solution.py:21
  281.7 0.8 broadcast_multiply_fusion.1
  282.5 0.1 copy.18
  282.6 0.9 fusion.15
  283.5 11.7 %cholesky.55 = f32[128,128]{1,0:T(8,128)S(1)} custom-call(f32[128,128]{1,0:T(8,128)S(1)} %fusion.15), custom_call_target="Cholesky" | custom-call | tf_op jit(solution)/shard_map/jit(cholesky)/cholesky | solution.py:31
  295.2 0.7 compare_reduce_fusion
  295.9 0.7 select_bitcast_fusion
  296.6 9.8 %custom-call.7 = f32[1,128,128]{1,2,0:T(8,128)S(1)} custom-call(f32[1,128,128]{2,1,0:T(8,128)S(1)} %select_bitcast_fusion), custom_call_target="InvertDiagBlocksLowerTriangular" | custom-call | tf_op jit(solution)/shard_map/triangular_solve/custom-call.0 | solution.py:32
  306.4 0.3 fusion.10
  306.7 2.9 fusion.28
  309.7 1.3 collective-permute-start.1
  311.0 4.2 collective-permute-start
  315.1 0.0 copy-done.3
  315.2 0.1 copy.20
  315.3 0.1 reshape.36
  315.3 0.1 copy.19
  315.5 0.0 collective-permute-done.1
  315.5 1.4 collective-permute-done
  316.8 2.3 pad_maximum_fusion
  319.1 3.6 gather_fusion
  322.7 0.0 copy-done
  322.7 2.5 fusion.6
  325.2 0.0 copy-start.2
  325.2 1.4 fusion.32
  326.6 0.0 all-reduce.8.cloned.1.call-update
  326.6 2.2 fusion.19
  328.8 125.1 %all-reduce.8.cloned.1.call-done = f32[128,128]{0,1:T(8,128)} async-done(((f32[128,128]{0,1:T(8,128)}), f32[128,128]{0,1:T(8,128)}) %all-reduce.8.cloned.1.call-update) | async-done | bytes 65552 | tf_op jit(solution)/shard_map/psum | solution.py:65
  453.9 0.8 broadcast_multiply_fusion
  454.7 0.7 copy.22
  455.5 0.0 copy-done.2
  (7 shorter events, 0.1 us)
Async XLA Ops:
  7.2 315.5 %copy-start = (bf16[16,4,128,128]{3,2,1,0:T(8,128)(2,1)S(1)}, bf16[16,4,128,128]{3,2,1,0:T(8,128)(2,1)}, u32[]{:S(2)}) copy-start(bf16[16,4,128,128]{3,2,1,0:T(8,128)(2,1)} %param.7) | copy-start | bytes 6291460
  7.2 127.2 %all-reduce.4.cloned.1.call-start = ((), (), s32[]{:S(2)}) async-start(), calls=%async_computation | async-start | bytes 131072 | tf_op jit(solution)/shard_map/psum | solution.py:21
  11.4 270.3 %all-reduce.6.cloned.1.call-start = ((), (), s32[]{:S(2)}) async-start(), calls=%async_computation.1 | async-start | bytes 131072 | tf_op jit(solution)/shard_map/psum | solution.py:21
  163.2 152.0 %copy-start.3 = (s32[16,4]{0,1:T(4,128)S(1)}, s32[16,4]{0,1:T(4,128)}, u32[]{:S(2)}) copy-start(s32[16,4]{0,1:T(4,128)} %param.8) | copy-start | bytes 772
  163.2 290.7 %all-reduce.8.cloned.1.call-start = ((), (), s32[]{:S(2)}) async-start(), calls=%async_computation.2 | async-start | bytes 131072 | tf_op jit(solution)/shard_map/psum | solution.py:65
  309.7 5.8 %collective-permute-start.1 = (bf16[2048,128]{1,0:T(8,128)(2,1)}, bf16[2048,128]{1,0:T(8,128)(2,1)S(1)}, u32[]{:S(2)}, u32[]{:S(2)}) collective-permute-start(bf16[2048,128]{1,0:T(8,128)(2,1)} %get-tuple-element.16), channel_id=1, source_target_pairs={{2,0},{4,2},{6,4},{8,6},{10,8},{12,10},{14,12},{16,14},{18,16},{20... | collective-permute-start | bytes 1572872 | tf_op jit(solution)/shard_map/ppermute | solution.py:15
  311.0 5.9 %collective-permute-start = (bf16[2048,128]{1,0:T(8,128)(2,1)}, bf16[2048,128]{1,0:T(8,128)(2,1)S(1)}, u32[]{:S(2)}, u32[]{:S(2)}) collective-permute-start(bf16[2048,128]{1,0:T(8,128)(2,1)} %get-tuple-element.16), channel_id=1, source_target_pairs={{0,2},{2,4},{4,6},{6,8},{8,10},{10,12},{12,14},{14,16},{16,18},{18... | collective-permute-start | bytes 1572872 | tf_op jit(solution)/shard_map/ppermute | solution.py:14
  322.7 2.5 copy-start.1
  325.2 130.3 %copy-start.2 = (bf16[16,128,128]{1,2,0:T(8,128)(2,1)}, bf16[16,128,128]{1,2,0:T(8,128)(2,1)S(1)}, u32[]{:S(2)}) copy-start(bf16[16,128,128]{1,2,0:T(8,128)(2,1)S(1)} %fusion.6) | copy-start | bytes 1572868
Sparse Core Ops, SparseCore 0:
  14.2 120.2 all-reduce.3
  163.3 118.2 all-reduce.5
  326.7 127.1 all-reduce.7
where the time goes:
time: 464 us; the launch traced here: 462 us
  waiting for transfers between devices  368 us (79%)
  other arithmetic  52.3 us (11%)
  matrix products  17.5 us (4%)
  between operations  13.9 us (3%)
  starting transfers between devices  5.74 us (1%)
  local copies, waits for them, and re-layouts  4.77 us (1%)
    psum x2, waiting for transfers between devices, total_gram(): return lax.psum(partial_value, ('bulk', 'span'))  241 us
    psum x1, waiting for transfers between devices, shards(): reduced = lax.psum(partial_value, ('bulk', 'span')) / row_count  125 us
    another operation x6, other arithmetic, cholesky_step(): lower = jnp.linalg.cholesky(gram)  24.9 us
    another operation x4, other arithmetic, cholesky_step(): lax.linalg.triangular_solve(lower, jnp.eye(width, dtype=jnp.float32), lef...  20.9 us
  transfers between devices with their start and end apart: 5, of which 4 were waited for; matrix products, arithmetic and copies ran while one was open for 1% of the time, Pallas kernels for 0%

commit v1 on v0

v1 whole, which is shorter than its diff:
```python
import jax
import jax.numpy as jnp
from jax import lax
from jax.experimental import pallas as pl
from jax.experimental.pallas import tpu as pltpu
from jax.sharding import PartitionSpec as P

F32 = jnp.float32
BF16 = jnp.bfloat16
HIGH = lax.Precision.HIGHEST
VMEM_LIMIT = 48 * 1024 * 1024


def mm(a, b):
    return lax.dot_general(a, b, (((1,), (0,)), ((), ())), preferred_element_type=F32)


def mm_tn(a, b):
    return lax.dot_general(a, b, (((0,), (0,)), ((), ())), preferred_element_type=F32)


def split2(x):
    h = x.astype(BF16)
    return h, (x - h.astype(F32)).astype(BF16)


def split3(x):
    h = x.astype(BF16)
    r = x - h.astype(F32)
    m = r.astype(BF16)
    return h, m, (r - m.astype(F32)).astype(BF16)


def rows_of(i, n):
    return pl.ds(pl.multiple_of(i * n, n), n)


def gram_kernel(s_ref, g_ref):
    rows, k = s_ref.shape
    step = 256
    hh = jnp.zeros((2 * k, 2 * k), F32)
    hl = jnp.zeros((k, k), F32)
    for c in range(rows // step):
        h, m, l = split3(s_ref[c * step : (c + 1) * step, :])
        hm = jnp.concatenate([h, m], axis=1)
        hh = hh + mm_tn(hm, hm)
        hl = hl + mm_tn(h, l)
    cross = hh[:k, k:] + hl
    g_ref[...] = hh[:k, :k] + (cross + cross.T + hh[k:, k:])


def local_gram(s):
    k = s.shape[1]
    return pl.pallas_call(
        gram_kernel,
        out_shape=jax.ShapeDtypeStruct((k, k), F32),
        compiler_params=pltpu.CompilerParams(vmem_limit_bytes=VMEM_LIMIT),
        name="local_gram",
    )(s)


def rsqrt_newton(d):
    y = lax.rsqrt(d)
    return y * (1.5 - (0.5 * d) * (y * y))


def factor_and_inverse(a):
    k = a.shape[0]
    blocks = [a[8 * i : 8 * i + 8, :] for i in range(k // 8)]
    lane = lax.broadcasted_iota(jnp.int32, (8, k), 1)
    sub = lax.broadcasted_iota(jnp.int32, (8, k), 0)
    for j in range(k):
        b, s = divmod(j, 8)
        row = jnp.broadcast_to(blocks[b][s : s + 1, :], (8, k))
        d = jnp.broadcast_to(row[:, j : j + 1], (8, k))
        rs = rsqrt_newton(d)
        u = row * rs
        here = lane == j
        v = jnp.where(here, rs, u)
        for i in range(b, k // 8):
            x = blocks[i]
            c = jnp.broadcast_to(x[:, j : j + 1], (8, k)) * rs
            new = jnp.where(here, 0.0, x) - c * v
            if i == b:
                new = jnp.where(sub > s, new, jnp.where(sub == s, u, x))
            blocks[i] = new
    x = jnp.concatenate(blocks, axis=0)
    r = lax.broadcasted_iota(jnp.int32, (k, k), 0)
    c = lax.broadcasted_iota(jnp.int32, (k, k), 1)
    upper = jnp.where(c >= r, x, 0.0)
    inverse = jnp.where(c < r, x, jnp.where(c == r, 1.0 / x, 0.0))
    return upper, inverse


def chol1_kernel(rows_total, g_ref, up_ref, w1_ref, w2_ref):
    k = g_ref.shape[0]
    g = g_ref[...] / rows_total
    up, inv = factor_and_inverse(0.5 * (g + g.T))
    up_ref[...] = up
    h, m, l = split3(inv.T)
    hm = jnp.concatenate([h, m], axis=1)
    w1_ref[...] = jnp.concatenate([hm, hm], axis=0)
    w2_ref[...] = jnp.concatenate([l, h], axis=0)


def chol1(g, rows_total):
    k = g.shape[0]
    return pl.pallas_call(
        lambda *refs: chol1_kernel(rows_total, *refs),
        out_shape=(
            jax.ShapeDtypeStruct((k, k), F32),
            jax.ShapeDtypeStruct((2 * k, 2 * k), BF16),
            jax.ShapeDtypeStruct((2 * k, k), BF16),
        ),
        compiler_params=pltpu.CompilerParams(vmem_limit_bytes=VMEM_LIMIT),
        name="factor_first",
    )(g)


def chol2_kernel(rows_total, g_ref, t_ref, up1_ref, w1_ref, fac_ref, red_ref):
    g = g_ref[...] / rows_total
    up, inv = factor_and_inverse(0.5 * (g + g.T))
    inv_t = inv.T
    h, m = split2(inv_t)
    hm = jnp.concatenate([h, m], axis=1)
    w1_ref[...] = jnp.concatenate([hm, hm], axis=0)
    fac_ref[...] = jnp.dot(up, up1_ref[...], precision=HIGH, preferred_element_type=F32)
    t = jnp.dot(inv, t_ref[...] / rows_total, precision=HIGH, preferred_element_type=F32)
    red_ref[...] = jnp.dot(t, inv_t, precision=HIGH, preferred_element_type=F32)


def chol2(g, t, up1, rows_total):
    k = g.shape[0]
    return pl.pallas_call(
        lambda *refs: chol2_kernel(rows_total, *refs),
        out_shape=(
            jax.ShapeDtypeStruct((2 * k, 2 * k), BF16),
            jax.ShapeDtypeStruct((k, k), F32),
            jax.ShapeDtypeStruct((k, k), F32),
        ),
        compiler_params=pltpu.CompilerParams(vmem_limit_bytes=VMEM_LIMIT),
        name="factor_second",
    )(g, t, up1)


def apply_blocks(cols_ref, jb_ref, source, width, store):
    block_rows, slots, blk, _ = jb_ref.shape
    start = cols_ref[0, 0]

    def body(r, carry):
        acc = jnp.zeros((blk, width), F32)
        for n in range(0, slots, 2):
            lhs = jnp.concatenate([jb_ref[r, n], jb_ref[r, n + 1]], axis=1)
            picked = []
            for p in (n, n + 1):
                index = cols_ref[r, p] - start + block_rows
                picked.append(source[rows_of(index, blk), :])
            acc = acc + mm(lhs, jnp.concatenate(picked, axis=0))
        store(r, acc)
        return carry

    lax.fori_loop(0, block_rows, body, 0, unroll=4)


def mid_kernel(cols_ref, before_ref, s_ref, after_ref, w1_ref, w2_ref, jb_ref, f_ref, g_ref, t_ref, y_ref):
    rows, k = s_ref.shape
    blk = jb_ref.shape[2]
    step = 256
    for part, ref in enumerate((before_ref, s_ref, after_ref)):

        def body(c, carry, ref=ref, part=part):
            h, m, l = split3(ref[rows_of(c, step), :])
            p = mm(jnp.concatenate([h, m], axis=1), w1_ref[...])
            q = mm(jnp.concatenate([h, l], axis=1), w2_ref[...])
            f = p[:, :k] + (p[:, k:] + q)
            f_ref[rows_of(c + part * (rows // step), step), :] = jnp.concatenate(split2(f), axis=1)
            return carry

        lax.fori_loop(0, rows // step, body, 0, unroll=4)

    def store(r, acc):
        y = acc[:, :k] + acc[:, k:]
        y_ref[rows_of(r, blk), :] = jnp.concatenate(split2(y), axis=1)

    apply_blocks(cols_ref, jb_ref, f_ref, 2 * k, store)

    def gram_body(c, acc):
        f = f_ref[rows_of(c + rows // step, step), :]
        y = y_ref[rows_of(c, step), :]
        acc = acc + mm_tn(f, jnp.concatenate([f[:, :k], y[:, :k]], axis=1))
        return acc + mm_tn(f, jnp.concatenate([f[:, k:], y[:, k:]], axis=1))

    acc = lax.fori_loop(0, rows // step, gram_body, jnp.zeros((2 * k, 2 * k), F32), unroll=4)
    acc = acc[:k, :] + acc[k:, :]
    g_ref[...] = acc[:, :k]
    t_ref[...] = acc[:, k:]


def mid(cols, before, s, after, w1, w2, jb):
    rows, k = s.shape
    vmem = pl.BlockSpec(memory_space=pltpu.VMEM)
    return pl.pallas_call(
        mid_kernel,
        in_specs=[pl.BlockSpec(memory_space=pltpu.SMEM)] + [vmem] * 6,
        out_specs=(vmem, vmem, vmem),
        out_shape=(
            jax.ShapeDtypeStruct((3 * rows, 2 * k), BF16),
            jax.ShapeDtypeStruct((k, k), F32),
            jax.ShapeDtypeStruct((k, k), F32),
        ),
        scratch_shapes=[pltpu.VMEM((rows, 2 * k), BF16)],
        compiler_params=pltpu.CompilerParams(vmem_limit_bytes=VMEM_LIMIT),
        name="first_and_sums",
    )(cols, before, s, after, w1, w2, jb)


def last_kernel(cols_ref, f_ref, w1_ref, jb_ref, modes_ref, jm_ref, mb_ref):
    rows, k = modes_ref.shape
    blk = jb_ref.shape[2]
    step = 256
    for part in range(3):

        def body(c, carry, part=part):
            at = rows_of(c + part * (rows // step), step)
            p = mm(f_ref[at, :], w1_ref[...])
            modes = p[:, :k] + p[:, k:]
            if part == 1:
                modes_ref[rows_of(c, step), :] = modes
            mb_ref[at, :] = modes.astype(BF16)
            return carry

        lax.fori_loop(0, rows // step, body, 0, unroll=4)

    def store(r, acc):
        jm_ref[rows_of(r, blk), :] = acc.astype(BF16)

    apply_blocks(cols_ref, jb_ref, mb_ref, k, store)


def last(cols, f, w1, jb):
    rows, k = f.shape[0] // 3, f.shape[1] // 2
    vmem = pl.BlockSpec(memory_space=pltpu.VMEM)
    return pl.pallas_call(
        last_kernel,
        in_specs=[pl.BlockSpec(memory_space=pltpu.SMEM)] + [vmem] * 3,
        out_specs=(vmem, vmem),
        out_shape=(
            jax.ShapeDtypeStruct((rows, k), F32),
            jax.ShapeDtypeStruct((rows, k), BF16),
        ),
        scratch_shapes=[pltpu.VMEM((3 * rows, k), BF16)],
        compiler_params=pltpu.CompilerParams(vmem_limit_bytes=VMEM_LIMIT),
        name="modes_and_apply",
    )(cols, f, w1, jb)


def solution(mesh):
    axes = tuple(mesh.axis_names)
    sizes = dict(mesh.shape)
    n_bulk, n_span = sizes["bulk"], sizes["span"]
    count = n_bulk * n_span
    weight = {"bulk": n_span, "span": 1} if axes[0] == "bulk" else {"bulk": 1, "span": n_bulk}
    bits = lambda n: [1 << i for i in range(n.bit_length() - 1)]
    core_mask = weight["bulk"]
    masks = [m * weight["span"] for m in bits(n_span)] + [m * weight["bulk"] for m in bits(n_bulk)[1:]]
    phases = [masks[i : i + 2] for i in range(0, len(masks), 2)]

    def swap(value, mask):
        return lax.ppermute(value, axes, [(i, i ^ mask) for i in range(count)])

    def sum_phases(value):
        for phase in phases:
            if len(phase) == 2:
                a, b = phase
                pa, pb, pab = swap(value, a), swap(value, b), swap(value, a | b)
                value = (value + pa) + (pb + pab)
            else:
                value = value + swap(value, phase[0])
        return value

    def shards(snapshots, jac_blocks, jac_cols):
        rows_total = snapshots.shape[0] * count
        up = [(i, i + 1) for i in range(n_bulk - 1)]
        down = [(i + 1, i) for i in range(n_bulk - 1)]
        before = lax.ppermute(snapshots, "bulk", up)
        after = lax.ppermute(snapshots, "bulk", down)
        gram = local_gram(snapshots)
        gram = sum_phases(gram + swap(gram, core_mask))
        up1, w1, w2 = chol1(gram, rows_total)
        f, g, t = mid(jac_cols, before, snapshots, after, w1, w2, jac_blocks)
        even = lax.axis_index("bulk") % 2 == 0
        mine = jnp.where(even, g, t) + swap(jnp.where(even, t, g), core_mask)
        mine = sum_phases(mine)
        other = swap(mine, core_mask)
        g, t = jnp.where(even, mine, other), jnp.where(even, other, mine)
        v1, factor, reduced = chol2(g, t, up1, rows_total)
        modes, jac_modes = last(jac_cols, f, v1, jac_blocks)
        return modes, factor, jac_modes, reduced

    rows = P(("span", "bulk"), None)
    return jax.shard_map(
        shards,
        mesh=mesh,
        in_specs=(rows, P(("span", "bulk"), None, None, None), rows),
        out_specs=(rows, P(), rows, P()),
        check_vma=False,
    )
```

time: 464 us -> 116 us (0.25)
  waiting for transfers between devices: 368 us -> 27 us
  other arithmetic: 52.3 us -> 0.11 us
  Pallas kernels: 0 us -> 49.9 us
  starting transfers between devices: 5.74 us -> 31.3 us
  matrix products: 17.5 us -> 0 us
  between operations: 13.9 us -> 0.75 us
    psum x3 -> x0, waiting for transfers between devices: 366 us -> none  [the longest x2 241 us: total_gram(): return lax.psum(partial_value, ('bulk', 'span'))]
    pallas_call x0 -> x5, Pallas kernels: none -> 49.9 us  [the longest x1 19.4 us: chol2(): pl.pallas_call(lambda *refs: chol2_kernel(rows_total, *refs), out_shape=(...]
    another operation x10 -> x0, other arithmetic: 45.7 us -> none  [the longest x6 24.9 us: cholesky_step(): lower = jnp.linalg.cholesky(gram)]
    ppermute x2 -> x17, starting transfers between devices: 5.44 us -> 31.3 us  [the longest x15 27.6 us: swap(): return lax.ppermute(value, axes, [(i, i ^ mask) for i in range(count)])]
    ppermute x2 -> x17, waiting for transfers between devices: 1.38 us -> 27 us  [the longest x15 27 us: swap(): return lax.ppermute(value, axes, [(i, i ^ mask) for i in range(count)])]
    dot_general x7 -> x0, matrix products: 17 us -> none  [the longest x2 5.75 us: cholesky_step(): lax.dot_general(data, data, (((0,), (0,)), ((), ())), precision=high, pre...]
    unnamed x9 -> x11, local copies, waits for them, and re-layouts: 0.75 us -> 6.68 us
  transfers between devices with their start and end apart: 5 -> 17, of which waited for: 4 -> 13; matrix products, arithmetic and copies ran while one was open for 1% -> 1% of each run, Pallas kernels for 0% -> 16%
where the time goes in v1:
time: 116 us
  Pallas kernels  49.9 us (43%)
  starting transfers between devices  31.3 us (27%)
  waiting for transfers between devices  27 us (23%)
  local copies, waits for them, and re-layouts  6.68 us (6%)
    ppermute x15, starting transfers between devices, swap(): return lax.ppermute(value, axes, [(i, i ^ mask) for i in range(count)])  27.6 us
    ppermute x15, waiting for transfers between devices, swap(): return lax.ppermute(value, axes, [(i, i ^ mask) for i in range(count)])  27 us
    pallas_call x1, Pallas kernels, chol2(): pl.pallas_call(lambda *refs: chol2_kernel(rows_total, *refs), out_shape=(...  19.4 us
    pallas_call x1, Pallas kernels, chol1(): pl.pallas_call(lambda *refs: chol1_kernel(rows_total, *refs), out_shape=(...  18.3 us
    pallas_call x1, Pallas kernels, mid(): pl.pallas_call(mid_kernel, in_specs=[pl.BlockSpec(memory_space=pltpu.SMEM...  6.93 us
    unnamed x11, local copies, waits for them, and re-layouts  6.68 us
    pallas_call x1, Pallas kernels, last(): pl.pallas_call(last_kernel, in_specs=[pl.BlockSpec(memory_space=pltpu.SME...  4.6 us
    ppermute x1, starting transfers between devices, shards(): before = lax.ppermute(snapshots, 'bulk', up)  2.43 us
  transfers between devices with their start and end apart: 17, of which 13 were waited for; matrix products, arithmetic and copies ran while one was open for 1% of the time, Pallas kernels for 16%

profile of v1, /device:TPU:0, one launch (start us, length us, event | category | flops | bytes accessed | tf_op | source)
XLA Modules:
  0.0 115.7 jit_solution(3459364020153859680)
XLA Ops:
  0.6 2.4 %collective-permute-start = (f32[2048,128]{1,0:T(8,128)}, f32[2048,128]{1,0:T(8,128)S(1)}, u32[]{:S(2)}, u32[]{:S(2)}) collective-permute-start(f32[2048,128]{1,0:T(8,128)} %s_ref.3), channel_id=1, source_target_pairs={{0,2},{2,4},{4,6},{6,8},{8,10},{10,12},{12,14},{14,16},{16,18},{18... | collective-permute-start | bytes 3145736 | tf_op jit(solution)/shard_map/ppermute | solution.py:285
  3.1 1.3 %collective-permute-start.1 = (f32[2048,128]{1,0:T(8,128)}, f32[2048,128]{1,0:T(8,128)S(1)}, u32[]{:S(2)}, u32[]{:S(2)}) collective-permute-start(f32[2048,128]{1,0:T(8,128)} %s_ref.3), channel_id=1, source_target_pairs={{2,0},{4,2},{6,4},{8,6},{10,8},{12,10},{14,12},{16,14},{18,16},{20... | collective-permute-start | bytes 3145736 | tf_op jit(solution)/shard_map/ppermute | solution.py:286
  4.4 0.0 copy-start.2
  4.4 1.2 %copy-done.2 = f32[2048,128]{1,0:T(8,128)S(1)} copy-done((f32[2048,128]{1,0:T(8,128)S(1)}, f32[2048,128]{1,0:T(8,128)}, u32[]{:S(2)}) %copy-start.2) | copy-done | bytes 1048600
  5.6 0.7 local_gram.1
  6.3 3.2 %collective-permute-start.2 = (f32[128,128]{1,0:T(8,128)S(1)}, f32[128,128]{1,0:T(8,128)S(1)}, u32[]{:S(2)}, u32[]{:S(2)}) collective-permute-start(f32[128,128]{1,0:T(8,128)S(1)} %local_gram.1), channel_id=1, source_target_pairs={{0,2},{1,3},{2,0},{3,1},{4,6},{5,7},{6,4},{7,5},{8,10},{9,11},{10,... | collective-permute-start | bytes 196616 | tf_op jit(solution)/shard_map/ppermute | solution.py:269
  9.5 0.9 collective-permute-done.2
  10.4 1.6 %collective-permute-start.3 = (f32[128,128]{1,0:T(8,128)S(1)}, f32[128,128]{1,0:T(8,128)S(1)}, u32[]{:S(2)}, u32[]{:S(2)}) collective-permute-start(f32[128,128]{1,0:T(8,128)S(1)} %add.46), channel_id=1, source_target_pairs={{0,1},{1,0},{2,3},{3,2},{4,5},{5,4},{6,7},{7,6},{8,9},{9,8},{10,11... | collective-permute-start | bytes 196616 | tf_op jit(solution)/shard_map/ppermute | solution.py:269
  12.0 2.0 %collective-permute-start.4 = (f32[128,128]{1,0:T(8,128)S(1)}, f32[128,128]{1,0:T(8,128)S(1)}, u32[]{:S(2)}, u32[]{:S(2)}) collective-permute-start(f32[128,128]{1,0:T(8,128)S(1)} %add.46), channel_id=1, source_target_pairs={{0,4},{1,5},{2,6},{3,7},{4,0},{5,1},{6,2},{7,3},{8,12},{9,13},{10,... | collective-permute-start | bytes 196616 | tf_op jit(solution)/shard_map/ppermute | solution.py:269
  14.0 0.0 collective-permute-start.5
  14.0 0.8 collective-permute-done.3
  14.8 9.4 %collective-permute-done.4 = f32[128,128]{1,0:T(8,128)S(1)} collective-permute-done((f32[128,128]{1,0:T(8,128)S(1)}, f32[128,128]{1,0:T(8,128)S(1)}, u32[]{:S(2)}, u32[]{:S(2)}) %collective-permute-start.4) | collective-permute-done | bytes 65568 | tf_op jit(solution)/shard_map/ppermute | solution.py:269
  24.2 1.7 %collective-permute-done.5 = f32[128,128]{1,0:T(8,128)S(1)} collective-permute-done((f32[128,128]{1,0:T(8,128)S(1)}, f32[128,128]{1,0:T(8,128)S(1)}, u32[]{:S(2)}, u32[]{:S(2)}) %collective-permute-start.5) | collective-permute-done | bytes 65568 | tf_op jit(solution)/shard_map/ppermute | solution.py:269
  25.9 10.1 %collective-permute-start.6 = (f32[128,128]{1,0:T(8,128)S(1)}, f32[128,128]{1,0:T(8,128)S(1)}, u32[]{:S(2)}, u32[]{:S(2)}) collective-permute-start(f32[128,128]{1,0:T(8,128)S(1)} %add_add_fusion.3), channel_id=1, source_target_pairs={{0,8},{1,9},{2,10},{3,11},{4,12},{5,13},{6,14},{7,15},{8,0},{9,1},... | collective-permute-start | bytes 196616 | tf_op jit(solution)/shard_map/ppermute | solution.py:269
  36.0 2.6 %collective-permute-start.7 = (f32[128,128]{1,0:T(8,128)S(1)}, f32[128,128]{1,0:T(8,128)S(1)}, u32[]{:S(2)}, u32[]{:S(2)}) collective-permute-start(f32[128,128]{1,0:T(8,128)S(1)} %add_add_fusion.3), channel_id=1, source_target_pairs={{0,16},{1,17},{2,18},{3,19},{4,20},{5,21},{6,22},{7,23},{8,24},{9,... | collective-permute-start | bytes 196616 | tf_op jit(solution)/shard_map/ppermute | solution.py:269
  38.6 0.0 collective-permute-start.8
  38.6 0.8 copy.8.cols_ref
  39.3 0.0 collective-permute-done.6
  39.3 2.5 %collective-permute-done.7 = f32[128,128]{1,0:T(8,128)S(1)} collective-permute-done((f32[128,128]{1,0:T(8,128)S(1)}, f32[128,128]{1,0:T(8,128)S(1)}, u32[]{:S(2)}, u32[]{:S(2)}) %collective-permute-start.7) | collective-permute-done | bytes 65568 | tf_op jit(solution)/shard_map/ppermute | solution.py:269
  41.8 2.8 %collective-permute-done.8 = f32[128,128]{1,0:T(8,128)S(1)} collective-permute-done((f32[128,128]{1,0:T(8,128)S(1)}, f32[128,128]{1,0:T(8,128)S(1)}, u32[]{:S(2)}, u32[]{:S(2)}) %collective-permute-start.8) | collective-permute-done | bytes 65568 | tf_op jit(solution)/shard_map/ppermute | solution.py:269
  44.6 18.3 %factor_first.1 = (f32[128,128]{1,0:T(8,128)S(1)}, bf16[256,256]{1,0:T(8,128)(2,1)S(1)}, bf16[256,128]{1,0:T(8,128)(2,1)S(1)}) custom-call(f32[128,128]{1,0:T(8,128)S(1)} %add_add_fusion.2.refs_0_), custom_call_target="tpu_custom_call" | custom-call | tf_op jit(solution)/shard_map/factor_first/pallas_call | solution.py:108
  63.0 0.0 collective-permute-done.before_ref
  63.0 0.0 collective-permute-done.1.after_ref
  63.0 0.0 copy-start
  63.0 1.6 %copy-done = bf16[16,4,128,128]{3,2,1,0:T(8,128)(2,1)S(1)} copy-done((bf16[16,4,128,128]{3,2,1,0:T(8,128)(2,1)S(1)}, bf16[16,4,128,128]{3,2,1,0:T(8,128)(2,1)}, u32[]{:S(2)}) %copy-start) | copy-done | bytes 2097176
  64.6 0.0 copy-start.3
  64.6 1.2 %copy-done.3 = f32[2048,128]{1,0:T(8,128)S(1)} copy-done((f32[2048,128]{1,0:T(8,128)S(1)}, f32[2048,128]{1,0:T(8,128)}, u32[]{:S(2)}) %copy-start.3) | copy-done | bytes 1048600
  65.8 6.9 %first_and_sums.1 = (bf16[6144,256]{1,0:T(8,128)(2,1)}, f32[128,128]{1,0:T(8,128)S(1)}, f32[128,128]{1,0:T(8,128)S(1)}) custom-call(s32[16,4]{1,0:T(8,128)S(1)} %copy.8.cols_ref, f32[2048,128]{1,0:T(8,128)S(1)} %collective-permute-done.before_ref, f32[2048,128]{1,0:T(8,128)S(1)} %copy-done.3, f32[2048,128]{1,0:T(8,128)S(1)} %collective-permute-done.1.after_ref, ...), custom_call_target="tpu_custom_call" | custom-call | tf_op jit(solution)/shard_map/first_and_sums/pallas_call | solution.py:202
  72.8 0.1 collective-permute-start.9
  72.8 1.2 %collective-permute-done.9 = f32[128,128]{1,0:T(8,128)S(1)} collective-permute-done((f32[128,128]{1,0:T(8,128)S(1)}, f32[128,128]{1,0:T(8,128)S(1)}, u32[]{:S(2)}, u32[]{:S(2)}) %collective-permute-start.9) | collective-permute-done | bytes 65568 | tf_op jit(solution)/shard_map/ppermute | solution.py:269
  74.1 0.6 collective-permute-start.10
  74.7 0.0 collective-permute-start.11
  74.7 3.0 %collective-permute-start.12 = (f32[128,128]{1,0:T(8,128)S(1)}, f32[128,128]{1,0:T(8,128)S(1)}, u32[]{:S(2)}, u32[]{:S(2)}) collective-permute-start(f32[128,128]{1,0:T(8,128)S(1)} %select_add_fusion), channel_id=1, source_target_pairs={{0,5},{1,4},{2,7},{3,6},{4,1},{5,0},{6,3},{7,2},{8,13},{9,12},{10,... | collective-permute-start | bytes 196616 | tf_op jit(solution)/shard_map/ppermute | solution.py:269
  77.7 0.8 collective-permute-done.10
  78.4 1.1 collective-permute-done.11
  79.5 1.4 %collective-permute-done.12 = f32[128,128]{1,0:T(8,128)S(1)} collective-permute-done((f32[128,128]{1,0:T(8,128)S(1)}, f32[128,128]{1,0:T(8,128)S(1)}, u32[]{:S(2)}, u32[]{:S(2)}) %collective-permute-start.12) | collective-permute-done | bytes 65568 | tf_op jit(solution)/shard_map/ppermute | solution.py:269
  80.9 0.1 collective-permute-start.13
  81.1 1.3 %collective-permute-start.14 = (f32[128,128]{1,0:T(8,128)S(1)}, f32[128,128]{1,0:T(8,128)S(1)}, u32[]{:S(2)}, u32[]{:S(2)}) collective-permute-start(f32[128,128]{1,0:T(8,128)S(1)} %add_add_fusion.1), channel_id=1, source_target_pairs={{0,16},{1,17},{2,18},{3,19},{4,20},{5,21},{6,22},{7,23},{8,24},{9,... | collective-permute-start | bytes 196616 | tf_op jit(solution)/shard_map/ppermute | solution.py:269
  82.4 3.0 %collective-permute-start.15 = (f32[128,128]{1,0:T(8,128)S(1)}, f32[128,128]{1,0:T(8,128)S(1)}, u32[]{:S(2)}, u32[]{:S(2)}) collective-permute-start(f32[128,128]{1,0:T(8,128)S(1)} %add_add_fusion.1), channel_id=1, source_target_pairs={{0,24},{1,25},{2,26},{3,27},{4,28},{5,29},{6,30},{7,31},{8,16},{9,... | collective-permute-start | bytes 196616 | tf_op jit(solution)/shard_map/ppermute | solution.py:269
  85.4 0.0 collective-permute-done.13
  85.4 2.3 %collective-permute-done.14 = f32[128,128]{1,0:T(8,128)S(1)} collective-permute-done((f32[128,128]{1,0:T(8,128)S(1)}, f32[128,128]{1,0:T(8,128)S(1)}, u32[]{:S(2)}, u32[]{:S(2)}) %collective-permute-start.14) | collective-permute-done | bytes 65568 | tf_op jit(solution)/shard_map/ppermute | solution.py:269
  87.7 0.8 collective-permute-done.15
  88.5 0.1 collective-permute-start.16
  88.6 1.2 %collective-permute-done.16 = f32[128,128]{1,0:T(8,128)S(1)} collective-permute-done((f32[128,128]{1,0:T(8,128)S(1)}, f32[128,128]{1,0:T(8,128)S(1)}, u32[]{:S(2)}, u32[]{:S(2)}) %collective-permute-start.16) | collective-permute-done | bytes 65568 | tf_op jit(solution)/shard_map/ppermute | solution.py:269
  89.9 19.4 %factor_second.1 = (bf16[256,256]{1,0:T(8,128)(2,1)S(1)}, f32[128,128]{1,0:T(8,128)}, f32[128,128]{1,0:T(8,128)}) custom-call(f32[128,128]{1,0:T(8,128)S(1)} %get-tuple-element.27.refs_0_, f32[128,128]{1,0:T(8,128)S(1)} %get-tuple-element.26.refs_1_, f32[128,128]{1,0:T(8,128)S(1)} %get-tuple-element.20.refs_2_), custom_call_target="tpu_custom_call" | custom-call | tf_op jit(solution)/shard_map/factor_second/pallas_call | solution.py:134
  109.2 0.0 copy-done.1
  109.2 1.9 %copy-done.4 = bf16[6144,256]{1,0:T(8,128)(2,1)S(1)} copy-done((bf16[6144,256]{1,0:T(8,128)(2,1)S(1)}, bf16[6144,256]{1,0:T(8,128)(2,1)}, u32[]{:S(2)}) %copy-start.4) | copy-done | bytes 3145752
  111.1 4.6 %modes_and_apply.1 = (f32[2048,128]{1,0:T(8,128)}, bf16[2048,128]{1,0:T(8,128)(2,1)}) custom-call(s32[16,4]{1,0:T(8,128)S(1)} %copy.8.cols_ref, bf16[6144,256]{1,0:T(8,128)(2,1)S(1)} %copy-done.4, bf16[256,256]{1,0:T(8,128)(2,1)S(1)} %get-tuple-element.21.w1_ref, bf16[16,4,128,128]{3,2,1,0:T(8,128)(2,1)S(1)} %copy-done.1), custom_call_target="tpu_custom_call" | custom-call | tf_op jit(solution)/shard_map/modes_and_apply/pallas_call | solution.py:243
  (10 shorter events, 0.1 us)
Async XLA Ops:
  0.6 62.4 %collective-permute-start = (f32[2048,128]{1,0:T(8,128)}, f32[2048,128]{1,0:T(8,128)S(1)}, u32[]{:S(2)}, u32[]{:S(2)}) collective-permute-start(f32[2048,128]{1,0:T(8,128)} %s_ref.3), channel_id=1, source_target_pairs={{0,2},{2,4},{4,6},{6,8},{8,10},{10,12},{12,14},{14,16},{16,18},{18... | collective-permute-start | bytes 3145736 | tf_op jit(solution)/shard_map/ppermute | solution.py:285
  3.1 59.9 %collective-permute-start.1 = (f32[2048,128]{1,0:T(8,128)}, f32[2048,128]{1,0:T(8,128)S(1)}, u32[]{:S(2)}, u32[]{:S(2)}) collective-permute-start(f32[2048,128]{1,0:T(8,128)} %s_ref.3), channel_id=1, source_target_pairs={{2,0},{4,2},{6,4},{8,6},{10,8},{12,10},{14,12},{16,14},{18,16},{20... | collective-permute-start | bytes 3145736 | tf_op jit(solution)/shard_map/ppermute | solution.py:286
  4.4 1.2 %copy-start.2 = (f32[2048,128]{1,0:T(8,128)S(1)}, f32[2048,128]{1,0:T(8,128)}, u32[]{:S(2)}) copy-start(f32[2048,128]{1,0:T(8,128)} %s_ref.3) | copy-start | bytes 3145732
  6.3 4.1 %collective-permute-start.2 = (f32[128,128]{1,0:T(8,128)S(1)}, f32[128,128]{1,0:T(8,128)S(1)}, u32[]{:S(2)}, u32[]{:S(2)}) collective-permute-start(f32[128,128]{1,0:T(8,128)S(1)} %local_gram.1), channel_id=1, source_target_pairs={{0,2},{1,3},{2,0},{3,1},{4,6},{5,7},{6,4},{7,5},{8,10},{9,11},{10,... | collective-permute-start | bytes 196616 | tf_op jit(solution)/shard_map/ppermute | solution.py:269
  10.4 4.4 %collective-permute-start.3 = (f32[128,128]{1,0:T(8,128)S(1)}, f32[128,128]{1,0:T(8,128)S(1)}, u32[]{:S(2)}, u32[]{:S(2)}) collective-permute-start(f32[128,128]{1,0:T(8,128)S(1)} %add.46), channel_id=1, source_target_pairs={{0,1},{1,0},{2,3},{3,2},{4,5},{5,4},{6,7},{7,6},{8,9},{9,8},{10,11... | collective-permute-start | bytes 196616 | tf_op jit(solution)/shard_map/ppermute | solution.py:269
  12.0 12.2 %collective-permute-start.4 = (f32[128,128]{1,0:T(8,128)S(1)}, f32[128,128]{1,0:T(8,128)S(1)}, u32[]{:S(2)}, u32[]{:S(2)}) collective-permute-start(f32[128,128]{1,0:T(8,128)S(1)} %add.46), channel_id=1, source_target_pairs={{0,4},{1,5},{2,6},{3,7},{4,0},{5,1},{6,2},{7,3},{8,12},{9,13},{10,... | collective-permute-start | bytes 196616 | tf_op jit(solution)/shard_map/ppermute | solution.py:269
  14.0 11.9 %collective-permute-start.5 = (f32[128,128]{1,0:T(8,128)S(1)}, f32[128,128]{1,0:T(8,128)S(1)}, u32[]{:S(2)}, u32[]{:S(2)}) collective-permute-start(f32[128,128]{1,0:T(8,128)S(1)} %add.46), channel_id=1, source_target_pairs={{0,5},{1,4},{2,7},{3,6},{4,1},{5,0},{6,3},{7,2},{8,13},{9,12},{10,... | collective-permute-start | bytes 196616 | tf_op jit(solution)/shard_map/ppermute | solution.py:269
  25.9 13.4 %collective-permute-start.6 = (f32[128,128]{1,0:T(8,128)S(1)}, f32[128,128]{1,0:T(8,128)S(1)}, u32[]{:S(2)}, u32[]{:S(2)}) collective-permute-start(f32[128,128]{1,0:T(8,128)S(1)} %add_add_fusion.3), channel_id=1, source_target_pairs={{0,8},{1,9},{2,10},{3,11},{4,12},{5,13},{6,14},{7,15},{8,0},{9,1},... | collective-permute-start | bytes 196616 | tf_op jit(solution)/shard_map/ppermute | solution.py:269
  36.0 5.9 %collective-permute-start.7 = (f32[128,128]{1,0:T(8,128)S(1)}, f32[128,128]{1,0:T(8,128)S(1)}, u32[]{:S(2)}, u32[]{:S(2)}) collective-permute-start(f32[128,128]{1,0:T(8,128)S(1)} %add_add_fusion.3), channel_id=1, source_target_pairs={{0,16},{1,17},{2,18},{3,19},{4,20},{5,21},{6,22},{7,23},{8,24},{9,... | collective-permute-start | bytes 196616 | tf_op jit(solution)/shard_map/ppermute | solution.py:269
  38.6 6.1 %collective-permute-start.8 = (f32[128,128]{1,0:T(8,128)S(1)}, f32[128,128]{1,0:T(8,128)S(1)}, u32[]{:S(2)}, u32[]{:S(2)}) collective-permute-start(f32[128,128]{1,0:T(8,128)S(1)} %add_add_fusion.3), channel_id=1, source_target_pairs={{0,24},{1,25},{2,26},{3,27},{4,28},{5,29},{6,30},{7,31},{8,16},{9,... | collective-permute-start | bytes 196616 | tf_op jit(solution)/shard_map/ppermute | solution.py:269
  63.0 1.6 %copy-start = (bf16[16,4,128,128]{3,2,1,0:T(8,128)(2,1)S(1)}, bf16[16,4,128,128]{3,2,1,0:T(8,128)(2,1)}, u32[]{:S(2)}) copy-start(bf16[16,4,128,128]{3,2,1,0:T(8,128)(2,1)} %jb_ref.3) | copy-start | bytes 6291460
  64.6 1.2 %copy-start.3 = (f32[2048,128]{1,0:T(8,128)S(1)}, f32[2048,128]{1,0:T(8,128)}, u32[]{:S(2)}) copy-start(f32[2048,128]{1,0:T(8,128)} %s_ref.3) | copy-start | bytes 3145732
  65.8 43.4 %copy-start.1 = (bf16[16,4,128,128]{3,2,1,0:T(8,128)(2,1)S(1)}, bf16[16,4,128,128]{3,2,1,0:T(8,128)(2,1)}, u32[]{:S(2)}) copy-start(bf16[16,4,128,128]{3,2,1,0:T(8,128)(2,1)} %jb_ref.3) | copy-start | bytes 6291460
  72.8 1.3 %collective-permute-start.9 = (f32[128,128]{1,0:T(8,128)S(1)}, f32[128,128]{1,0:T(8,128)S(1)}, u32[]{:S(2)}, u32[]{:S(2)}) collective-permute-start(f32[128,128]{1,0:T(8,128)S(1)} %broadcast_select_fusion.2), channel_id=1, source_target_pairs={{0,2},{1,3},{2,0},{3,1},{4,6},{5,7},{6,4},{7,5},{8,10},{9,11},{10,... | collective-permute-start | bytes 196616 | tf_op jit(solution)/shard_map/ppermute | solution.py:269
  74.1 4.3 %collective-permute-start.10 = (f32[128,128]{1,0:T(8,128)S(1)}, f32[128,128]{1,0:T(8,128)S(1)}, u32[]{:S(2)}, u32[]{:S(2)}) collective-permute-start(f32[128,128]{1,0:T(8,128)S(1)} %select_add_fusion), channel_id=1, source_target_pairs={{0,1},{1,0},{2,3},{3,2},{4,5},{5,4},{6,7},{7,6},{8,9},{9,8},{10,11... | collective-permute-start | bytes 196616 | tf_op jit(solution)/shard_map/ppermute | solution.py:269
  74.7 4.8 %collective-permute-start.11 = (f32[128,128]{1,0:T(8,128)S(1)}, f32[128,128]{1,0:T(8,128)S(1)}, u32[]{:S(2)}, u32[]{:S(2)}) collective-permute-start(f32[128,128]{1,0:T(8,128)S(1)} %select_add_fusion), channel_id=1, source_target_pairs={{0,4},{1,5},{2,6},{3,7},{4,0},{5,1},{6,2},{7,3},{8,12},{9,13},{10,... | collective-permute-start | bytes 196616 | tf_op jit(solution)/shard_map/ppermute | solution.py:269
  74.7 6.2 %collective-permute-start.12 = (f32[128,128]{1,0:T(8,128)S(1)}, f32[128,128]{1,0:T(8,128)S(1)}, u32[]{:S(2)}, u32[]{:S(2)}) collective-permute-start(f32[128,128]{1,0:T(8,128)S(1)} %select_add_fusion), channel_id=1, source_target_pairs={{0,5},{1,4},{2,7},{3,6},{4,1},{5,0},{6,3},{7,2},{8,13},{9,12},{10,... | collective-permute-start | bytes 196616 | tf_op jit(solution)/shard_map/ppermute | solution.py:269
  80.9 4.5 %collective-permute-start.13 = (f32[128,128]{1,0:T(8,128)S(1)}, f32[128,128]{1,0:T(8,128)S(1)}, u32[]{:S(2)}, u32[]{:S(2)}) collective-permute-start(f32[128,128]{1,0:T(8,128)S(1)} %add_add_fusion.1), channel_id=1, source_target_pairs={{0,8},{1,9},{2,10},{3,11},{4,12},{5,13},{6,14},{7,15},{8,0},{9,1},... | collective-permute-start | bytes 196616 | tf_op jit(solution)/shard_map/ppermute | solution.py:269
  81.1 6.6 %collective-permute-start.14 = (f32[128,128]{1,0:T(8,128)S(1)}, f32[128,128]{1,0:T(8,128)S(1)}, u32[]{:S(2)}, u32[]{:S(2)}) collective-permute-start(f32[128,128]{1,0:T(8,128)S(1)} %add_add_fusion.1), channel_id=1, source_target_pairs={{0,16},{1,17},{2,18},{3,19},{4,20},{5,21},{6,22},{7,23},{8,24},{9,... | collective-permute-start | bytes 196616 | tf_op jit(solution)/shard_map/ppermute | solution.py:269
  82.4 6.1 %collective-permute-start.15 = (f32[128,128]{1,0:T(8,128)S(1)}, f32[128,128]{1,0:T(8,128)S(1)}, u32[]{:S(2)}, u32[]{:S(2)}) collective-permute-start(f32[128,128]{1,0:T(8,128)S(1)} %add_add_fusion.1), channel_id=1, source_target_pairs={{0,24},{1,25},{2,26},{3,27},{4,28},{5,29},{6,30},{7,31},{8,16},{9,... | collective-permute-start | bytes 196616 | tf_op jit(solution)/shard_map/ppermute | solution.py:269
  88.5 1.3 %collective-permute-start.16 = (f32[128,128]{1,0:T(8,128)S(1)}, f32[128,128]{1,0:T(8,128)S(1)}, u32[]{:S(2)}, u32[]{:S(2)}) collective-permute-start(f32[128,128]{1,0:T(8,128)S(1)} %add_add_fusion), channel_id=1, source_target_pairs={{0,2},{1,3},{2,0},{3,1},{4,6},{5,7},{6,4},{7,5},{8,10},{9,11},{10,... | collective-permute-start | bytes 196616 | tf_op jit(solution)/shard_map/ppermute | solution.py:269
  109.2 1.9 %copy-start.4 = (bf16[6144,256]{1,0:T(8,128)(2,1)S(1)}, bf16[6144,256]{1,0:T(8,128)(2,1)}, u32[]{:S(2)}) copy-start(bf16[6144,256]{1,0:T(8,128)(2,1)} %get-tuple-element.17.f_ref) | copy-start | bytes 9437188

commit v2 on v1

--- a/solution.py
+++ b/solution.py
@@ -8,7 +8,7 @@
 F32 = jnp.float32
 BF16 = jnp.bfloat16
 HIGH = lax.Precision.HIGHEST
-VMEM_LIMIT = 48 * 1024 * 1024
+VMEM_LIMIT = 16 * 1024 * 1024
 
 
 def mm(a, b):
@@ -59,37 +59,52 @@
     )(s)
 
 
-def rsqrt_newton(d):
-    y = lax.rsqrt(d)
-    return y * (1.5 - (0.5 * d) * (y * y))
-
-
 def factor_and_inverse(a):
-    k = a.shape[0]
-    blocks = [a[8 * i : 8 * i + 8, :] for i in range(k // 8)]
-    lane = lax.broadcasted_iota(jnp.int32, (8, k), 1)
-    sub = lax.broadcasted_iota(jnp.int32, (8, k), 0)
-    for j in range(k):
-        b, s = divmod(j, 8)
-        row = jnp.broadcast_to(blocks[b][s : s + 1, :], (8, k))
-        d = jnp.broadcast_to(row[:, j : j + 1], (8, k))
-        rs = rsqrt_newton(d)
-        u = row * rs
-        here = lane == j
-        v = jnp.where(here, rs, u)
-        for i in range(b, k // 8):
+    k, n = a.shape[0], 8
+    blocks = [a[n * i : n * i + n, :] for i in range(k // n)]
+    lane = lax.broadcasted_iota(jnp.int32, (n, k), 1)
+    sub = lax.broadcasted_iota(jnp.int32, (n, k), 0)
+    full = lambda value: jnp.broadcast_to(value, (n, k))
+    for p in range(k // n):
+        x = blocks[p]
+        at = n * p
+        columns = [full(x[:, at + t : at + t + 1]) for t in range(n)]
+        d = {(s, t): full(columns[t][s : s + 1, :]) for t in range(n) for s in range(t, n)}
+        row = [full(x[s : s + 1, :]) for s in range(n)]
+        done, scale, low = [], [], {}
+        for t in range(n):
+            scale.append(lax.rsqrt(d[t, t]))
+            here = lane == at + t
+            done.append(jnp.where(here, scale[t], row[t] * scale[t]))
+            for s in range(t + 1, n):
+                low[s, t] = d[s, t] * scale[t]
+            for u in range(t + 1, n):
+                for s in range(u, n):
+                    d[s, u] = d[s, u] - low[s, t] * low[u, t]
+            for s in range(t + 1, n):
+                row[s] = jnp.where(here, 0.0, row[s]) - low[s, t] * done[t]
+        out = done[0]
+        for t in range(1, n):
+            out = jnp.where(sub == t, done[t], out)
+        blocks[p] = out
+        panel = (lane >= at) & (lane < at + n)
+        terms = [jnp.where(panel & (lane > at + t), 0.0, done[t]) for t in range(n)]
+        for i in range(p + 1, k // n):
             x = blocks[i]
-            c = jnp.broadcast_to(x[:, j : j + 1], (8, k)) * rs
-            new = jnp.where(here, 0.0, x) - c * v
-            if i == b:
-                new = jnp.where(sub > s, new, jnp.where(sub == s, u, x))
+            new = jnp.where(panel, 0.0, x)
+            column = []
+            for t in range(n):
+                c = full(x[:, at + t : at + t + 1])
+                for u in range(t):
+                    c = c - column[u] * low[t, u]
+                column.append(c * scale[t])
+                new = new - column[t] * terms[t]
             blocks[i] = new
     x = jnp.concatenate(blocks, axis=0)
     r = lax.broadcasted_iota(jnp.int32, (k, k), 0)
     c = lax.broadcasted_iota(jnp.int32, (k, k), 1)
-    upper = jnp.where(c >= r, x, 0.0)
-    inverse = jnp.where(c < r, x, jnp.where(c == r, 1.0 / x, 0.0))
-    return upper, inverse
+    upper = jnp.where(c > r, x, jnp.where(c == r, 1.0 / x, 0.0))
+    return upper, jnp.where(c <= r, x, 0.0)
 
 
 def chol1_kernel(rows_total, g_ref, up_ref, w1_ref, w2_ref):
@@ -268,7 +283,7 @@
     def swap(value, mask):
         return lax.ppermute(value, axes, [(i, i ^ mask) for i in range(count)])
 
-    def sum_phases(value):
+    def sum_phases(value, phases):
         for phase in phases:
             if len(phase) == 2:
                 a, b = phase
@@ -285,12 +300,12 @@
         before = lax.ppermute(snapshots, "bulk", up)
         after = lax.ppermute(snapshots, "bulk", down)
         gram = local_gram(snapshots)
-        gram = sum_phases(gram + swap(gram, core_mask))
+        gram = sum_phases(gram + swap(gram, core_mask), phases[::-1])
         up1, w1, w2 = chol1(gram, rows_total)
         f, g, t = mid(jac_cols, before, snapshots, after, w1, w2, jac_blocks)
         even = lax.axis_index("bulk") % 2 == 0
         mine = jnp.where(even, g, t) + swap(jnp.where(even, t, g), core_mask)
-        mine = sum_phases(mine)
+        mine = sum_phases(mine, phases)
         other = swap(mine, core_mask)
         g, t = jnp.where(even, mine, other), jnp.where(even, other, mine)
         v1, factor, reduced = chol2(g, t, up1, rows_total)

time: 116 us -> 77.4 us (0.67)
  Pallas kernels: 49.9 us -> 20.5 us
  starting transfers between devices: 31.3 us -> 24.3 us
  local copies, waits for them, and re-layouts: 6.68 us -> 4.79 us
    pallas_call x1, Pallas kernels: 18.3 us -> 4.02 us  [chol1(): pl.pallas_call(lambda *refs: chol1_kernel(rows_total, *refs), out_shape=(...]
    pallas_call x1, Pallas kernels: 19.4 us -> 5.69 us  [chol2(): pl.pallas_call(lambda *refs: chol2_kernel(rows_total, *refs), out_shape=(...]
    ppermute x15, starting transfers between devices: 27.6 us -> 20.6 us  [swap(): return lax.ppermute(value, axes, [(i, i ^ mask) for i in range(count)])]
    unnamed x11 -> x9, local copies, waits for them, and re-layouts: 6.68 us -> 4.79 us
    pallas_call x1, Pallas kernels: 6.93 us -> 5.55 us  [mid(): pl.pallas_call(mid_kernel, in_specs=[pl.BlockSpec(memory_space=pltpu.SMEM...]
  transfers between devices with their start and end apart: 17 -> 17, of which waited for: 13 -> 12; matrix products, arithmetic and copies ran while one was open for 1% -> 1% of each run, Pallas kernels for 16% -> 6%
where the time goes in v2:
time: 77.4 us; the launch traced here: 77.1 us
  waiting for transfers between devices  26.6 us (34%)
  starting transfers between devices  24.3 us (31%)
  Pallas kernels  20.5 us (26%)
  local copies, waits for them, and re-layouts  4.79 us (6%)
    ppermute x15, waiting for transfers between devices, swap(): return lax.ppermute(value, axes, [(i, i ^ mask) for i in range(count)])  26.6 us
    ppermute x15, starting transfers between devices, swap(): return lax.ppermute(value, axes, [(i, i ^ mask) for i in range(count)])  20.6 us
    pallas_call x1, Pallas kernels, chol2(): pl.pallas_call(lambda *refs: chol2_kernel(rows_total, *refs), out_shape=(...  5.69 us
    pallas_call x1, Pallas kernels, mid(): pl.pallas_call(mid_kernel, in_specs=[pl.BlockSpec(memory_space=pltpu.SMEM...  5.55 us
    unnamed x9, local copies, waits for them, and re-layouts  4.79 us
    pallas_call x1, Pallas kernels, last(): pl.pallas_call(last_kernel, in_specs=[pl.BlockSpec(memory_space=pltpu.SME...  4.6 us
    pallas_call x1, Pallas kernels, chol1(): pl.pallas_call(lambda *refs: chol1_kernel(rows_total, *refs), out_shape=(...  4.02 us
    ppermute x1, starting transfers between devices, shards(): before = lax.ppermute(snapshots, 'bulk', up)  2.43 us
  transfers between devices with their start and end apart: 17, of which 12 were waited for; matrix products, arithmetic and copies ran while one was open for 1% of the time, Pallas kernels for 6%

profile of v2, /device:TPU:0, one launch (start us, length us, event | category | flops | bytes accessed | tf_op | source)
XLA Modules:
  0.0 77.1 jit_solution(987457144808595719)
XLA Ops:
  0.6 2.4 %collective-permute-start = (f32[2048,128]{1,0:T(8,128)}, f32[2048,128]{1,0:T(8,128)S(1)}, u32[]{:S(2)}, u32[]{:S(2)}) collective-permute-start(f32[2048,128]{1,0:T(8,128)} %s_ref.3), channel_id=1, source_target_pairs={{0,2},{2,4},{4,6},{6,8},{8,10},{10,12},{12,14},{14,16},{16,18},{18... | collective-permute-start | bytes 3145736 | tf_op jit(solution)/shard_map/ppermute | solution.py:300
  3.1 1.3 %collective-permute-start.1 = (f32[2048,128]{1,0:T(8,128)}, f32[2048,128]{1,0:T(8,128)S(1)}, u32[]{:S(2)}, u32[]{:S(2)}) collective-permute-start(f32[2048,128]{1,0:T(8,128)} %s_ref.3), channel_id=1, source_target_pairs={{2,0},{4,2},{6,4},{8,6},{10,8},{12,10},{14,12},{16,14},{18,16},{20... | collective-permute-start | bytes 3145736 | tf_op jit(solution)/shard_map/ppermute | solution.py:301
  4.4 0.0 copy-start.2
  4.4 1.2 %copy-done.2 = f32[2048,128]{1,0:T(8,128)S(1)} copy-done((f32[2048,128]{1,0:T(8,128)S(1)}, f32[2048,128]{1,0:T(8,128)}, u32[]{:S(2)}) %copy-start.2) | copy-done | bytes 1048600
  5.6 0.7 local_gram.1
  6.3 3.2 %collective-permute-start.2 = (f32[128,128]{1,0:T(8,128)S(1)}, f32[128,128]{1,0:T(8,128)S(1)}, u32[]{:S(2)}, u32[]{:S(2)}) collective-permute-start(f32[128,128]{1,0:T(8,128)S(1)} %local_gram.1), channel_id=1, source_target_pairs={{0,2},{1,3},{2,0},{3,1},{4,6},{5,7},{6,4},{7,5},{8,10},{9,11},{10,... | collective-permute-start | bytes 196616 | tf_op jit(solution)/shard_map/ppermute | solution.py:284
  9.5 0.9 %collective-permute-done.2 = f32[128,128]{1,0:T(8,128)S(1)} collective-permute-done((f32[128,128]{1,0:T(8,128)S(1)}, f32[128,128]{1,0:T(8,128)S(1)}, u32[]{:S(2)}, u32[]{:S(2)}) %collective-permute-start.2) | collective-permute-done | bytes 65568 | tf_op jit(solution)/shard_map/ppermute | solution.py:284
  10.4 3.0 %collective-permute-start.3 = (f32[128,128]{1,0:T(8,128)S(1)}, f32[128,128]{1,0:T(8,128)S(1)}, u32[]{:S(2)}, u32[]{:S(2)}) collective-permute-start(f32[128,128]{1,0:T(8,128)S(1)} %add.46), channel_id=1, source_target_pairs={{0,8},{1,9},{2,10},{3,11},{4,12},{5,13},{6,14},{7,15},{8,0},{9,1},... | collective-permute-start | bytes 196616 | tf_op jit(solution)/shard_map/ppermute | solution.py:284
  13.4 2.6 %collective-permute-start.4 = (f32[128,128]{1,0:T(8,128)S(1)}, f32[128,128]{1,0:T(8,128)S(1)}, u32[]{:S(2)}, u32[]{:S(2)}) collective-permute-start(f32[128,128]{1,0:T(8,128)S(1)} %add.46), channel_id=1, source_target_pairs={{0,16},{1,17},{2,18},{3,19},{4,20},{5,21},{6,22},{7,23},{8,24},{9,... | collective-permute-start | bytes 196616 | tf_op jit(solution)/shard_map/ppermute | solution.py:284
  16.0 0.0 collective-permute-start.5
  16.0 9.9 %collective-permute-done.3 = f32[128,128]{1,0:T(8,128)S(1)} collective-permute-done((f32[128,128]{1,0:T(8,128)S(1)}, f32[128,128]{1,0:T(8,128)S(1)}, u32[]{:S(2)}, u32[]{:S(2)}) %collective-permute-start.3) | collective-permute-done | bytes 65568 | tf_op jit(solution)/shard_map/ppermute | solution.py:284
  26.0 1.7 %collective-permute-done.4 = f32[128,128]{1,0:T(8,128)S(1)} collective-permute-done((f32[128,128]{1,0:T(8,128)S(1)}, f32[128,128]{1,0:T(8,128)S(1)}, u32[]{:S(2)}, u32[]{:S(2)}) %collective-permute-start.4) | collective-permute-done | bytes 65568 | tf_op jit(solution)/shard_map/ppermute | solution.py:284
  27.7 1.8 %collective-permute-done.5 = f32[128,128]{1,0:T(8,128)S(1)} collective-permute-done((f32[128,128]{1,0:T(8,128)S(1)}, f32[128,128]{1,0:T(8,128)S(1)}, u32[]{:S(2)}, u32[]{:S(2)}) %collective-permute-start.5) | collective-permute-done | bytes 65568 | tf_op jit(solution)/shard_map/ppermute | solution.py:284
  29.5 1.6 %collective-permute-start.6 = (f32[128,128]{1,0:T(8,128)S(1)}, f32[128,128]{1,0:T(8,128)S(1)}, u32[]{:S(2)}, u32[]{:S(2)}) collective-permute-start(f32[128,128]{1,0:T(8,128)S(1)} %add_add_fusion.3), channel_id=1, source_target_pairs={{0,1},{1,0},{2,3},{3,2},{4,5},{5,4},{6,7},{7,6},{8,9},{9,8},{10,11... | collective-permute-start | bytes 196616 | tf_op jit(solution)/shard_map/ppermute | solution.py:284
  31.1 0.0 collective-permute-start.7
  31.1 2.0 %collective-permute-start.8 = (f32[128,128]{1,0:T(8,128)S(1)}, f32[128,128]{1,0:T(8,128)S(1)}, u32[]{:S(2)}, u32[]{:S(2)}) collective-permute-start(f32[128,128]{1,0:T(8,128)S(1)} %add_add_fusion.3), channel_id=1, source_target_pairs={{0,5},{1,4},{2,7},{3,6},{4,1},{5,0},{6,3},{7,2},{8,13},{9,12},{10,... | collective-permute-start | bytes 196616 | tf_op jit(solution)/shard_map/ppermute | solution.py:284
  33.1 0.8 copy.8.cols_ref
  33.8 0.0 collective-permute-done.6
  33.8 1.5 %collective-permute-done.7 = f32[128,128]{1,0:T(8,128)S(1)} collective-permute-done((f32[128,128]{1,0:T(8,128)S(1)}, f32[128,128]{1,0:T(8,128)S(1)}, u32[]{:S(2)}, u32[]{:S(2)}) %collective-permute-start.7) | collective-permute-done | bytes 65568 | tf_op jit(solution)/shard_map/ppermute | solution.py:284
  35.4 0.9 %collective-permute-done.8 = f32[128,128]{1,0:T(8,128)S(1)} collective-permute-done((f32[128,128]{1,0:T(8,128)S(1)}, f32[128,128]{1,0:T(8,128)S(1)}, u32[]{:S(2)}, u32[]{:S(2)}) %collective-permute-start.8) | collective-permute-done | bytes 65568 | tf_op jit(solution)/shard_map/ppermute | solution.py:284
  36.3 4.0 %factor_first.1 = (f32[128,128]{1,0:T(8,128)S(1)}, bf16[256,256]{1,0:T(8,128)(2,1)S(1)}, bf16[256,128]{1,0:T(8,128)(2,1)S(1)}) custom-call(f32[128,128]{1,0:T(8,128)S(1)} %add_add_fusion.2.refs_0_), custom_call_target="tpu_custom_call" | custom-call | tf_op jit(solution)/shard_map/factor_first/pallas_call | solution.py:123
  40.3 0.0 collective-permute-done.before_ref
  40.3 0.0 collective-permute-done.1.after_ref
  40.3 0.0 copy-start
  40.3 1.6 %copy-done = bf16[16,4,128,128]{3,2,1,0:T(8,128)(2,1)S(1)} copy-done((bf16[16,4,128,128]{3,2,1,0:T(8,128)(2,1)S(1)}, bf16[16,4,128,128]{3,2,1,0:T(8,128)(2,1)}, u32[]{:S(2)}) %copy-start) | copy-done | bytes 2097176
  41.9 0.0 copy-start.3
  41.9 1.2 %copy-done.3 = f32[2048,128]{1,0:T(8,128)S(1)} copy-done((f32[2048,128]{1,0:T(8,128)S(1)}, f32[2048,128]{1,0:T(8,128)}, u32[]{:S(2)}) %copy-start.3) | copy-done | bytes 1048600
  43.1 0.0 copy-start.1
  43.1 5.5 %first_and_sums.1 = (bf16[6144,256]{1,0:T(8,128)(2,1)S(1)}, f32[128,128]{1,0:T(8,128)S(1)}, f32[128,128]{1,0:T(8,128)S(1)}) custom-call(s32[16,4]{1,0:T(8,128)S(1)} %copy.8.cols_ref, f32[2048,128]{1,0:T(8,128)S(1)} %collective-permute-done.before_ref, f32[2048,128]{1,0:T(8,128)S(1)} %copy-done.3, f32[2048,128]{1,0:T(8,128)S(1)} %collective-permute-done.1.after_ref, ...), custom_call_target="tpu_custom_call" | custom-call | tf_op jit(solution)/shard_map/first_and_sums/pallas_call | solution.py:217
  48.7 0.1 collective-permute-start.9
  48.8 1.2 %collective-permute-done.9 = f32[128,128]{1,0:T(8,128)S(1)} collective-permute-done((f32[128,128]{1,0:T(8,128)S(1)}, f32[128,128]{1,0:T(8,128)S(1)}, u32[]{:S(2)}, u32[]{:S(2)}) %collective-permute-start.9) | collective-permute-done | bytes 65568 | tf_op jit(solution)/shard_map/ppermute | solution.py:284
  50.1 1.3 %collective-permute-start.10 = (f32[128,128]{1,0:T(8,128)S(1)}, f32[128,128]{1,0:T(8,128)S(1)}, u32[]{:S(2)}, u32[]{:S(2)}) collective-permute-start(f32[128,128]{1,0:T(8,128)S(1)} %select_add_fusion), channel_id=1, source_target_pairs={{0,1},{1,0},{2,3},{3,2},{4,5},{5,4},{6,7},{7,6},{8,9},{9,8},{10,11... | collective-permute-start | bytes 196616 | tf_op jit(solution)/shard_map/ppermute | solution.py:284
  51.4 1.3 %collective-permute-start.11 = (f32[128,128]{1,0:T(8,128)S(1)}, f32[128,128]{1,0:T(8,128)S(1)}, u32[]{:S(2)}, u32[]{:S(2)}) collective-permute-start(f32[128,128]{1,0:T(8,128)S(1)} %select_add_fusion), channel_id=1, source_target_pairs={{0,4},{1,5},{2,6},{3,7},{4,0},{5,1},{6,2},{7,3},{8,12},{9,13},{10,... | collective-permute-start | bytes 196616 | tf_op jit(solution)/shard_map/ppermute | solution.py:284
  52.7 1.0 %collective-permute-start.12 = (f32[128,128]{1,0:T(8,128)S(1)}, f32[128,128]{1,0:T(8,128)S(1)}, u32[]{:S(2)}, u32[]{:S(2)}) collective-permute-start(f32[128,128]{1,0:T(8,128)S(1)} %select_add_fusion), channel_id=1, source_target_pairs={{0,5},{1,4},{2,7},{3,6},{4,1},{5,0},{6,3},{7,2},{8,13},{9,12},{10,... | collective-permute-start | bytes 196616 | tf_op jit(solution)/shard_map/ppermute | solution.py:284
  53.6 0.8 %collective-permute-done.10 = f32[128,128]{1,0:T(8,128)S(1)} collective-permute-done((f32[128,128]{1,0:T(8,128)S(1)}, f32[128,128]{1,0:T(8,128)S(1)}, u32[]{:S(2)}, u32[]{:S(2)}) %collective-permute-start.10) | collective-permute-done | bytes 65568 | tf_op jit(solution)/shard_map/ppermute | solution.py:284
  54.4 1.3 %collective-permute-done.11 = f32[128,128]{1,0:T(8,128)S(1)} collective-permute-done((f32[128,128]{1,0:T(8,128)S(1)}, f32[128,128]{1,0:T(8,128)S(1)}, u32[]{:S(2)}, u32[]{:S(2)}) %collective-permute-start.11) | collective-permute-done | bytes 65568 | tf_op jit(solution)/shard_map/ppermute | solution.py:284
  55.7 2.2 %collective-permute-done.12 = f32[128,128]{1,0:T(8,128)S(1)} collective-permute-done((f32[128,128]{1,0:T(8,128)S(1)}, f32[128,128]{1,0:T(8,128)S(1)}, u32[]{:S(2)}, u32[]{:S(2)}) %collective-permute-start.12) | collective-permute-done | bytes 65568 | tf_op jit(solution)/shard_map/ppermute | solution.py:284
  57.8 0.9 %collective-permute-start.13 = (f32[128,128]{1,0:T(8,128)S(1)}, f32[128,128]{1,0:T(8,128)S(1)}, u32[]{:S(2)}, u32[]{:S(2)}) collective-permute-start(f32[128,128]{1,0:T(8,128)S(1)} %add_add_fusion.1), channel_id=1, source_target_pairs={{0,8},{1,9},{2,10},{3,11},{4,12},{5,13},{6,14},{7,15},{8,0},{9,1},... | collective-permute-start | bytes 196616 | tf_op jit(solution)/shard_map/ppermute | solution.py:284
  58.8 0.4 collective-permute-start.14
  59.2 3.1 %collective-permute-start.15 = (f32[128,128]{1,0:T(8,128)S(1)}, f32[128,128]{1,0:T(8,128)S(1)}, u32[]{:S(2)}, u32[]{:S(2)}) collective-permute-start(f32[128,128]{1,0:T(8,128)S(1)} %add_add_fusion.1), channel_id=1, source_target_pairs={{0,24},{1,25},{2,26},{3,27},{4,28},{5,29},{6,30},{7,31},{8,16},{9,... | collective-permute-start | bytes 196616 | tf_op jit(solution)/shard_map/ppermute | solution.py:284
  62.3 0.0 collective-permute-done.13
  62.3 3.1 %collective-permute-done.14 = f32[128,128]{1,0:T(8,128)S(1)} collective-permute-done((f32[128,128]{1,0:T(8,128)S(1)}, f32[128,128]{1,0:T(8,128)S(1)}, u32[]{:S(2)}, u32[]{:S(2)}) %collective-permute-start.14) | collective-permute-done | bytes 65568 | tf_op jit(solution)/shard_map/ppermute | solution.py:284
  65.4 0.0 collective-permute-done.15
  65.5 0.1 collective-permute-start.16
  65.5 1.2 %collective-permute-done.16 = f32[128,128]{1,0:T(8,128)S(1)} collective-permute-done((f32[128,128]{1,0:T(8,128)S(1)}, f32[128,128]{1,0:T(8,128)S(1)}, u32[]{:S(2)}, u32[]{:S(2)}) %collective-permute-start.16) | collective-permute-done | bytes 65568 | tf_op jit(solution)/shard_map/ppermute | solution.py:284
  66.8 5.7 %factor_second.1 = (bf16[256,256]{1,0:T(8,128)(2,1)S(1)}, f32[128,128]{1,0:T(8,128)}, f32[128,128]{1,0:T(8,128)}) custom-call(f32[128,128]{1,0:T(8,128)S(1)} %get-tuple-element.27.refs_0_, f32[128,128]{1,0:T(8,128)S(1)} %get-tuple-element.26.refs_1_, f32[128,128]{1,0:T(8,128)S(1)} %get-tuple-element.20.refs_2_), custom_call_target="tpu_custom_call" | custom-call | tf_op jit(solution)/shard_map/factor_second/pallas_call | solution.py:149
  72.5 0.0 copy-done.1
  72.5 4.6 %modes_and_apply.1 = (f32[2048,128]{1,0:T(8,128)}, bf16[2048,128]{1,0:T(8,128)(2,1)}) custom-call(s32[16,4]{1,0:T(8,128)S(1)} %copy.8.cols_ref, bf16[6144,256]{1,0:T(8,128)(2,1)S(1)} %get-tuple-element.17.f_ref, bf16[256,256]{1,0:T(8,128)(2,1)S(1)} %get-tuple-element.21.w1_ref, bf16[16,4,128,128]{3,2,1,0:T(8,128)(2,1)S(1)} %copy-done.1), custom_call_target="tpu_custom_call" | custom-call | tf_op jit(solution)/shard_map/modes_and_apply/pallas_call | solution.py:258
  (8 shorter events, 0.1 us)
Async XLA Ops:
  0.6 39.7 %collective-permute-start = (f32[2048,128]{1,0:T(8,128)}, f32[2048,128]{1,0:T(8,128)S(1)}, u32[]{:S(2)}, u32[]{:S(2)}) collective-permute-start(f32[2048,128]{1,0:T(8,128)} %s_ref.3), channel_id=1, source_target_pairs={{0,2},{2,4},{4,6},{6,8},{8,10},{10,12},{12,14},{14,16},{16,18},{18... | collective-permute-start | bytes 3145736 | tf_op jit(solution)/shard_map/ppermute | solution.py:300
  3.1 37.3 %collective-permute-start.1 = (f32[2048,128]{1,0:T(8,128)}, f32[2048,128]{1,0:T(8,128)S(1)}, u32[]{:S(2)}, u32[]{:S(2)}) collective-permute-start(f32[2048,128]{1,0:T(8,128)} %s_ref.3), channel_id=1, source_target_pairs={{2,0},{4,2},{6,4},{8,6},{10,8},{12,10},{14,12},{16,14},{18,16},{20... | collective-permute-start | bytes 3145736 | tf_op jit(solution)/shard_map/ppermute | solution.py:301
  4.4 1.2 %copy-start.2 = (f32[2048,128]{1,0:T(8,128)S(1)}, f32[2048,128]{1,0:T(8,128)}, u32[]{:S(2)}) copy-start(f32[2048,128]{1,0:T(8,128)} %s_ref.3) | copy-start | bytes 3145732
  6.3 4.2 %collective-permute-start.2 = (f32[128,128]{1,0:T(8,128)S(1)}, f32[128,128]{1,0:T(8,128)S(1)}, u32[]{:S(2)}, u32[]{:S(2)}) collective-permute-start(f32[128,128]{1,0:T(8,128)S(1)} %local_gram.1), channel_id=1, source_target_pairs={{0,2},{1,3},{2,0},{3,1},{4,6},{5,7},{6,4},{7,5},{8,10},{9,11},{10,... | collective-permute-start | bytes 196616 | tf_op jit(solution)/shard_map/ppermute | solution.py:284
  10.4 15.5 %collective-permute-start.3 = (f32[128,128]{1,0:T(8,128)S(1)}, f32[128,128]{1,0:T(8,128)S(1)}, u32[]{:S(2)}, u32[]{:S(2)}) collective-permute-start(f32[128,128]{1,0:T(8,128)S(1)} %add.46), channel_id=1, source_target_pairs={{0,8},{1,9},{2,10},{3,11},{4,12},{5,13},{6,14},{7,15},{8,0},{9,1},... | collective-permute-start | bytes 196616 | tf_op jit(solution)/shard_map/ppermute | solution.py:284
  13.4 14.2 %collective-permute-start.4 = (f32[128,128]{1,0:T(8,128)S(1)}, f32[128,128]{1,0:T(8,128)S(1)}, u32[]{:S(2)}, u32[]{:S(2)}) collective-permute-start(f32[128,128]{1,0:T(8,128)S(1)} %add.46), channel_id=1, source_target_pairs={{0,16},{1,17},{2,18},{3,19},{4,20},{5,21},{6,22},{7,23},{8,24},{9,... | collective-permute-start | bytes 196616 | tf_op jit(solution)/shard_map/ppermute | solution.py:284
  16.0 13.5 %collective-permute-start.5 = (f32[128,128]{1,0:T(8,128)S(1)}, f32[128,128]{1,0:T(8,128)S(1)}, u32[]{:S(2)}, u32[]{:S(2)}) collective-permute-start(f32[128,128]{1,0:T(8,128)S(1)} %add.46), channel_id=1, source_target_pairs={{0,24},{1,25},{2,26},{3,27},{4,28},{5,29},{6,30},{7,31},{8,16},{9,... | collective-permute-start | bytes 196616 | tf_op jit(solution)/shard_map/ppermute | solution.py:284
  29.5 4.3 %collective-permute-start.6 = (f32[128,128]{1,0:T(8,128)S(1)}, f32[128,128]{1,0:T(8,128)S(1)}, u32[]{:S(2)}, u32[]{:S(2)}) collective-permute-start(f32[128,128]{1,0:T(8,128)S(1)} %add_add_fusion.3), channel_id=1, source_target_pairs={{0,1},{1,0},{2,3},{3,2},{4,5},{5,4},{6,7},{7,6},{8,9},{9,8},{10,11... | collective-permute-start | bytes 196616 | tf_op jit(solution)/shard_map/ppermute | solution.py:284
  31.1 4.3 %collective-permute-start.7 = (f32[128,128]{1,0:T(8,128)S(1)}, f32[128,128]{1,0:T(8,128)S(1)}, u32[]{:S(2)}, u32[]{:S(2)}) collective-permute-start(f32[128,128]{1,0:T(8,128)S(1)} %add_add_fusion.3), channel_id=1, source_target_pairs={{0,4},{1,5},{2,6},{3,7},{4,0},{5,1},{6,2},{7,3},{8,12},{9,13},{10,... | collective-permute-start | bytes 196616 | tf_op jit(solution)/shard_map/ppermute | solution.py:284
  31.1 5.2 %collective-permute-start.8 = (f32[128,128]{1,0:T(8,128)S(1)}, f32[128,128]{1,0:T(8,128)S(1)}, u32[]{:S(2)}, u32[]{:S(2)}) collective-permute-start(f32[128,128]{1,0:T(8,128)S(1)} %add_add_fusion.3), channel_id=1, source_target_pairs={{0,5},{1,4},{2,7},{3,6},{4,1},{5,0},{6,3},{7,2},{8,13},{9,12},{10,... | collective-permute-start | bytes 196616 | tf_op jit(solution)/shard_map/ppermute | solution.py:284
  40.3 1.6 %copy-start = (bf16[16,4,128,128]{3,2,1,0:T(8,128)(2,1)S(1)}, bf16[16,4,128,128]{3,2,1,0:T(8,128)(2,1)}, u32[]{:S(2)}) copy-start(bf16[16,4,128,128]{3,2,1,0:T(8,128)(2,1)} %jb_ref.3) | copy-start | bytes 6291460
  41.9 1.2 %copy-start.3 = (f32[2048,128]{1,0:T(8,128)S(1)}, f32[2048,128]{1,0:T(8,128)}, u32[]{:S(2)}) copy-start(f32[2048,128]{1,0:T(8,128)} %s_ref.3) | copy-start | bytes 3145732
  43.1 29.4 %copy-start.1 = (bf16[16,4,128,128]{3,2,1,0:T(8,128)(2,1)S(1)}, bf16[16,4,128,128]{3,2,1,0:T(8,128)(2,1)}, u32[]{:S(2)}) copy-start(bf16[16,4,128,128]{3,2,1,0:T(8,128)(2,1)} %jb_ref.3) | copy-start | bytes 6291460
  48.7 1.3 %collective-permute-start.9 = (f32[128,128]{1,0:T(8,128)S(1)}, f32[128,128]{1,0:T(8,128)S(1)}, u32[]{:S(2)}, u32[]{:S(2)}) collective-permute-start(f32[128,128]{1,0:T(8,128)S(1)} %broadcast_select_fusion.2), channel_id=1, source_target_pairs={{0,2},{1,3},{2,0},{3,1},{4,6},{5,7},{6,4},{7,5},{8,10},{9,11},{10,... | collective-permute-start | bytes 196616 | tf_op jit(solution)/shard_map/ppermute | solution.py:284
  50.1 4.3 %collective-permute-start.10 = (f32[128,128]{1,0:T(8,128)S(1)}, f32[128,128]{1,0:T(8,128)S(1)}, u32[]{:S(2)}, u32[]{:S(2)}) collective-permute-start(f32[128,128]{1,0:T(8,128)S(1)} %select_add_fusion), channel_id=1, source_target_pairs={{0,1},{1,0},{2,3},{3,2},{4,5},{5,4},{6,7},{7,6},{8,9},{9,8},{10,11... | collective-permute-start | bytes 196616 | tf_op jit(solution)/shard_map/ppermute | solution.py:284
  51.4 4.3 %collective-permute-start.11 = (f32[128,128]{1,0:T(8,128)S(1)}, f32[128,128]{1,0:T(8,128)S(1)}, u32[]{:S(2)}, u32[]{:S(2)}) collective-permute-start(f32[128,128]{1,0:T(8,128)S(1)} %select_add_fusion), channel_id=1, source_target_pairs={{0,4},{1,5},{2,6},{3,7},{4,0},{5,1},{6,2},{7,3},{8,12},{9,13},{10,... | collective-permute-start | bytes 196616 | tf_op jit(solution)/shard_map/ppermute | solution.py:284
  52.7 5.2 %collective-permute-start.12 = (f32[128,128]{1,0:T(8,128)S(1)}, f32[128,128]{1,0:T(8,128)S(1)}, u32[]{:S(2)}, u32[]{:S(2)}) collective-permute-start(f32[128,128]{1,0:T(8,128)S(1)} %select_add_fusion), channel_id=1, source_target_pairs={{0,5},{1,4},{2,7},{3,6},{4,1},{5,0},{6,3},{7,2},{8,13},{9,12},{10,... | collective-permute-start | bytes 196616 | tf_op jit(solution)/shard_map/ppermute | solution.py:284
  57.8 4.5 %collective-permute-start.13 = (f32[128,128]{1,0:T(8,128)S(1)}, f32[128,128]{1,0:T(8,128)S(1)}, u32[]{:S(2)}, u32[]{:S(2)}) collective-permute-start(f32[128,128]{1,0:T(8,128)S(1)} %add_add_fusion.1), channel_id=1, source_target_pairs={{0,8},{1,9},{2,10},{3,11},{4,12},{5,13},{6,14},{7,15},{8,0},{9,1},... | collective-permute-start | bytes 196616 | tf_op jit(solution)/shard_map/ppermute | solution.py:284
  58.8 6.7 %collective-permute-start.14 = (f32[128,128]{1,0:T(8,128)S(1)}, f32[128,128]{1,0:T(8,128)S(1)}, u32[]{:S(2)}, u32[]{:S(2)}) collective-permute-start(f32[128,128]{1,0:T(8,128)S(1)} %add_add_fusion.1), channel_id=1, source_target_pairs={{0,16},{1,17},{2,18},{3,19},{4,20},{5,21},{6,22},{7,23},{8,24},{9,... | collective-permute-start | bytes 196616 | tf_op jit(solution)/shard_map/ppermute | solution.py:284
  59.2 6.3 %collective-permute-start.15 = (f32[128,128]{1,0:T(8,128)S(1)}, f32[128,128]{1,0:T(8,128)S(1)}, u32[]{:S(2)}, u32[]{:S(2)}) collective-permute-start(f32[128,128]{1,0:T(8,128)S(1)} %add_add_fusion.1), channel_id=1, source_target_pairs={{0,24},{1,25},{2,26},{3,27},{4,28},{5,29},{6,30},{7,31},{8,16},{9,... | collective-permute-start | bytes 196616 | tf_op jit(solution)/shard_map/ppermute | solution.py:284
  65.5 1.3 %collective-permute-start.16 = (f32[128,128]{1,0:T(8,128)S(1)}, f32[128,128]{1,0:T(8,128)S(1)}, u32[]{:S(2)}, u32[]{:S(2)}) collective-permute-start(f32[128,128]{1,0:T(8,128)S(1)} %add_add_fusion), channel_id=1, source_target_pairs={{0,2},{1,3},{2,0},{3,1},{4,6},{5,7},{6,4},{7,5},{8,10},{9,11},{10,... | collective-permute-start | bytes 196616 | tf_op jit(solution)/shard_map/ppermute | solution.py:284

commit v3 on v2

v3 whole, which is shorter than its diff:
```python
import math

import jax
import jax.numpy as jnp
from jax import lax
from jax.experimental import pallas as pl
from jax.experimental.pallas import tpu as pltpu
from jax.sharding import PartitionSpec as P

F32 = jnp.float32
BF16 = jnp.bfloat16
HIGH = lax.Precision.HIGHEST
VMEM_LIMIT = 24 * 1024 * 1024
CHUNK = 512
TILE = 256


def mm(a, b, contract=(1, 0)):
    return lax.dot_general(a, b, (((contract[0],), (contract[1],)), ((), ())), preferred_element_type=F32)


def split2(x):
    h = x.astype(BF16)
    return h, (x - h.astype(F32)).astype(BF16)


def split3(x):
    h = x.astype(BF16)
    r = x - h.astype(F32)
    m = r.astype(BF16)
    return h, m, (r - m.astype(F32)).astype(BF16)


def rows_of(i, n):
    return pl.ds(pl.multiple_of(i * n, n), n)


def two_sum(a, b):
    s = a + b
    t = s - a
    return s, (a - (s - t)) + (b - t)


def descending(terms):
    high, low = terms[0], jnp.zeros_like(terms[0])
    for term in terms[1:]:
        high, error = two_sum(high, term)
        low = low + error
    return high, low


def add_pairs(a, b):
    high, error = two_sum(a[0], b[0])
    low = (a[1] + b[1]) + error
    total = high + low
    return jnp.stack([total, low - (total - high)])


def power_of_two(x):
    q = x * float(2**23 + 1)
    return 2.0 * jnp.abs(q - q * (1.0 - 2.0**-24))


def cut(x, size, n):
    grid = size * (1.5 * 2.0**16)
    parts = []
    for _ in range(n):
        part = (x + grid) - grid
        x = x - part
        parts.append(part.astype(BF16))
        grid = grid * 2.0**-8
    return parts, x


def gram_kernel(s_hbm, g_ref, s_ref, sem):
    rows, k = s_ref.shape
    chunks = rows // CHUNK
    copies = [
        pltpu.make_async_copy(s_hbm.at[pl.ds(c * CHUNK, CHUNK)], s_ref.at[pl.ds(c * CHUNK, CHUNK)], sem.at[c])
        for c in range(chunks)
    ]
    for copy in copies:
        copy.start()
    top = jnp.zeros((8, k), F32)
    for c, copy in enumerate(copies):
        copy.wait()
        rows_here = jnp.abs(s_ref[c * CHUNK : (c + 1) * CHUNK, :])
        top = jnp.maximum(top, jnp.max(rows_here.reshape(CHUNK // 8, 8, k), axis=0))
    size = power_of_two(jnp.max(top, axis=0, keepdims=True))
    zero = jnp.zeros((k, k), F32)
    aa, aa_low, ab, ab_low, odd, even = zero, zero, zero, zero, zero, zero
    for c in range(chunks):
        one, two, three = jnp.zeros((k, 2 * k), F32), jnp.zeros((2 * k, 2 * k), F32), zero
        for at in range(c * CHUNK, (c + 1) * CHUNK, TILE):
            (p, q, r), _ = cut(s_ref[at : at + TILE, :], size, 3)
            pq = jnp.concatenate([p, q], axis=1)
            one = one + mm(p, pq, (0, 0))
            two = two + mm(pq, jnp.concatenate([r, q], axis=1), (0, 0))
            three = three + mm(r, r, (0, 0))
        aa, error = two_sum(aa, one[:, :k])
        aa_low = aa_low + error
        ab, error = two_sum(ab, one[:, k:])
        ab_low = ab_low + error
        odd = odd + (two[:k, :k] + two[k:, :k])
        even = even + (two[k:, k:] + three)
    cross, cross_low = two_sum(ab, ab.T)
    total, total_low = two_sum(aa, cross)
    low = ab_low + (odd + 0.5 * even)
    low = (aa_low + (cross_low + total_low)) + (low + low.T)
    high = total + low
    g_ref[0] = high
    g_ref[1] = low - (high - total)


def local_gram(s):
    rows, k = s.shape
    return pl.pallas_call(
        gram_kernel,
        in_specs=[pl.BlockSpec(memory_space=pl.ANY)],
        out_shape=jax.ShapeDtypeStruct((2, k, k), F32),
        scratch_shapes=[pltpu.VMEM((rows, k), F32), pltpu.SemaphoreType.DMA((rows // CHUNK,))],
        compiler_params=pltpu.CompilerParams(vmem_limit_bytes=VMEM_LIMIT),
        name="local_gram",
    )(s)


def factor_and_inverse(a):
    k, n = a.shape[0], 8
    blocks = [a[n * i : n * i + n, :] for i in range(k // n)]
    lane = lax.broadcasted_iota(jnp.int32, (n, k), 1)
    sub = lax.broadcasted_iota(jnp.int32, (n, k), 0)
    full = lambda value: jnp.broadcast_to(value, (n, k))
    for p in range(k // n):
        x = blocks[p]
        at = n * p
        columns = [full(x[:, at + t : at + t + 1]) for t in range(n)]
        d = {(s, t): full(columns[t][s : s + 1, :]) for t in range(n) for s in range(t, n)}
        row = [full(x[s : s + 1, :]) for s in range(n)]
        done, scale, low = [], [], {}
        for t in range(n):
            scale.append(lax.rsqrt(d[t, t]))
            here = lane == at + t
            done.append(jnp.where(here, scale[t], row[t] * scale[t]))
            for s in range(t + 1, n):
                low[s, t] = d[s, t] * scale[t]
            for u in range(t + 1, n):
                for s in range(u, n):
                    d[s, u] = d[s, u] - low[s, t] * low[u, t]
            for s in range(t + 1, n):
                row[s] = jnp.where(here, 0.0, row[s]) - low[s, t] * done[t]
        out = done[0]
        for t in range(1, n):
            out = jnp.where(sub == t, done[t], out)
        blocks[p] = out
        panel = (lane >= at) & (lane < at + n)
        terms = [jnp.where(panel & (lane > at + t), 0.0, done[t]) for t in range(n)]
        for i in range(p + 1, k // n):
            x = blocks[i]
            new = jnp.where(panel, 0.0, x)
            column = []
            for t in range(n):
                c = full(x[:, at + t : at + t + 1])
                for u in range(t):
                    c = c - column[u] * low[t, u]
                column.append(c * scale[t])
                new = new - column[t] * terms[t]
            blocks[i] = new
    x = jnp.concatenate(blocks, axis=0)
    r = lax.broadcasted_iota(jnp.int32, (k, k), 0)
    c = lax.broadcasted_iota(jnp.int32, (k, k), 1)
    upper = jnp.where(c > r, x, jnp.where(c == r, 1.0 / x, 0.0))
    return upper, jnp.where(c <= r, x, 0.0)


def scaled(high, low):
    k = high.shape[0]
    r = lax.broadcasted_iota(jnp.int32, (k, k), 0)
    c = lax.broadcasted_iota(jnp.int32, (k, k), 1)
    diagonal = jnp.where(r == c, high, 0.0)
    row = power_of_two(jnp.sqrt(jnp.max(diagonal, axis=0, keepdims=True)))
    col = power_of_two(jnp.sqrt(jnp.max(diagonal, axis=1, keepdims=True)))
    return (high / row) / col, (low / row) / col, row


def by_weight(products, k, n, m):
    block = lambda i, j: products[i * k : (i + 1) * k, j * k : (j + 1) * k]
    return [sum(block(i, t - i) for i in range(n) if 0 <= t - i < m) for t in range(n + m - 1)]


def factors_kernel(count, g_ref, up_ref, w1_ref, w2_ref):
    k = g_ref.shape[1]
    high, low, row = scaled(g_ref[0], g_ref[1])
    up1, inv1 = factor_and_inverse(0.5 * (high + high.T))
    size = power_of_two(jnp.max(jnp.abs(inv1), axis=1, keepdims=True))
    p, left = cut(inv1, size, 3)
    inv1 = inv1 - left
    g, left = cut(high, 1.0, 3)
    g += cut(left + low, 2.0**-24, 2)[0]
    p_rows = jnp.concatenate(p, axis=0)
    y, y_low = descending(by_weight(mm(p_rows, jnp.concatenate(g, axis=1)), k, 3, 5))
    size = power_of_two(jnp.max(jnp.abs(y), axis=1, keepdims=True))
    y, left = cut(y, size, 3)
    y += cut(left + y_low, size * 2.0**-24, 1)[0]
    gram2, low = descending(by_weight(mm(jnp.concatenate(y, axis=0), p_rows, (1, 1)), k, 4, 3))
    gram2 = gram2 + low
    up2, inv2 = factor_and_inverse(0.5 * (gram2 + gram2.T))
    inverse = jnp.dot(inv2, inv1, precision=HIGH, preferred_element_type=F32)
    inverse = (inverse / row) * math.sqrt(count)
    h, m, l = split3(inverse.T)
    hm = jnp.concatenate([h, m], axis=1)
    w1_ref[...] = jnp.concatenate([hm, hm], axis=0)
    w2_ref[...] = jnp.concatenate([l, h], axis=0)
    upper = jnp.dot(up2, up1, precision=HIGH, preferred_element_type=F32)
    up_ref[...] = (upper * row) / math.sqrt(count)


def factors(g, count):
    k = g.shape[1]
    return pl.pallas_call(
        lambda *refs: factors_kernel(count, *refs),
        out_shape=(
            jax.ShapeDtypeStruct((k, k), F32),
            jax.ShapeDtypeStruct((2 * k, 2 * k), BF16),
            jax.ShapeDtypeStruct((2 * k, k), BF16),
        ),
        compiler_params=pltpu.CompilerParams(vmem_limit_bytes=VMEM_LIMIT),
        name="factors",
    )(g)


def last_kernel(
    cols_ref, s_hbm, chip_hbm, inner_hbm, outer_hbm, w1_ref, w2_ref, jb_hbm, modes_hbm, jm_hbm, red_ref,
    s_ref, jb_ref, modes_ref, jm_ref, mb_ref, hm_ref, sem,
):
    _, rows, k = s_ref.shape
    block_rows, slots, blk, _ = jb_ref.shape
    per = rows // TILE
    place = lax.axis_index("bulk")
    get = [pltpu.make_async_copy(ref, s_ref.at[i], sem.at[i]) for i, ref in enumerate((s_hbm, chip_hbm, inner_hbm))]
    get_outer = pltpu.make_async_copy(outer_hbm, s_ref.at[2], sem.at[2])
    get_jb = pltpu.make_async_copy(jb_hbm, jb_ref, sem.at[3])
    put_modes = pltpu.make_async_copy(modes_ref, modes_hbm, sem.at[4])
    put_jm = pltpu.make_async_copy(jm_ref, jm_hbm, sem.at[5])
    is_inner = (place % 4 == 1) | (place % 4 == 2)
    get[0].start()
    get[1].start()

    @pl.when(is_inner)
    def _():
        get[2].start()

    @pl.when(jnp.logical_not(is_inner))
    def _():
        get_outer.start()

    get_jb.start()
    odd = place % 2
    offsets = (per, (2 - 2 * odd) * per, 2 * odd * per)

    for part, offset in enumerate(offsets):
        get[part].wait()

        def body(c, carry, part=part, offset=offset):
            h, m, l = split3(s_ref[part, rows_of(c, TILE), :])
            p = mm(jnp.concatenate([h, m], axis=1), w1_ref[...])
            q = mm(jnp.concatenate([h, l], axis=1), w2_ref[...])
            modes = p[:, :k] + (p[:, k:] + q)
            high, low = split2(modes)
            mb_ref[rows_of(c + offset, TILE), :] = high
            if part == 0:
                modes_ref[rows_of(c, TILE), :] = modes
                hm_ref[rows_of(c, TILE), :] = jnp.concatenate([high, low], axis=1)
            return carry

        lax.fori_loop(0, per, body, 0, unroll=4)
        if part == 0:
            put_modes.start()

    get_jb.wait()
    start = cols_ref[0, 0]

    def apply(r, carry):
        acc = jnp.zeros((blk, k), F32)
        for n in range(0, slots, 2):
            lhs = jnp.concatenate([jb_ref[r, n], jb_ref[r, n + 1]], axis=1)
            picked = []
            for p in (n, n + 1):
                index = cols_ref[r, p] - start + block_rows
                picked.append(mb_ref[rows_of(index, blk), :])
            acc = acc + mm(lhs, jnp.concatenate(picked, axis=0))
        jm_ref[rows_of(r, blk), :] = acc.astype(BF16)
        return carry

    lax.fori_loop(0, block_rows, apply, 0, unroll=4)
    put_jm.start()

    def project(c, acc):
        at = rows_of(c, TILE)
        return acc + mm(hm_ref[at, :], jm_ref[at, :], (0, 0))

    acc = lax.fori_loop(0, per, project, jnp.zeros((2 * k, k), F32), unroll=4)
    red_ref[...] = acc[:k, :] + acc[k:, :]
    put_modes.wait()
    put_jm.wait()


def last(cols, s, chip, inner, outer, w1, w2, jb):
    rows, k = s.shape
    vmem, hbm = pl.BlockSpec(memory_space=pltpu.VMEM), pl.BlockSpec(memory_space=pl.ANY)
    return pl.pallas_call(
        last_kernel,
        in_specs=[pl.BlockSpec(memory_space=pltpu.SMEM)] + [hbm] * 4 + [vmem] * 2 + [hbm],
        out_specs=(hbm, hbm, vmem),
        out_shape=(
            jax.ShapeDtypeStruct((rows, k), F32),
            jax.ShapeDtypeStruct((rows, k), BF16),
            jax.ShapeDtypeStruct((k, k), F32),
        ),
        scratch_shapes=[
            pltpu.VMEM((3, rows, k), F32),
            pltpu.VMEM(jb.shape, BF16),
            pltpu.VMEM((rows, k), F32),
            pltpu.VMEM((rows, k), BF16),
            pltpu.VMEM((3 * rows, k), BF16),
            pltpu.VMEM((rows, 2 * k), BF16),
            pltpu.SemaphoreType.DMA((6,)),
        ],
        compiler_params=pltpu.CompilerParams(vmem_limit_bytes=VMEM_LIMIT),
        name="modes_and_apply",
    )(cols, s, chip, inner, outer, w1, w2, jb)


def solution(mesh):
    axes = tuple(mesh.axis_names)
    sizes = dict(mesh.shape)
    n_bulk, n_span = sizes["bulk"], sizes["span"]
    count = n_bulk * n_span
    weight = {"bulk": n_span, "span": 1} if axes[0] == "bulk" else {"bulk": 1, "span": n_bulk}
    bits = lambda n: [1 << i for i in range(n.bit_length() - 1)]
    core_mask = weight["bulk"]
    masks = [m * weight["span"] for m in bits(n_span)] + [m * weight["bulk"] for m in bits(n_bulk)[1:]]
    phases = [masks[i : i + 2] for i in range(0, len(masks), 2)]
    masks_x, masks_y = [core_mask * 2], masks[:1]
    others = [m for m in masks if m not in masks_x + masks_y]
    masks_far = [others[i : i + 2] for i in range(0, len(others), 2)]

    def swap(value, mask):
        return lax.ppermute(value, axes, [(i, i ^ mask) for i in range(count)])

    def exchange(value, phase, add):
        if len(phase) == 1:
            return add(value, swap(value, phase[0]))
        a, b = phase
        pa, pb, pab = swap(value, a), swap(value, b), swap(value, a | b)
        return add(add(value, pa), add(pb, pab))

    def shards(snapshots, jac_blocks, jac_cols):
        rows_total = snapshots.shape[0] * count
        even = lax.axis_index("bulk") % 2 == 0
        pairs = lambda first: [p for i in range(first, n_bulk - 1, 4) for p in ((i, i + 1), (i + 1, i))]
        chip = swap(snapshots, core_mask)
        inner = lax.ppermute(snapshots, "bulk", pairs(1))
        gram = local_gram(snapshots)
        half = gram.shape[1] // 2
        upper, lower = gram[:, :half], gram[:, half:]
        mine = add_pairs(jnp.where(even, upper, lower), swap(jnp.where(even, lower, upper), core_mask))
        for phase in masks_far:
            mine = exchange(mine, phase, add_pairs)
        mine, inner = lax.optimization_barrier((mine, inner))
        mine = exchange(mine, masks_x, add_pairs)
        mine, late = lax.optimization_barrier((mine, snapshots))
        outer = lax.ppermute(late, "bulk", pairs(3))
        mine = exchange(mine, masks_y, add_pairs)
        other = swap(mine, core_mask)
        gram = jnp.concatenate([jnp.where(even, mine, other), jnp.where(even, other, mine)], axis=1)
        factor, w1, w2 = factors(gram, rows_total)
        modes, jac_modes, reduced = last(jac_cols, snapshots, chip, inner, outer, w1, w2, jac_blocks)
        reduced = reduced + swap(reduced, core_mask)
        for phase in phases:
            reduced = exchange(reduced, phase, jnp.add)
        return modes, factor, jac_modes, reduced / rows_total

    rows = P(("span", "bulk"), None)
    return jax.shard_map(
        shards,
        mesh=mesh,
        in_specs=(rows, P(("span", "bulk"), None, None, None), rows),
        out_specs=(rows, P(), rows, P()),
        check_vma=False,
    )
```

time: 77.4 us -> 64.3 us (0.83)
  waiting for transfers between devices: 26.6 us -> 21.9 us
  local copies, waits for them, and re-layouts: 4.79 us -> 1.32 us
  Pallas kernels: 20.5 us -> 17.1 us
  starting transfers between devices: 24.3 us -> 22.2 us
    ppermute x15, waiting for transfers between devices: 26.6 us -> 21.9 us  [swap(): return lax.ppermute(value, axes, [(i, i ^ mask) for i in range(count)])]
    pallas_call x4 -> x2, Pallas kernels: 15.9 us -> 11.3 us  [the longest x1 10.2 us: factors(): pl.pallas_call(lambda *refs: factors_kernel(count, *refs), out_shape=(jax...]
    unnamed x9, local copies, waits for them, and re-layouts: 4.79 us -> 1.32 us
    ppermute x15, starting transfers between devices: 20.6 us -> 18.9 us  [swap(): return lax.ppermute(value, axes, [(i, i ^ mask) for i in range(count)])]
    pallas_call x1, Pallas kernels: 4.6 us -> 5.72 us  [last(): pl.pallas_call(last_kernel, in_specs=[pl.BlockSpec(memory_space=pltpu.SME...]
  transfers between devices with their start and end apart: 17 -> 17, of which waited for: 12 -> 12; matrix products, arithmetic and copies ran while one was open for 1% -> 0% of each run, Pallas kernels for 6% -> 18%
where the time goes in v3:
time: 64.3 us; the launch traced here: 64.1 us
  starting transfers between devices  22.2 us (35%)
  waiting for transfers between devices  21.9 us (34%)
  Pallas kernels  17.1 us (27%)
  local copies, waits for them, and re-layouts  1.32 us (2%)
  other arithmetic  0.85 us (1%)
  between operations  0.79 us (1%)
    ppermute x15, waiting for transfers between devices, swap(): return lax.ppermute(value, axes, [(i, i ^ mask) for i in range(count)])  21.9 us
    ppermute x15, starting transfers between devices, swap(): return lax.ppermute(value, axes, [(i, i ^ mask) for i in range(count)])  18.9 us
    pallas_call x1, Pallas kernels, factors(): pl.pallas_call(lambda *refs: factors_kernel(count, *refs), out_shape=(jax...  10.2 us
    pallas_call x1, Pallas kernels, last(): pl.pallas_call(last_kernel, in_specs=[pl.BlockSpec(memory_space=pltpu.SME...  5.72 us
    ppermute x1, starting transfers between devices, shards(): outer = lax.ppermute(late, 'bulk', pairs(3))  1.65 us
    ppermute x1, starting transfers between devices, shards(): inner = lax.ppermute(snapshots, 'bulk', pairs(1))  1.62 us
    unnamed x9, local copies, waits for them, and re-layouts  1.32 us
  transfers between devices with their start and end apart: 17, of which 12 were waited for; matrix products, arithmetic and copies ran while one was open for 0% of the time, Pallas kernels for 18%

profile of v3, /device:TPU:0, one launch (start us, length us, event | category | flops | bytes accessed | tf_op | source)
XLA Modules:
  0.0 64.1 jit_solution(15525270141484093766)
XLA Ops:
  0.6 0.0 copy-start.3
  0.6 1.6 %collective-permute-start.5 = (f32[2048,128]{1,0:T(8,128)}, f32[2048,128]{1,0:T(8,128)}, u32[]{:S(2)}, u32[]{:S(2)}) collective-permute-start(f32[2048,128]{1,0:T(8,128)} %s_hbm.3), channel_id=1, source_target_pairs={{2,4},{4,2},{10,12},{12,10},{18,20},{20,18},{26,28},{28,26},{3,5},... | collective-permute-start | bytes 3145736 | tf_op jit(solution)/shard_map/ppermute | solution.py:362
  2.3 0.0 copy-start
  2.3 1.2 %copy-done = f32[2048,128]{1,0:T(8,128)S(1)} copy-done((f32[2048,128]{1,0:T(8,128)S(1)}, f32[2048,128]{1,0:T(8,128)}, u32[]{:S(2)}) %copy-start) | copy-done | bytes 1048600
  3.5 0.0 copy-start.1
  3.5 0.0 copy-start.2
  3.5 1.2 %local_gram.1 = f32[2,128,128]{2,1,0:T(8,128)S(1)} custom-call(f32[2048,128]{1,0:T(8,128)S(1)} %copy-done), custom_call_target="tpu_custom_call" | custom-call | tf_op jit(solution)/shard_map/local_gram/pallas_call | solution.py:117
  4.7 3.4 %collective-permute-start.1 = (f32[2,64,128]{2,1,0:T(8,128)S(1)}, f32[2,64,128]{2,1,0:T(8,128)S(1)}, u32[]{:S(2)}, u32[]{:S(2)}) collective-permute-start(f32[2,64,128]{2,1,0:T(8,128)S(1)} %get-tuple-element.37), channel_id=1, source_target_pairs={{0,2},{1,3},{2,0},{3,1},{4,6},{5,7},{6,4},{7,5},{8,10},{9,11},{10,... | collective-permute-start | bytes 196616 | tf_op jit(solution)/shard_map/ppermute | solution.py:348
  8.1 0.9 %collective-permute-done.1 = f32[2,64,128]{2,1,0:T(8,128)S(1)} collective-permute-done((f32[2,64,128]{2,1,0:T(8,128)S(1)}, f32[2,64,128]{2,1,0:T(8,128)S(1)}, u32[]{:S(2)}, u32[]{:S(2)}) %collective-permute-start.1) | collective-permute-done | bytes 65568 | tf_op jit(solution)/shard_map/ppermute | solution.py:348
  9.1 3.7 %collective-permute-start.4 = (f32[2,64,128]{2,1,0:T(8,128)S(1)}, f32[2,64,128]{2,1,0:T(8,128)S(1)}, u32[]{:S(2)}, u32[]{:S(2)}) collective-permute-start(f32[2,64,128]{2,1,0:T(8,128)S(1)} %pad_maximum_fusion.1), channel_id=1, source_target_pairs={{0,24},{1,25},{2,26},{3,27},{4,28},{5,29},{6,30},{7,31},{8,16},{9,... | collective-permute-start | bytes 196616 | tf_op jit(solution)/shard_map/ppermute | solution.py:348
  12.7 0.0 collective-permute-start.3
  12.7 0.8 %collective-permute-start.2 = (f32[2,64,128]{2,1,0:T(8,128)S(1)}, f32[2,64,128]{2,1,0:T(8,128)S(1)}, u32[]{:S(2)}, u32[]{:S(2)}) collective-permute-start(f32[2,64,128]{2,1,0:T(8,128)S(1)} %pad_maximum_fusion.1), channel_id=1, source_target_pairs={{0,8},{1,9},{2,10},{3,11},{4,12},{5,13},{6,14},{7,15},{8,0},{9,1},... | collective-permute-start | bytes 196616 | tf_op jit(solution)/shard_map/ppermute | solution.py:348
  13.5 2.1 %collective-permute-done.4 = f32[2,64,128]{2,1,0:T(8,128)S(1)} collective-permute-done((f32[2,64,128]{2,1,0:T(8,128)S(1)}, f32[2,64,128]{2,1,0:T(8,128)S(1)}, u32[]{:S(2)}, u32[]{:S(2)}) %collective-permute-start.4) | collective-permute-done | bytes 65568 | tf_op jit(solution)/shard_map/ppermute | solution.py:348
  15.6 3.1 %collective-permute-done.3 = f32[2,64,128]{2,1,0:T(8,128)S(1)} collective-permute-done((f32[2,64,128]{2,1,0:T(8,128)S(1)}, f32[2,64,128]{2,1,0:T(8,128)S(1)}, u32[]{:S(2)}, u32[]{:S(2)}) %collective-permute-start.3) | collective-permute-done | bytes 65568 | tf_op jit(solution)/shard_map/ppermute | solution.py:348
  18.7 0.0 collective-permute-done.2
  18.8 0.0 collective-permute-done.5.inner_hbm
  18.8 1.2 %collective-permute-start.6 = (f32[2,64,128]{2,1,0:T(8,128)S(1)}, f32[2,64,128]{2,1,0:T(8,128)S(1)}, u32[]{:S(2)}, u32[]{:S(2)}) collective-permute-start(f32[2,64,128]{2,1,0:T(8,128)S(1)} %pad_maximum_fusion.2), channel_id=1, source_target_pairs={{0,4},{1,5},{2,6},{3,7},{4,0},{5,1},{6,2},{7,3},{8,12},{9,13},{10,... | collective-permute-start | bytes 196616 | tf_op jit(solution)/shard_map/ppermute | solution.py:348
  20.0 0.0 copy-done.1
  20.0 0.0 collective-permute-start
  20.0 3.1 %collective-permute-done.6 = f32[2,64,128]{2,1,0:T(8,128)S(1)} collective-permute-done((f32[2,64,128]{2,1,0:T(8,128)S(1)}, f32[2,64,128]{2,1,0:T(8,128)S(1)}, u32[]{:S(2)}, u32[]{:S(2)}) %collective-permute-start.6) | collective-permute-done | bytes 65568 | tf_op jit(solution)/shard_map/ppermute | solution.py:348
  23.2 1.7 %collective-permute-start.7 = (f32[2048,128]{1,0:T(8,128)S(1)}, f32[2048,128]{1,0:T(8,128)}, u32[]{:S(2)}, u32[]{:S(2)}) collective-permute-start(f32[2048,128]{1,0:T(8,128)S(1)} %copy-done.1), channel_id=1, source_target_pairs={{6,8},{8,6},{14,16},{16,14},{22,24},{24,22},{7,9},{9,7},{15,17},{1... | collective-permute-start | bytes 3145736 | tf_op jit(solution)/shard_map/ppermute | solution.py:372
  24.8 1.5 %collective-permute-start.8 = (f32[2,64,128]{2,1,0:T(8,128)S(1)}, f32[2,64,128]{2,1,0:T(8,128)S(1)}, u32[]{:S(2)}, u32[]{:S(2)}) collective-permute-start(f32[2,64,128]{2,1,0:T(8,128)S(1)} %pad_maximum_fusion.3), channel_id=1, source_target_pairs={{0,1},{1,0},{2,3},{3,2},{4,5},{5,4},{6,7},{7,6},{8,9},{9,8},{10,11... | collective-permute-start | bytes 196616 | tf_op jit(solution)/shard_map/ppermute | solution.py:348
  26.4 2.7 %collective-permute-done.8 = f32[2,64,128]{2,1,0:T(8,128)S(1)} collective-permute-done((f32[2,64,128]{2,1,0:T(8,128)S(1)}, f32[2,64,128]{2,1,0:T(8,128)S(1)}, u32[]{:S(2)}, u32[]{:S(2)}) %collective-permute-start.8) | collective-permute-done | bytes 65568 | tf_op jit(solution)/shard_map/ppermute | solution.py:348
  29.1 0.1 collective-permute-start.9
  29.2 0.0 copy-done.3
  29.2 0.1 copy.7.cols_ref
  29.3 1.1 %collective-permute-done.9 = f32[2,64,128]{2,1,0:T(8,128)S(1)} collective-permute-done((f32[2,64,128]{2,1,0:T(8,128)S(1)}, f32[2,64,128]{2,1,0:T(8,128)S(1)}, u32[]{:S(2)}, u32[]{:S(2)}) %collective-permute-start.9) | collective-permute-done | bytes 65568 | tf_op jit(solution)/shard_map/ppermute | solution.py:348
  30.5 10.2 %factors.1 = (f32[128,128]{1,0:T(8,128)}, bf16[256,256]{1,0:T(8,128)(2,1)S(1)}, bf16[256,128]{1,0:T(8,128)(2,1)S(1)}) custom-call(f32[2,128,128]{2,1,0:T(8,128)S(1)} %pad_maximum_fusion.refs_0_), custom_call_target="tpu_custom_call" | custom-call | tf_op jit(solution)/shard_map/factors/pallas_call | solution.py:219
  40.7 0.0 collective-permute-done.chip_hbm
  40.7 0.0 collective-permute-done.7.outer_hbm
  40.7 0.0 copy-done.2
  40.7 5.7 %modes_and_apply.1 = (f32[2048,128]{1,0:T(8,128)}, bf16[2048,128]{1,0:T(8,128)(2,1)}, f32[128,128]{1,0:T(8,128)S(1)}) custom-call(s32[16,4]{1,0:T(8,128)S(1)} %copy.7.cols_ref, f32[2048,128]{1,0:T(8,128)S(1)} %copy-done.1, f32[2048,128]{1,0:T(8,128)} %collective-permute-done.chip_hbm, f32[2048,128]{1,0:T(8,128)} %collective-permute-done.5.inner_hbm, ...), custom_call_target="tpu_custom_call" | custom-call | tf_op jit(solution)/shard_map/modes_and_apply/pallas_call | solution.py:310
  46.4 0.2 collective-permute-start.10
  46.6 1.1 %collective-permute-done.10 = f32[128,128]{1,0:T(8,128)S(1)} collective-permute-done((f32[128,128]{1,0:T(8,128)S(1)}, f32[128,128]{1,0:T(8,128)S(1)}, u32[]{:S(2)}, u32[]{:S(2)}) %collective-permute-start.10) | collective-permute-done | bytes 65568 | tf_op jit(solution)/shard_map/ppermute | solution.py:348
  47.7 2.6 %collective-permute-start.13 = (f32[128,128]{1,0:T(8,128)S(1)}, f32[128,128]{1,0:T(8,128)S(1)}, u32[]{:S(2)}, u32[]{:S(2)}) collective-permute-start(f32[128,128]{1,0:T(8,128)S(1)} %add.216), channel_id=1, source_target_pairs={{0,5},{1,4},{2,7},{3,6},{4,1},{5,0},{6,3},{7,2},{8,13},{9,12},{10,... | collective-permute-start | bytes 196616 | tf_op jit(solution)/shard_map/ppermute | solution.py:348
  50.4 0.4 collective-permute-start.12
  50.8 0.5 collective-permute-start.11
  51.3 1.7 %collective-permute-done.13 = f32[128,128]{1,0:T(8,128)S(1)} collective-permute-done((f32[128,128]{1,0:T(8,128)S(1)}, f32[128,128]{1,0:T(8,128)S(1)}, u32[]{:S(2)}, u32[]{:S(2)}) %collective-permute-start.13) | collective-permute-done | bytes 65568 | tf_op jit(solution)/shard_map/ppermute | solution.py:348
  53.0 1.7 %collective-permute-done.12 = f32[128,128]{1,0:T(8,128)S(1)} collective-permute-done((f32[128,128]{1,0:T(8,128)S(1)}, f32[128,128]{1,0:T(8,128)S(1)}, u32[]{:S(2)}, u32[]{:S(2)}) %collective-permute-start.12) | collective-permute-done | bytes 65568 | tf_op jit(solution)/shard_map/ppermute | solution.py:348
  54.6 0.4 collective-permute-done.11
  55.1 3.3 %collective-permute-start.16 = (f32[128,128]{1,0:T(8,128)S(1)}, f32[128,128]{1,0:T(8,128)S(1)}, u32[]{:S(2)}, u32[]{:S(2)}) collective-permute-start(f32[128,128]{1,0:T(8,128)S(1)} %add_add_fusion), channel_id=1, source_target_pairs={{0,24},{1,25},{2,26},{3,27},{4,28},{5,29},{6,30},{7,31},{8,16},{9,... | collective-permute-start | bytes 196616 | tf_op jit(solution)/shard_map/ppermute | solution.py:348
  58.3 0.0 collective-permute-start.15
  58.3 1.2 %collective-permute-start.14 = (f32[128,128]{1,0:T(8,128)S(1)}, f32[128,128]{1,0:T(8,128)S(1)}, u32[]{:S(2)}, u32[]{:S(2)}) collective-permute-start(f32[128,128]{1,0:T(8,128)S(1)} %add_add_fusion), channel_id=1, source_target_pairs={{0,8},{1,9},{2,10},{3,11},{4,12},{5,13},{6,14},{7,15},{8,0},{9,1},... | collective-permute-start | bytes 196616 | tf_op jit(solution)/shard_map/ppermute | solution.py:348
  59.5 1.8 %collective-permute-done.16 = f32[128,128]{1,0:T(8,128)S(1)} collective-permute-done((f32[128,128]{1,0:T(8,128)S(1)}, f32[128,128]{1,0:T(8,128)S(1)}, u32[]{:S(2)}, u32[]{:S(2)}) %collective-permute-start.16) | collective-permute-done | bytes 65568 | tf_op jit(solution)/shard_map/ppermute | solution.py:348
  61.3 2.2 %collective-permute-done.15 = f32[128,128]{1,0:T(8,128)S(1)} collective-permute-done((f32[128,128]{1,0:T(8,128)S(1)}, f32[128,128]{1,0:T(8,128)S(1)}, u32[]{:S(2)}, u32[]{:S(2)}) %collective-permute-start.15) | collective-permute-done | bytes 65568 | tf_op jit(solution)/shard_map/ppermute | solution.py:348
  63.5 0.0 collective-permute-done.14
  63.5 0.6 %add_multiply_fusion = f32[128,128]{1,0:T(8,128)} fusion(f32[128,128]{1,0:T(8,128)S(1)} %collective-permute-done.15, f32[128,128]{1,0:T(8,128)S(1)} %collective-permute-done.16, f32[128,128]{1,0:T(8,128)S(1)} %add_add_fusion, f32[128,128]{1,0:T(8,128)S(1)} %collective-permute-done.14), kind=kLoop, calls=%fused_computation.5 | loop fusion | flops 65536 | bytes 327680 | tf_op jit(solution)/shard_map/div | solution.py:381
  (14 shorter events, 0.2 us)
Async XLA Ops:
  0.6 28.6 %copy-start.3 = (s32[16,4]{0,1:T(4,128)S(1)}, s32[16,4]{0,1:T(4,128)}, u32[]{:S(2)}) copy-start(s32[16,4]{0,1:T(4,128)} %param.5) | copy-start | bytes 772
  0.6 18.2 %collective-permute-start.5 = (f32[2048,128]{1,0:T(8,128)}, f32[2048,128]{1,0:T(8,128)}, u32[]{:S(2)}, u32[]{:S(2)}) collective-permute-start(f32[2048,128]{1,0:T(8,128)} %s_hbm.3), channel_id=1, source_target_pairs={{2,4},{4,2},{10,12},{12,10},{18,20},{20,18},{26,28},{28,26},{3,5},... | collective-permute-start | bytes 3145736 | tf_op jit(solution)/shard_map/ppermute | solution.py:362
  2.3 1.2 %copy-start = (f32[2048,128]{1,0:T(8,128)S(1)}, f32[2048,128]{1,0:T(8,128)}, u32[]{:S(2)}) copy-start(f32[2048,128]{1,0:T(8,128)} %s_hbm.3) | copy-start | bytes 3145732
  3.5 16.5 %copy-start.1 = (f32[2048,128]{1,0:T(8,128)S(1)}, f32[2048,128]{1,0:T(8,128)}, u32[]{:S(2)}) copy-start(f32[2048,128]{1,0:T(8,128)} %s_hbm.3) | copy-start | bytes 3145732
  3.5 37.2 %copy-start.2 = (bf16[16,4,128,128]{3,2,1,0:T(8,128)(2,1)S(1)}, bf16[16,4,128,128]{3,2,1,0:T(8,128)(2,1)}, u32[]{:S(2)}) copy-start(bf16[16,4,128,128]{3,2,1,0:T(8,128)(2,1)} %jb_hbm.1) | copy-start | bytes 6291460
  4.7 4.3 %collective-permute-start.1 = (f32[2,64,128]{2,1,0:T(8,128)S(1)}, f32[2,64,128]{2,1,0:T(8,128)S(1)}, u32[]{:S(2)}, u32[]{:S(2)}) collective-permute-start(f32[2,64,128]{2,1,0:T(8,128)S(1)} %get-tuple-element.37), channel_id=1, source_target_pairs={{0,2},{1,3},{2,0},{3,1},{4,6},{5,7},{6,4},{7,5},{8,10},{9,11},{10,... | collective-permute-start | bytes 196616 | tf_op jit(solution)/shard_map/ppermute | solution.py:348
  9.1 6.5 %collective-permute-start.4 = (f32[2,64,128]{2,1,0:T(8,128)S(1)}, f32[2,64,128]{2,1,0:T(8,128)S(1)}, u32[]{:S(2)}, u32[]{:S(2)}) collective-permute-start(f32[2,64,128]{2,1,0:T(8,128)S(1)} %pad_maximum_fusion.1), channel_id=1, source_target_pairs={{0,24},{1,25},{2,26},{3,27},{4,28},{5,29},{6,30},{7,31},{8,16},{9,... | collective-permute-start | bytes 196616 | tf_op jit(solution)/shard_map/ppermute | solution.py:348
  12.7 6.0 %collective-permute-start.3 = (f32[2,64,128]{2,1,0:T(8,128)S(1)}, f32[2,64,128]{2,1,0:T(8,128)S(1)}, u32[]{:S(2)}, u32[]{:S(2)}) collective-permute-start(f32[2,64,128]{2,1,0:T(8,128)S(1)} %pad_maximum_fusion.1), channel_id=1, source_target_pairs={{0,16},{1,17},{2,18},{3,19},{4,20},{5,21},{6,22},{7,23},{8,24},{9,... | collective-permute-start | bytes 196616 | tf_op jit(solution)/shard_map/ppermute | solution.py:348
  12.7 6.0 %collective-permute-start.2 = (f32[2,64,128]{2,1,0:T(8,128)S(1)}, f32[2,64,128]{2,1,0:T(8,128)S(1)}, u32[]{:S(2)}, u32[]{:S(2)}) collective-permute-start(f32[2,64,128]{2,1,0:T(8,128)S(1)} %pad_maximum_fusion.1), channel_id=1, source_target_pairs={{0,8},{1,9},{2,10},{3,11},{4,12},{5,13},{6,14},{7,15},{8,0},{9,1},... | collective-permute-start | bytes 196616 | tf_op jit(solution)/shard_map/ppermute | solution.py:348
  18.8 4.3 %collective-permute-start.6 = (f32[2,64,128]{2,1,0:T(8,128)S(1)}, f32[2,64,128]{2,1,0:T(8,128)S(1)}, u32[]{:S(2)}, u32[]{:S(2)}) collective-permute-start(f32[2,64,128]{2,1,0:T(8,128)S(1)} %pad_maximum_fusion.2), channel_id=1, source_target_pairs={{0,4},{1,5},{2,6},{3,7},{4,0},{5,1},{6,2},{7,3},{8,12},{9,13},{10,... | collective-permute-start | bytes 196616 | tf_op jit(solution)/shard_map/ppermute | solution.py:348
  20.0 20.6 %collective-permute-start = (f32[2048,128]{1,0:T(8,128)S(1)}, f32[2048,128]{1,0:T(8,128)}, u32[]{:S(2)}, u32[]{:S(2)}) collective-permute-start(f32[2048,128]{1,0:T(8,128)S(1)} %copy-done.1), channel_id=1, source_target_pairs={{0,2},{1,3},{2,0},{3,1},{4,6},{5,7},{6,4},{7,5},{8,10},{9,11},{10,... | collective-permute-start | bytes 3145736 | tf_op jit(solution)/shard_map/ppermute | solution.py:348
  23.2 17.5 %collective-permute-start.7 = (f32[2048,128]{1,0:T(8,128)S(1)}, f32[2048,128]{1,0:T(8,128)}, u32[]{:S(2)}, u32[]{:S(2)}) collective-permute-start(f32[2048,128]{1,0:T(8,128)S(1)} %copy-done.1), channel_id=1, source_target_pairs={{6,8},{8,6},{14,16},{16,14},{22,24},{24,22},{7,9},{9,7},{15,17},{1... | collective-permute-start | bytes 3145736 | tf_op jit(solution)/shard_map/ppermute | solution.py:372
  24.8 4.3 %collective-permute-start.8 = (f32[2,64,128]{2,1,0:T(8,128)S(1)}, f32[2,64,128]{2,1,0:T(8,128)S(1)}, u32[]{:S(2)}, u32[]{:S(2)}) collective-permute-start(f32[2,64,128]{2,1,0:T(8,128)S(1)} %pad_maximum_fusion.3), channel_id=1, source_target_pairs={{0,1},{1,0},{2,3},{3,2},{4,5},{5,4},{6,7},{7,6},{8,9},{9,8},{10,11... | collective-permute-start | bytes 196616 | tf_op jit(solution)/shard_map/ppermute | solution.py:348
  29.1 1.3 %collective-permute-start.9 = (f32[2,64,128]{2,1,0:T(8,128)S(1)}, f32[2,64,128]{2,1,0:T(8,128)S(1)}, u32[]{:S(2)}, u32[]{:S(2)}) collective-permute-start(f32[2,64,128]{2,1,0:T(8,128)S(1)} %pad_maximum_fusion.4), channel_id=1, source_target_pairs={{0,2},{1,3},{2,0},{3,1},{4,6},{5,7},{6,4},{7,5},{8,10},{9,11},{10,... | collective-permute-start | bytes 196616 | tf_op jit(solution)/shard_map/ppermute | solution.py:348
  46.4 1.3 %collective-permute-start.10 = (f32[128,128]{1,0:T(8,128)S(1)}, f32[128,128]{1,0:T(8,128)S(1)}, u32[]{:S(2)}, u32[]{:S(2)}) collective-permute-start(f32[128,128]{1,0:T(8,128)S(1)} %get-tuple-element.23), channel_id=1, source_target_pairs={{0,2},{1,3},{2,0},{3,1},{4,6},{5,7},{6,4},{7,5},{8,10},{9,11},{10,... | collective-permute-start | bytes 196616 | tf_op jit(solution)/shard_map/ppermute | solution.py:348
  47.7 5.3 %collective-permute-start.13 = (f32[128,128]{1,0:T(8,128)S(1)}, f32[128,128]{1,0:T(8,128)S(1)}, u32[]{:S(2)}, u32[]{:S(2)}) collective-permute-start(f32[128,128]{1,0:T(8,128)S(1)} %add.216), channel_id=1, source_target_pairs={{0,5},{1,4},{2,7},{3,6},{4,1},{5,0},{6,3},{7,2},{8,13},{9,12},{10,... | collective-permute-start | bytes 196616 | tf_op jit(solution)/shard_map/ppermute | solution.py:348
  50.4 4.3 %collective-permute-start.12 = (f32[128,128]{1,0:T(8,128)S(1)}, f32[128,128]{1,0:T(8,128)S(1)}, u32[]{:S(2)}, u32[]{:S(2)}) collective-permute-start(f32[128,128]{1,0:T(8,128)S(1)} %add.216), channel_id=1, source_target_pairs={{0,4},{1,5},{2,6},{3,7},{4,0},{5,1},{6,2},{7,3},{8,12},{9,13},{10,... | collective-permute-start | bytes 196616 | tf_op jit(solution)/shard_map/ppermute | solution.py:348
  50.8 4.3 %collective-permute-start.11 = (f32[128,128]{1,0:T(8,128)S(1)}, f32[128,128]{1,0:T(8,128)S(1)}, u32[]{:S(2)}, u32[]{:S(2)}) collective-permute-start(f32[128,128]{1,0:T(8,128)S(1)} %add.216), channel_id=1, source_target_pairs={{0,1},{1,0},{2,3},{3,2},{4,5},{5,4},{6,7},{7,6},{8,9},{9,8},{10,11... | collective-permute-start | bytes 196616 | tf_op jit(solution)/shard_map/ppermute | solution.py:348
  55.1 6.2 %collective-permute-start.16 = (f32[128,128]{1,0:T(8,128)S(1)}, f32[128,128]{1,0:T(8,128)S(1)}, u32[]{:S(2)}, u32[]{:S(2)}) collective-permute-start(f32[128,128]{1,0:T(8,128)S(1)} %add_add_fusion), channel_id=1, source_target_pairs={{0,24},{1,25},{2,26},{3,27},{4,28},{5,29},{6,30},{7,31},{8,16},{9,... | collective-permute-start | bytes 196616 | tf_op jit(solution)/shard_map/ppermute | solution.py:348
  58.3 5.2 %collective-permute-start.15 = (f32[128,128]{1,0:T(8,128)S(1)}, f32[128,128]{1,0:T(8,128)S(1)}, u32[]{:S(2)}, u32[]{:S(2)}) collective-permute-start(f32[128,128]{1,0:T(8,128)S(1)} %add_add_fusion), channel_id=1, source_target_pairs={{0,16},{1,17},{2,18},{3,19},{4,20},{5,21},{6,22},{7,23},{8,24},{9,... | collective-permute-start | bytes 196616 | tf_op jit(solution)/shard_map/ppermute | solution.py:348
  58.3 5.2 %collective-permute-start.14 = (f32[128,128]{1,0:T(8,128)S(1)}, f32[128,128]{1,0:T(8,128)S(1)}, u32[]{:S(2)}, u32[]{:S(2)}) collective-permute-start(f32[128,128]{1,0:T(8,128)S(1)} %add_add_fusion), channel_id=1, source_target_pairs={{0,8},{1,9},{2,10},{3,11},{4,12},{5,13},{6,14},{7,15},{8,0},{9,1},... | collective-permute-start | bytes 196616 | tf_op jit(solution)/shard_map/ppermute | solution.py:348

commit v4 on v3

--- a/solution.py
+++ b/solution.py
@@ -29,6 +29,10 @@
     r = x - h.astype(F32)
     m = r.astype(BF16)
     return h, m, (r - m.astype(F32)).astype(BF16)
+
+
+def in_vmem(x):
+    return pltpu.with_memory_space_constraint(x, pltpu.VMEM)
 
 
 def rows_of(i, n):
@@ -124,18 +128,21 @@
     )(s)
 
 
-def factor_and_inverse(a):
+def inverse_factor(a):
     k, n = a.shape[0], 8
     blocks = [a[n * i : n * i + n, :] for i in range(k // n)]
     lane = lax.broadcasted_iota(jnp.int32, (n, k), 1)
     sub = lax.broadcasted_iota(jnp.int32, (n, k), 0)
     full = lambda value: jnp.broadcast_to(value, (n, k))
+    column_of = lambda x, j: full(x[:, j : j + 1])
+    row_of = lambda x, s: full(x[s : s + 1, :])
+    below = [(s, t) for t in range(n) for s in range(t, n)]
+    first = [column_of(blocks[0], t) for t in range(n)]
+    d = {(s, t): row_of(first[t], s) for s, t in below}
+    rows = []
     for p in range(k // n):
-        x = blocks[p]
         at = n * p
-        columns = [full(x[:, at + t : at + t + 1]) for t in range(n)]
-        d = {(s, t): full(columns[t][s : s + 1, :]) for t in range(n) for s in range(t, n)}
-        row = [full(x[s : s + 1, :]) for s in range(n)]
+        row = [row_of(blocks[p], s) for s in range(n)]
         done, scale, low = [], [], {}
         for t in range(n):
             scale.append(lax.rsqrt(d[t, t]))
@@ -151,7 +158,7 @@
         out = done[0]
         for t in range(1, n):
             out = jnp.where(sub == t, done[t], out)
-        blocks[p] = out
+        rows.append(out)
         panel = (lane >= at) & (lane < at + n)
         terms = [jnp.where(panel & (lane > at + t), 0.0, done[t]) for t in range(n)]
         for i in range(p + 1, k // n):
@@ -159,17 +166,44 @@
             new = jnp.where(panel, 0.0, x)
             column = []
             for t in range(n):
-                c = full(x[:, at + t : at + t + 1])
+                c = column_of(x, at + t)
                 for u in range(t):
                     c = c - column[u] * low[t, u]
                 column.append(c * scale[t])
                 new = new - column[t] * terms[t]
             blocks[i] = new
-    x = jnp.concatenate(blocks, axis=0)
+            if i == p + 1:
+                ahead = [column_of(x, at + n + s) for s in range(n)]
+                parts = [[row_of(c, s) for s in range(n)] for c in column]
+                for t in range(n - 1):
+                    for s in range(n):
+                        ahead[s] = ahead[s] - column[t] * parts[t][s]
+                last = parts[n - 1]
+                d = {(s, t): row_of(ahead[t], s) - last[s] * last[t] for s, t in below}
+    x = jnp.concatenate(rows, axis=0)
     r = lax.broadcasted_iota(jnp.int32, (k, k), 0)
     c = lax.broadcasted_iota(jnp.int32, (k, k), 1)
-    upper = jnp.where(c > r, x, jnp.where(c == r, 1.0 / x, 0.0))
-    return upper, jnp.where(c <= r, x, 0.0)
+    return jnp.where(c <= r, x, 0.0)
+
+
+def mm3(a, b, contract=(1, 0)):
+    ah, am = split2(a)
+    bh, bm = split2(b)
+    return mm(ah, bh, contract) + (mm(ah, bm, contract) + mm(am, bh, contract))
+
+
+def inverse_factor_near_one(e):
+    k = e.shape[0]
+    r = lax.broadcasted_iota(jnp.int32, (k, k), 0)
+    c = lax.broadcasted_iota(jnp.int32, (k, k), 1)
+    half = lambda x: jnp.where(c < r, x, jnp.where(c == r, 0.5 * x, 0.0))
+    f = half(e)
+    ff = mm3(f, f)
+    n = half(mm3(f, f, (1, 1)) + (ff + ff.T)) - f
+    ne = mm3(n, e)
+    left = (e + (n + n.T)) + ((ne + ne.T) + mm3(n + ne, n, (1, 1)))
+    step = half(left)
+    return jnp.where(c == r, 1.0, 0.0) + (n - (step + mm3(step, n)))
 
 
 def scaled(high, low):
@@ -187,10 +221,10 @@
     return [sum(block(i, t - i) for i in range(n) if 0 <= t - i < m) for t in range(n + m - 1)]
 
 
-def factors_kernel(count, g_ref, up_ref, w1_ref, w2_ref):
+def factors_kernel(count, g_ref, up_ref, w1_ref, w2_ref, inv2_ref):
     k = g_ref.shape[1]
     high, low, row = scaled(g_ref[0], g_ref[1])
-    up1, inv1 = factor_and_inverse(0.5 * (high + high.T))
+    inv1 = inverse_factor(0.5 * (high + high.T))
     size = power_of_two(jnp.max(jnp.abs(inv1), axis=1, keepdims=True))
     p, left = cut(inv1, size, 3)
     inv1 = inv1 - left
@@ -199,19 +233,30 @@
     p_rows = jnp.concatenate(p, axis=0)
     y, y_low = descending(by_weight(mm(p_rows, jnp.concatenate(g, axis=1)), k, 3, 5))
     size = power_of_two(jnp.max(jnp.abs(y), axis=1, keepdims=True))
-    y, left = cut(y, size, 3)
-    y += cut(left + y_low, size * 2.0**-24, 1)[0]
-    gram2, low = descending(by_weight(mm(jnp.concatenate(y, axis=0), p_rows, (1, 1)), k, 4, 3))
-    gram2 = gram2 + low
-    up2, inv2 = factor_and_inverse(0.5 * (gram2 + gram2.T))
-    inverse = jnp.dot(inv2, inv1, precision=HIGH, preferred_element_type=F32)
-    inverse = (inverse / row) * math.sqrt(count)
+    parts, left = cut(y, size, 3)
+    parts += cut(left + y_low, size * 2.0**-24, 1)[0]
+    gram2, low = descending(by_weight(mm(jnp.concatenate(parts, axis=0), p_rows, (1, 1)), k, 4, 3))
+    r = lax.broadcasted_iota(jnp.int32, (k, k), 0)
+    c = lax.broadcasted_iota(jnp.int32, (k, k), 1)
+    e = jnp.where(c == r, gram2 - 1.0, gram2) + low
+    e = 0.5 * (e + e.T)
+    near = jnp.sum(e * e) <= 1.0 / 64.0
+
+    @pl.when(near)
+    def _():
+        inv2_ref[...] = inverse_factor_near_one(e)
+
+    @pl.when(jnp.logical_not(near))
+    def _():
+        inv2_ref[...] = inverse_factor(jnp.where(c == r, 1.0 + e, e))
+
+    both = jnp.dot(inv2_ref[...], jnp.concatenate([inv1, y], axis=1), precision=HIGH, preferred_element_type=F32)
+    inverse = (both[:, :k] / row) * math.sqrt(count)
     h, m, l = split3(inverse.T)
     hm = jnp.concatenate([h, m], axis=1)
     w1_ref[...] = jnp.concatenate([hm, hm], axis=0)
     w2_ref[...] = jnp.concatenate([l, h], axis=0)
-    upper = jnp.dot(up2, up1, precision=HIGH, preferred_element_type=F32)
-    up_ref[...] = (upper * row) / math.sqrt(count)
+    up_ref[...] = jnp.where(c >= r, (both[:, k:] * row) / math.sqrt(count), 0.0)
 
 
 def factors(g, count):
@@ -223,111 +268,141 @@
             jax.ShapeDtypeStruct((2 * k, 2 * k), BF16),
             jax.ShapeDtypeStruct((2 * k, k), BF16),
         ),
+        scratch_shapes=[pltpu.VMEM((k, k), F32)],
         compiler_params=pltpu.CompilerParams(vmem_limit_bytes=VMEM_LIMIT),
         name="factors",
     )(g)
 
 
-def last_kernel(
-    cols_ref, s_hbm, chip_hbm, inner_hbm, outer_hbm, w1_ref, w2_ref, jb_hbm, modes_hbm, jm_hbm, red_ref,
-    s_ref, jb_ref, modes_ref, jm_ref, mb_ref, hm_ref, sem,
+def modes_of(rows, w1, w2):
+    k = rows.shape[1]
+    h, m, l = split3(rows)
+    p = mm(jnp.concatenate([h, m], axis=1), w1)
+    q = mm(jnp.concatenate([h, l], axis=1), w2)
+    return p[:, :k] + (p[:, k:] + q)
+
+
+def pieces(source, target, sem):
+    n = target.shape[0] // 4
+    return [
+        pltpu.make_async_copy(source.at[pl.ds(i * n, n)], target.at[pl.ds(i * n, n)], sem.at[i]) for i in range(4)
+    ]
+
+
+def chip_kernel(s_ref, chip_ref, w1_ref, w2_ref, modes_hbm, low_ref, mb_ref, modes_ref, put_sem):
+    rows = s_ref.shape[0]
+    put = pieces(modes_ref, modes_hbm, put_sem)
+    per = rows // TILE // 4
+    for c in range(4 * per):
+        at = slice(c * TILE, (c + 1) * TILE)
+        modes = modes_of(s_ref[at, :], w1_ref[...], w2_ref[...])
+        modes_ref[at, :] = modes
+        mb_ref[0, at, :], low_ref[at, :] = split2(modes)
+        if (c + 1) % per == 0:
+            put[c // per].start()
+    for c in range(4 * per):
+        at = slice(c * TILE, (c + 1) * TILE)
+        mb_ref[1, at, :] = modes_of(chip_ref[at, :], w1_ref[...], w2_ref[...]).astype(BF16)
+    for copy in put:
+        copy.wait()
+
+
+def chip_modes(s, chip, w1, w2):
+    rows, k = s.shape
+    vmem, hbm = pl.BlockSpec(memory_space=pltpu.VMEM), pl.BlockSpec(memory_space=pl.ANY)
+    return pl.pallas_call(
+        chip_kernel,
+        in_specs=[vmem] * 4,
+        out_specs=(hbm, vmem, vmem),
+        out_shape=(
+            jax.ShapeDtypeStruct((rows, k), F32),
+            pltpu.VMEM((rows, k), BF16),
+            pltpu.VMEM((2, rows, k), BF16),
+        ),
+        scratch_shapes=[
+            pltpu.VMEM((rows, k), F32),
+            pltpu.SemaphoreType.DMA((4,)),
+        ],
+        compiler_params=pltpu.CompilerParams(vmem_limit_bytes=VMEM_LIMIT),
+        name="chip_modes",
+    )(in_vmem(s), in_vmem(chip), in_vmem(w1), in_vmem(w2))
+
+
+def apply_kernel(
+    cols_hbm, low_ref, mb_ref, inner_ref, outer_ref, w1_ref, w2_ref, jb_ref, jm_hbm, red_ref,
+    all_ref, jm_ref, cols_ref, sem, put_sem,
 ):
-    _, rows, k = s_ref.shape
+    rows, k = low_ref.shape
     block_rows, slots, blk, _ = jb_ref.shape
-    per = rows // TILE
     place = lax.axis_index("bulk")
-    get = [pltpu.make_async_copy(ref, s_ref.at[i], sem.at[i]) for i, ref in enumerate((s_hbm, chip_hbm, inner_hbm))]
-    get_outer = pltpu.make_async_copy(outer_hbm, s_ref.at[2], sem.at[2])
-    get_jb = pltpu.make_async_copy(jb_hbm, jb_ref, sem.at[3])
-    put_modes = pltpu.make_async_copy(modes_ref, modes_hbm, sem.at[4])
-    put_jm = pltpu.make_async_copy(jm_ref, jm_hbm, sem.at[5])
+    odd = place % 2
+    offsets = (rows, (2 - 2 * odd) * rows, 2 * odd * rows)
+    at = [pl.ds(pl.multiple_of(offset, blk), rows) for offset in offsets]
+    own = pltpu.make_async_copy(mb_ref.at[0], all_ref.at[at[0]], sem.at[0])
+    other = pltpu.make_async_copy(mb_ref.at[1], all_ref.at[at[1]], sem.at[1])
+    get_cols = pltpu.make_async_copy(cols_hbm, cols_ref, sem.at[2])
+    put = pieces(jm_ref, jm_hbm, put_sem)
+    get_cols.start()
+    own.start()
+    other.start()
+
+    def further(ref):
+        for c in range(rows // TILE):
+            modes = modes_of(ref[c * TILE : (c + 1) * TILE, :], w1_ref[...], w2_ref[...])
+            all_ref[rows_of(c + offsets[2] // TILE, TILE), :] = modes.astype(BF16)
+
     is_inner = (place % 4 == 1) | (place % 4 == 2)
-    get[0].start()
-    get[1].start()
-
-    @pl.when(is_inner)
-    def _():
-        get[2].start()
-
-    @pl.when(jnp.logical_not(is_inner))
-    def _():
-        get_outer.start()
-
-    get_jb.start()
-    odd = place % 2
-    offsets = (per, (2 - 2 * odd) * per, 2 * odd * per)
-
-    for part, offset in enumerate(offsets):
-        get[part].wait()
-
-        def body(c, carry, part=part, offset=offset):
-            h, m, l = split3(s_ref[part, rows_of(c, TILE), :])
-            p = mm(jnp.concatenate([h, m], axis=1), w1_ref[...])
-            q = mm(jnp.concatenate([h, l], axis=1), w2_ref[...])
-            modes = p[:, :k] + (p[:, k:] + q)
-            high, low = split2(modes)
-            mb_ref[rows_of(c + offset, TILE), :] = high
-            if part == 0:
-                modes_ref[rows_of(c, TILE), :] = modes
-                hm_ref[rows_of(c, TILE), :] = jnp.concatenate([high, low], axis=1)
-            return carry
-
-        lax.fori_loop(0, per, body, 0, unroll=4)
-        if part == 0:
-            put_modes.start()
-
-    get_jb.wait()
+    pl.when(is_inner)(lambda: further(inner_ref))
+    pl.when(jnp.logical_not(is_inner))(lambda: further(outer_ref))
+    own.wait()
+    other.wait()
+    get_cols.wait()
     start = cols_ref[0, 0]
 
-    def apply(r, carry):
+    def apply(r):
         acc = jnp.zeros((blk, k), F32)
         for n in range(0, slots, 2):
             lhs = jnp.concatenate([jb_ref[r, n], jb_ref[r, n + 1]], axis=1)
             picked = []
             for p in (n, n + 1):
                 index = cols_ref[r, p] - start + block_rows
-                picked.append(mb_ref[rows_of(index, blk), :])
+                picked.append(all_ref[rows_of(index, blk), :])
             acc = acc + mm(lhs, jnp.concatenate(picked, axis=0))
         jm_ref[rows_of(r, blk), :] = acc.astype(BF16)
-        return carry
-
-    lax.fori_loop(0, block_rows, apply, 0, unroll=4)
-    put_jm.start()
+
+    for r in range(block_rows):
+        apply(r)
+        if (r + 1) % (block_rows // 4) == 0:
+            put[r // (block_rows // 4)].start()
 
     def project(c, acc):
         at = rows_of(c, TILE)
-        return acc + mm(hm_ref[at, :], jm_ref[at, :], (0, 0))
-
-    acc = lax.fori_loop(0, per, project, jnp.zeros((2 * k, k), F32), unroll=4)
+        return acc + mm(jnp.concatenate([mb_ref[0, at, :], low_ref[at, :]], axis=1), jm_ref[at, :], (0, 0))
+
+    acc = lax.fori_loop(0, rows // TILE, project, jnp.zeros((2 * k, k), F32), unroll=True)
     red_ref[...] = acc[:k, :] + acc[k:, :]
-    put_modes.wait()
-    put_jm.wait()
-
-
-def last(cols, s, chip, inner, outer, w1, w2, jb):
-    rows, k = s.shape
+    for copy in put:
+        copy.wait()
+
+
+def apply_and_project(cols, low, mb, inner, outer, w1, w2, jb):
+    rows, k = low.shape
     vmem, hbm = pl.BlockSpec(memory_space=pltpu.VMEM), pl.BlockSpec(memory_space=pl.ANY)
     return pl.pallas_call(
-        last_kernel,
-        in_specs=[pl.BlockSpec(memory_space=pltpu.SMEM)] + [hbm] * 4 + [vmem] * 2 + [hbm],
-        out_specs=(hbm, hbm, vmem),
-        out_shape=(
-            jax.ShapeDtypeStruct((rows, k), F32),
-            jax.ShapeDtypeStruct((rows, k), BF16),
-            jax.ShapeDtypeStruct((k, k), F32),
-        ),
+        apply_kernel,
+        in_specs=[hbm] + [vmem] * 7,
+        out_specs=(hbm, vmem),
+        out_shape=(jax.ShapeDtypeStruct((rows, k), BF16), jax.ShapeDtypeStruct((k, k), F32)),
         scratch_shapes=[
-            pltpu.VMEM((3, rows, k), F32),
-            pltpu.VMEM(jb.shape, BF16),
-            pltpu.VMEM((rows, k), F32),
+            pltpu.VMEM((3 * rows, k), BF16),
             pltpu.VMEM((rows, k), BF16),
-            pltpu.VMEM((3 * rows, k), BF16),
-            pltpu.VMEM((rows, 2 * k), BF16),
-            pltpu.SemaphoreType.DMA((6,)),
+            pltpu.SMEM(cols.shape, jnp.int32),
+            pltpu.SemaphoreType.DMA((3,)),
+            pltpu.SemaphoreType.DMA((4,)),
         ],
         compiler_params=pltpu.CompilerParams(vmem_limit_bytes=VMEM_LIMIT),
-        name="modes_and_apply",
-    )(cols, s, chip, inner, outer, w1, w2, jb)
+        name="apply_and_project",
+    )(cols, in_vmem(low), in_vmem(mb), in_vmem(inner), in_vmem(outer), in_vmem(w1), in_vmem(w2), in_vmem(jb))
 
 
 def solution(mesh):
@@ -374,7 +449,8 @@
         other = swap(mine, core_mask)
         gram = jnp.concatenate([jnp.where(even, mine, other), jnp.where(even, other, mine)], axis=1)
         factor, w1, w2 = factors(gram, rows_total)
-        modes, jac_modes, reduced = last(jac_cols, snapshots, chip, inner, outer, w1, w2, jac_blocks)
+        modes, low, mb = chip_modes(snapshots, chip, w1, w2)
+        jac_modes, reduced = apply_and_project(jac_cols, low, mb, inner, outer, w1, w2, jac_blocks)
         reduced = reduced + swap(reduced, core_mask)
         for phase in phases:
             reduced = exchange(reduced, phase, jnp.add)

time: 64.3 us -> 63 us (0.980)
  Pallas kernels: 17.1 us -> 13.5 us
  waiting for transfers between devices: 21.9 us -> 25.1 us
  starting transfers between devices: 22.2 us -> 21.1 us
    pallas_call x1, Pallas kernels: 10.2 us -> 5.87 us  [factors(): pl.pallas_call(lambda *refs: factors_kernel(count, *refs), out_shape=(jax...]
    ppermute x15, waiting for transfers between devices: 21.9 us -> 25.1 us  [swap(): return lax.ppermute(value, axes, [(i, i ^ mask) for i in range(count)])]
    ppermute x15, starting transfers between devices: 18.9 us -> 17.8 us  [swap(): return lax.ppermute(value, axes, [(i, i ^ mask) for i in range(count)])]
    pallas_call x1 -> x2, Pallas kernels: 5.72 us -> 6.49 us  [the longest x1 3.82 us: apply_and_project(): pl.pallas_call(apply_kernel, in_specs=[hbm] + [vmem] * 7, out_specs=(hbm,...]
  transfers between devices with their start and end apart: 17 -> 17, of which waited for: 12 -> 14; matrix products, arithmetic and copies ran while one was open for 0% -> 0% of each run, Pallas kernels for 18% -> 15%
where the time goes in v4:
time: 63 us; the launch traced here: 62.8 us
  waiting for transfers between devices  25.1 us (40%)
  starting transfers between devices  21.1 us (33%)
  Pallas kernels  13.5 us (21%)
  local copies, waits for them, and re-layouts  1.32 us (2%)
  other arithmetic  0.85 us (1%)
  between operations  0.81 us (1%)
    ppermute x15, waiting for transfers between devices, swap(): return lax.ppermute(value, axes, [(i, i ^ mask) for i in range(count)])  25.1 us
    ppermute x15, starting transfers between devices, swap(): return lax.ppermute(value, axes, [(i, i ^ mask) for i in range(count)])  17.8 us
    pallas_call x1, Pallas kernels, factors(): pl.pallas_call(lambda *refs: factors_kernel(count, *refs), out_shape=(jax...  5.87 us
    pallas_call x1, Pallas kernels, apply_and_project(): pl.pallas_call(apply_kernel, in_specs=[hbm] + [vmem] * 7, out_specs=(hbm,...  3.82 us
    pallas_call x1, Pallas kernels, chip_modes(): pl.pallas_call(chip_kernel, in_specs=[vmem] * 4, out_specs=(hbm, vmem, vm...  2.67 us
    ppermute x1, starting transfers between devices, shards(): inner = lax.ppermute(snapshots, 'bulk', pairs(1))  1.66 us
    ppermute x1, starting transfers between devices, shards(): outer = lax.ppermute(late, 'bulk', pairs(3))  1.64 us
    unnamed x9, local copies, waits for them, and re-layouts  1.32 us
  transfers between devices with their start and end apart: 17, of which 14 were waited for; matrix products, arithmetic and copies ran while one was open for 0% of the time, Pallas kernels for 15%

profile of v4, /device:TPU:0, one launch (start us, length us, event | category | flops | bytes accessed | tf_op | source)
XLA Modules:
  0.0 62.8 jit_solution(5632312354527479410)
XLA Ops:
  0.6 1.7 %collective-permute-start.5 = (f32[2048,128]{1,0:T(8,128)}, f32[2048,128]{1,0:T(8,128)}, u32[]{:S(2)}, u32[]{:S(2)}) collective-permute-start(f32[2048,128]{1,0:T(8,128)} %s_ref.1), channel_id=1, source_target_pairs={{2,4},{4,2},{10,12},{12,10},{18,20},{20,18},{26,28},{28,26},{3,5},... | collective-permute-start | bytes 3145736 | tf_op jit(solution)/shard_map/ppermute | solution.py:437
  2.3 0.0 copy-start
  2.3 1.2 %copy-done = f32[2048,128]{1,0:T(8,128)S(1)} copy-done((f32[2048,128]{1,0:T(8,128)S(1)}, f32[2048,128]{1,0:T(8,128)}, u32[]{:S(2)}) %copy-start) | copy-done | bytes 1048600
  3.5 0.0 copy-start.1
  3.5 0.0 copy-start.3
  3.5 1.2 %local_gram.1 = f32[2,128,128]{2,1,0:T(8,128)S(1)} custom-call(f32[2048,128]{1,0:T(8,128)S(1)} %copy-done), custom_call_target="tpu_custom_call" | custom-call | tf_op jit(solution)/shard_map/local_gram/pallas_call | solution.py:121
  4.7 3.4 %collective-permute-start.1 = (f32[2,64,128]{2,1,0:T(8,128)S(1)}, f32[2,64,128]{2,1,0:T(8,128)S(1)}, u32[]{:S(2)}, u32[]{:S(2)}) collective-permute-start(f32[2,64,128]{2,1,0:T(8,128)S(1)} %get-tuple-element.41), channel_id=1, source_target_pairs={{0,2},{1,3},{2,0},{3,1},{4,6},{5,7},{6,4},{7,5},{8,10},{9,11},{10,... | collective-permute-start | bytes 196616 | tf_op jit(solution)/shard_map/ppermute | solution.py:423
  8.1 0.9 %collective-permute-done.1 = f32[2,64,128]{2,1,0:T(8,128)S(1)} collective-permute-done((f32[2,64,128]{2,1,0:T(8,128)S(1)}, f32[2,64,128]{2,1,0:T(8,128)S(1)}, u32[]{:S(2)}, u32[]{:S(2)}) %collective-permute-start.1) | collective-permute-done | bytes 65568 | tf_op jit(solution)/shard_map/ppermute | solution.py:423
  9.1 0.0 copy-start.2
  9.1 1.6 %collective-permute-start.2 = (f32[2,64,128]{2,1,0:T(8,128)S(1)}, f32[2,64,128]{2,1,0:T(8,128)S(1)}, u32[]{:S(2)}, u32[]{:S(2)}) collective-permute-start(f32[2,64,128]{2,1,0:T(8,128)S(1)} %pad_maximum_fusion.1), channel_id=1, source_target_pairs={{0,8},{1,9},{2,10},{3,11},{4,12},{5,13},{6,14},{7,15},{8,0},{9,1},... | collective-permute-start | bytes 196616 | tf_op jit(solution)/shard_map/ppermute | solution.py:423
  10.7 2.5 %collective-permute-start.4 = (f32[2,64,128]{2,1,0:T(8,128)S(1)}, f32[2,64,128]{2,1,0:T(8,128)S(1)}, u32[]{:S(2)}, u32[]{:S(2)}) collective-permute-start(f32[2,64,128]{2,1,0:T(8,128)S(1)} %pad_maximum_fusion.1), channel_id=1, source_target_pairs={{0,24},{1,25},{2,26},{3,27},{4,28},{5,29},{6,30},{7,31},{8,16},{9,... | collective-permute-start | bytes 196616 | tf_op jit(solution)/shard_map/ppermute | solution.py:423
  13.2 0.1 collective-permute-start.3
  13.3 0.2 collective-permute-done.2
  13.5 3.9 %collective-permute-done.4 = f32[2,64,128]{2,1,0:T(8,128)S(1)} collective-permute-done((f32[2,64,128]{2,1,0:T(8,128)S(1)}, f32[2,64,128]{2,1,0:T(8,128)S(1)}, u32[]{:S(2)}, u32[]{:S(2)}) %collective-permute-start.4) | collective-permute-done | bytes 65568 | tf_op jit(solution)/shard_map/ppermute | solution.py:423
  17.4 2.5 %collective-permute-done.3 = f32[2,64,128]{2,1,0:T(8,128)S(1)} collective-permute-done((f32[2,64,128]{2,1,0:T(8,128)S(1)}, f32[2,64,128]{2,1,0:T(8,128)S(1)}, u32[]{:S(2)}, u32[]{:S(2)}) %collective-permute-start.3) | collective-permute-done | bytes 65568 | tf_op jit(solution)/shard_map/ppermute | solution.py:423
  19.9 0.0 collective-permute-done.5.inner_ref
  19.9 0.2 collective-permute-start.6
  20.1 0.0 copy-done.1
  20.1 0.1 collective-permute-start
  20.2 4.1 %collective-permute-done.6 = f32[2,64,128]{2,1,0:T(8,128)S(1)} collective-permute-done((f32[2,64,128]{2,1,0:T(8,128)S(1)}, f32[2,64,128]{2,1,0:T(8,128)S(1)}, u32[]{:S(2)}, u32[]{:S(2)}) %collective-permute-start.6) | collective-permute-done | bytes 65568 | tf_op jit(solution)/shard_map/ppermute | solution.py:423
  24.3 1.6 %collective-permute-start.9 = (f32[2048,128]{1,0:T(8,128)S(1)}, f32[2048,128]{1,0:T(8,128)}, u32[]{:S(2)}, u32[]{:S(2)}) collective-permute-start(f32[2048,128]{1,0:T(8,128)S(1)} %copy-done.1), channel_id=1, source_target_pairs={{6,8},{8,6},{14,16},{16,14},{22,24},{24,22},{7,9},{9,7},{15,17},{1... | collective-permute-start | bytes 3145736 | tf_op jit(solution)/shard_map/ppermute | solution.py:447
  25.9 1.5 %collective-permute-start.7 = (f32[2,64,128]{2,1,0:T(8,128)S(1)}, f32[2,64,128]{2,1,0:T(8,128)S(1)}, u32[]{:S(2)}, u32[]{:S(2)}) collective-permute-start(f32[2,64,128]{2,1,0:T(8,128)S(1)} %pad_maximum_fusion.3), channel_id=1, source_target_pairs={{0,1},{1,0},{2,3},{3,2},{4,5},{5,4},{6,7},{7,6},{8,9},{9,8},{10,11... | collective-permute-start | bytes 196616 | tf_op jit(solution)/shard_map/ppermute | solution.py:423
  27.5 2.7 %collective-permute-done.7 = f32[2,64,128]{2,1,0:T(8,128)S(1)} collective-permute-done((f32[2,64,128]{2,1,0:T(8,128)S(1)}, f32[2,64,128]{2,1,0:T(8,128)S(1)}, u32[]{:S(2)}, u32[]{:S(2)}) %collective-permute-start.7) | collective-permute-done | bytes 65568 | tf_op jit(solution)/shard_map/ppermute | solution.py:423
  30.2 0.1 collective-permute-start.8
  30.3 0.0 copy-done.3
  30.3 0.1 copy.7.cols_hbm
  30.4 1.1 %collective-permute-done.8 = f32[2,64,128]{2,1,0:T(8,128)S(1)} collective-permute-done((f32[2,64,128]{2,1,0:T(8,128)S(1)}, f32[2,64,128]{2,1,0:T(8,128)S(1)}, u32[]{:S(2)}, u32[]{:S(2)}) %collective-permute-start.8) | collective-permute-done | bytes 65568 | tf_op jit(solution)/shard_map/ppermute | solution.py:423
  31.6 5.9 %factors.1 = (f32[128,128]{1,0:T(8,128)}, bf16[256,256]{1,0:T(8,128)(2,1)S(1)}, bf16[256,128]{1,0:T(8,128)(2,1)S(1)}) custom-call(f32[2,128,128]{2,1,0:T(8,128)S(1)} %pad_maximum_fusion.refs_0_), custom_call_target="tpu_custom_call" | custom-call | tf_op jit(solution)/shard_map/factors/pallas_call | solution.py:264
  37.5 0.0 collective-permute-done.chip_ref
  37.5 2.7 %chip_modes.1 = (f32[2048,128]{1,0:T(8,128)}, bf16[2048,128]{1,0:T(8,128)(2,1)S(1)}, bf16[2,2048,128]{2,1,0:T(8,128)(2,1)S(1)}) custom-call(f32[2048,128]{1,0:T(8,128)S(1)} %copy-done.1, f32[2048,128]{1,0:T(8,128)} %collective-permute-done.chip_ref, bf16[256,256]{1,0:T(8,128)(2,1)S(1)} %get-tuple-element.18.w1_ref, bf16[256,128]{1,0:T(8,128)(2,1)S(1)} %get-tuple-element.19.w2_ref), custom_call_target="tpu_custom_call" | custom-call | tf_op jit(solution)/shard_map/chip_modes/pallas_call | solution.py:313
  40.2 0.0 collective-permute-done.9.outer_ref
  40.2 0.0 copy-done.2
  40.2 3.8 %apply_and_project.1 = (bf16[2048,128]{1,0:T(8,128)(2,1)}, f32[128,128]{1,0:T(8,128)S(1)}) custom-call(s32[16,4]{1,0:T(8,128)S(1)} %copy.7.cols_hbm, bf16[2048,128]{1,0:T(8,128)(2,1)S(1)} %get-tuple-element.22.low_ref, bf16[2,2048,128]{2,1,0:T(8,128)(2,1)S(1)} %get-tuple-element.23.mb_ref, f32[2048,128]{1,0:T(8,128)} %collective-permute-done.5.inner_ref, ...), custom_call_target="tpu_custom_call" | custom-call | tf_op jit(solution)/shard_map/apply_and_project/pallas_call | solution.py:391
  44.0 0.2 collective-permute-start.10
  44.2 1.1 %collective-permute-done.10 = f32[128,128]{1,0:T(8,128)S(1)} collective-permute-done((f32[128,128]{1,0:T(8,128)S(1)}, f32[128,128]{1,0:T(8,128)S(1)}, u32[]{:S(2)}, u32[]{:S(2)}) %collective-permute-start.10) | collective-permute-done | bytes 65568 | tf_op jit(solution)/shard_map/ppermute | solution.py:423
  45.3 0.6 collective-permute-start.12
  45.9 2.5 %collective-permute-start.13 = (f32[128,128]{1,0:T(8,128)S(1)}, f32[128,128]{1,0:T(8,128)S(1)}, u32[]{:S(2)}, u32[]{:S(2)}) collective-permute-start(f32[128,128]{1,0:T(8,128)S(1)} %add.216), channel_id=1, source_target_pairs={{0,5},{1,4},{2,7},{3,6},{4,1},{5,0},{6,3},{7,2},{8,13},{9,12},{10,... | collective-permute-start | bytes 196616 | tf_op jit(solution)/shard_map/ppermute | solution.py:423
  48.4 0.5 collective-permute-start.11
  48.9 1.2 %collective-permute-done.12 = f32[128,128]{1,0:T(8,128)S(1)} collective-permute-done((f32[128,128]{1,0:T(8,128)S(1)}, f32[128,128]{1,0:T(8,128)S(1)}, u32[]{:S(2)}, u32[]{:S(2)}) %collective-permute-start.12) | collective-permute-done | bytes 65568 | tf_op jit(solution)/shard_map/ppermute | solution.py:423
  50.1 1.9 %collective-permute-done.13 = f32[128,128]{1,0:T(8,128)S(1)} collective-permute-done((f32[128,128]{1,0:T(8,128)S(1)}, f32[128,128]{1,0:T(8,128)S(1)}, u32[]{:S(2)}, u32[]{:S(2)}) %collective-permute-start.13) | collective-permute-done | bytes 65568 | tf_op jit(solution)/shard_map/ppermute | solution.py:423
  52.0 0.9 %collective-permute-done.11 = f32[128,128]{1,0:T(8,128)S(1)} collective-permute-done((f32[128,128]{1,0:T(8,128)S(1)}, f32[128,128]{1,0:T(8,128)S(1)}, u32[]{:S(2)}, u32[]{:S(2)}) %collective-permute-start.11) | collective-permute-done | bytes 65568 | tf_op jit(solution)/shard_map/ppermute | solution.py:423
  53.0 2.7 %collective-permute-start.15 = (f32[128,128]{1,0:T(8,128)S(1)}, f32[128,128]{1,0:T(8,128)S(1)}, u32[]{:S(2)}, u32[]{:S(2)}) collective-permute-start(f32[128,128]{1,0:T(8,128)S(1)} %add_add_fusion), channel_id=1, source_target_pairs={{0,16},{1,17},{2,18},{3,19},{4,20},{5,21},{6,22},{7,23},{8,24},{9,... | collective-permute-start | bytes 196616 | tf_op jit(solution)/shard_map/ppermute | solution.py:423
  55.7 1.4 %collective-permute-start.16 = (f32[128,128]{1,0:T(8,128)S(1)}, f32[128,128]{1,0:T(8,128)S(1)}, u32[]{:S(2)}, u32[]{:S(2)}) collective-permute-start(f32[128,128]{1,0:T(8,128)S(1)} %add_add_fusion), channel_id=1, source_target_pairs={{0,24},{1,25},{2,26},{3,27},{4,28},{5,29},{6,30},{7,31},{8,16},{9,... | collective-permute-start | bytes 196616 | tf_op jit(solution)/shard_map/ppermute | solution.py:423
  57.1 0.5 collective-permute-start.14
  57.6 3.0 %collective-permute-done.15 = f32[128,128]{1,0:T(8,128)S(1)} collective-permute-done((f32[128,128]{1,0:T(8,128)S(1)}, f32[128,128]{1,0:T(8,128)S(1)}, u32[]{:S(2)}, u32[]{:S(2)}) %collective-permute-start.15) | collective-permute-done | bytes 65568 | tf_op jit(solution)/shard_map/ppermute | solution.py:423
  60.6 1.3 %collective-permute-done.16 = f32[128,128]{1,0:T(8,128)S(1)} collective-permute-done((f32[128,128]{1,0:T(8,128)S(1)}, f32[128,128]{1,0:T(8,128)S(1)}, u32[]{:S(2)}, u32[]{:S(2)}) %collective-permute-start.16) | collective-permute-done | bytes 65568 | tf_op jit(solution)/shard_map/ppermute | solution.py:423
  61.9 0.3 collective-permute-done.14
  62.1 0.6 %add_multiply_fusion = f32[128,128]{1,0:T(8,128)} fusion(f32[128,128]{1,0:T(8,128)S(1)} %collective-permute-done.15, f32[128,128]{1,0:T(8,128)S(1)} %collective-permute-done.16, f32[128,128]{1,0:T(8,128)S(1)} %add_add_fusion, f32[128,128]{1,0:T(8,128)S(1)} %collective-permute-done.14), kind=kLoop, calls=%fused_computation.5 | loop fusion | flops 65536 | bytes 327680 | tf_op jit(solution)/shard_map/div | solution.py:457
  (14 shorter events, 0.2 us)
Async XLA Ops:
  0.6 19.3 %collective-permute-start.5 = (f32[2048,128]{1,0:T(8,128)}, f32[2048,128]{1,0:T(8,128)}, u32[]{:S(2)}, u32[]{:S(2)}) collective-permute-start(f32[2048,128]{1,0:T(8,128)} %s_ref.1), channel_id=1, source_target_pairs={{2,4},{4,2},{10,12},{12,10},{18,20},{20,18},{26,28},{28,26},{3,5},... | collective-permute-start | bytes 3145736 | tf_op jit(solution)/shard_map/ppermute | solution.py:437
  2.3 1.2 %copy-start = (f32[2048,128]{1,0:T(8,128)S(1)}, f32[2048,128]{1,0:T(8,128)}, u32[]{:S(2)}) copy-start(f32[2048,128]{1,0:T(8,128)} %s_ref.1) | copy-start | bytes 3145732
  3.5 16.6 %copy-start.1 = (f32[2048,128]{1,0:T(8,128)S(1)}, f32[2048,128]{1,0:T(8,128)}, u32[]{:S(2)}) copy-start(f32[2048,128]{1,0:T(8,128)} %s_ref.1) | copy-start | bytes 3145732
  3.5 26.8 %copy-start.3 = (s32[16,4]{0,1:T(4,128)S(1)}, s32[16,4]{0,1:T(4,128)}, u32[]{:S(2)}) copy-start(s32[16,4]{0,1:T(4,128)} %param.5) | copy-start | bytes 772
  4.7 4.3 %collective-permute-start.1 = (f32[2,64,128]{2,1,0:T(8,128)S(1)}, f32[2,64,128]{2,1,0:T(8,128)S(1)}, u32[]{:S(2)}, u32[]{:S(2)}) collective-permute-start(f32[2,64,128]{2,1,0:T(8,128)S(1)} %get-tuple-element.41), channel_id=1, source_target_pairs={{0,2},{1,3},{2,0},{3,1},{4,6},{5,7},{6,4},{7,5},{8,10},{9,11},{10,... | collective-permute-start | bytes 196616 | tf_op jit(solution)/shard_map/ppermute | solution.py:423
  9.1 31.1 %copy-start.2 = (bf16[16,4,128,128]{3,2,1,0:T(8,128)(2,1)S(1)}, bf16[16,4,128,128]{3,2,1,0:T(8,128)(2,1)}, u32[]{:S(2)}) copy-start(bf16[16,4,128,128]{3,2,1,0:T(8,128)(2,1)} %jb_ref.1) | copy-start | bytes 6291460
  9.1 4.4 %collective-permute-start.2 = (f32[2,64,128]{2,1,0:T(8,128)S(1)}, f32[2,64,128]{2,1,0:T(8,128)S(1)}, u32[]{:S(2)}, u32[]{:S(2)}) collective-permute-start(f32[2,64,128]{2,1,0:T(8,128)S(1)} %pad_maximum_fusion.1), channel_id=1, source_target_pairs={{0,8},{1,9},{2,10},{3,11},{4,12},{5,13},{6,14},{7,15},{8,0},{9,1},... | collective-permute-start | bytes 196616 | tf_op jit(solution)/shard_map/ppermute | solution.py:423
  10.7 6.7 %collective-permute-start.4 = (f32[2,64,128]{2,1,0:T(8,128)S(1)}, f32[2,64,128]{2,1,0:T(8,128)S(1)}, u32[]{:S(2)}, u32[]{:S(2)}) collective-permute-start(f32[2,64,128]{2,1,0:T(8,128)S(1)} %pad_maximum_fusion.1), channel_id=1, source_target_pairs={{0,24},{1,25},{2,26},{3,27},{4,28},{5,29},{6,30},{7,31},{8,16},{9,... | collective-permute-start | bytes 196616 | tf_op jit(solution)/shard_map/ppermute | solution.py:423
  13.2 6.7 %collective-permute-start.3 = (f32[2,64,128]{2,1,0:T(8,128)S(1)}, f32[2,64,128]{2,1,0:T(8,128)S(1)}, u32[]{:S(2)}, u32[]{:S(2)}) collective-permute-start(f32[2,64,128]{2,1,0:T(8,128)S(1)} %pad_maximum_fusion.1), channel_id=1, source_target_pairs={{0,16},{1,17},{2,18},{3,19},{4,20},{5,21},{6,22},{7,23},{8,24},{9,... | collective-permute-start | bytes 196616 | tf_op jit(solution)/shard_map/ppermute | solution.py:423
  19.9 4.3 %collective-permute-start.6 = (f32[2,64,128]{2,1,0:T(8,128)S(1)}, f32[2,64,128]{2,1,0:T(8,128)S(1)}, u32[]{:S(2)}, u32[]{:S(2)}) collective-permute-start(f32[2,64,128]{2,1,0:T(8,128)S(1)} %pad_maximum_fusion.2), channel_id=1, source_target_pairs={{0,4},{1,5},{2,6},{3,7},{4,0},{5,1},{6,2},{7,3},{8,12},{9,13},{10,... | collective-permute-start | bytes 196616 | tf_op jit(solution)/shard_map/ppermute | solution.py:423
  20.1 17.4 %collective-permute-start = (f32[2048,128]{1,0:T(8,128)S(1)}, f32[2048,128]{1,0:T(8,128)}, u32[]{:S(2)}, u32[]{:S(2)}) collective-permute-start(f32[2048,128]{1,0:T(8,128)S(1)} %copy-done.1), channel_id=1, source_target_pairs={{0,2},{1,3},{2,0},{3,1},{4,6},{5,7},{6,4},{7,5},{8,10},{9,11},{10,... | collective-permute-start | bytes 3145736 | tf_op jit(solution)/shard_map/ppermute | solution.py:423
  24.3 15.9 %collective-permute-start.9 = (f32[2048,128]{1,0:T(8,128)S(1)}, f32[2048,128]{1,0:T(8,128)}, u32[]{:S(2)}, u32[]{:S(2)}) collective-permute-start(f32[2048,128]{1,0:T(8,128)S(1)} %copy-done.1), channel_id=1, source_target_pairs={{6,8},{8,6},{14,16},{16,14},{22,24},{24,22},{7,9},{9,7},{15,17},{1... | collective-permute-start | bytes 3145736 | tf_op jit(solution)/shard_map/ppermute | solution.py:447
  25.9 4.3 %collective-permute-start.7 = (f32[2,64,128]{2,1,0:T(8,128)S(1)}, f32[2,64,128]{2,1,0:T(8,128)S(1)}, u32[]{:S(2)}, u32[]{:S(2)}) collective-permute-start(f32[2,64,128]{2,1,0:T(8,128)S(1)} %pad_maximum_fusion.3), channel_id=1, source_target_pairs={{0,1},{1,0},{2,3},{3,2},{4,5},{5,4},{6,7},{7,6},{8,9},{9,8},{10,11... | collective-permute-start | bytes 196616 | tf_op jit(solution)/shard_map/ppermute | solution.py:423
  30.2 1.3 %collective-permute-start.8 = (f32[2,64,128]{2,1,0:T(8,128)S(1)}, f32[2,64,128]{2,1,0:T(8,128)S(1)}, u32[]{:S(2)}, u32[]{:S(2)}) collective-permute-start(f32[2,64,128]{2,1,0:T(8,128)S(1)} %pad_maximum_fusion.4), channel_id=1, source_target_pairs={{0,2},{1,3},{2,0},{3,1},{4,6},{5,7},{6,4},{7,5},{8,10},{9,11},{10,... | collective-permute-start | bytes 196616 | tf_op jit(solution)/shard_map/ppermute | solution.py:423
  44.0 1.3 %collective-permute-start.10 = (f32[128,128]{1,0:T(8,128)S(1)}, f32[128,128]{1,0:T(8,128)S(1)}, u32[]{:S(2)}, u32[]{:S(2)}) collective-permute-start(f32[128,128]{1,0:T(8,128)S(1)} %get-tuple-element.27), channel_id=1, source_target_pairs={{0,2},{1,3},{2,0},{3,1},{4,6},{5,7},{6,4},{7,5},{8,10},{9,11},{10,... | collective-permute-start | bytes 196616 | tf_op jit(solution)/shard_map/ppermute | solution.py:423
  45.3 4.7 %collective-permute-start.12 = (f32[128,128]{1,0:T(8,128)S(1)}, f32[128,128]{1,0:T(8,128)S(1)}, u32[]{:S(2)}, u32[]{:S(2)}) collective-permute-start(f32[128,128]{1,0:T(8,128)S(1)} %add.216), channel_id=1, source_target_pairs={{0,4},{1,5},{2,6},{3,7},{4,0},{5,1},{6,2},{7,3},{8,12},{9,13},{10,... | collective-permute-start | bytes 196616 | tf_op jit(solution)/shard_map/ppermute | solution.py:423
  45.9 6.1 %collective-permute-start.13 = (f32[128,128]{1,0:T(8,128)S(1)}, f32[128,128]{1,0:T(8,128)S(1)}, u32[]{:S(2)}, u32[]{:S(2)}) collective-permute-start(f32[128,128]{1,0:T(8,128)S(1)} %add.216), channel_id=1, source_target_pairs={{0,5},{1,4},{2,7},{3,6},{4,1},{5,0},{6,3},{7,2},{8,13},{9,12},{10,... | collective-permute-start | bytes 196616 | tf_op jit(solution)/shard_map/ppermute | solution.py:423
  48.4 4.6 %collective-permute-start.11 = (f32[128,128]{1,0:T(8,128)S(1)}, f32[128,128]{1,0:T(8,128)S(1)}, u32[]{:S(2)}, u32[]{:S(2)}) collective-permute-start(f32[128,128]{1,0:T(8,128)S(1)} %add.216), channel_id=1, source_target_pairs={{0,1},{1,0},{2,3},{3,2},{4,5},{5,4},{6,7},{7,6},{8,9},{9,8},{10,11... | collective-permute-start | bytes 196616 | tf_op jit(solution)/shard_map/ppermute | solution.py:423
  53.0 7.6 %collective-permute-start.15 = (f32[128,128]{1,0:T(8,128)S(1)}, f32[128,128]{1,0:T(8,128)S(1)}, u32[]{:S(2)}, u32[]{:S(2)}) collective-permute-start(f32[128,128]{1,0:T(8,128)S(1)} %add_add_fusion), channel_id=1, source_target_pairs={{0,16},{1,17},{2,18},{3,19},{4,20},{5,21},{6,22},{7,23},{8,24},{9,... | collective-permute-start | bytes 196616 | tf_op jit(solution)/shard_map/ppermute | solution.py:423
  55.7 6.2 %collective-permute-start.16 = (f32[128,128]{1,0:T(8,128)S(1)}, f32[128,128]{1,0:T(8,128)S(1)}, u32[]{:S(2)}, u32[]{:S(2)}) collective-permute-start(f32[128,128]{1,0:T(8,128)S(1)} %add_add_fusion), channel_id=1, source_target_pairs={{0,24},{1,25},{2,26},{3,27},{4,28},{5,29},{6,30},{7,31},{8,16},{9,... | collective-permute-start | bytes 196616 | tf_op jit(solution)/shard_map/ppermute | solution.py:423
  57.1 5.0 %collective-permute-start.14 = (f32[128,128]{1,0:T(8,128)S(1)}, f32[128,128]{1,0:T(8,128)S(1)}, u32[]{:S(2)}, u32[]{:S(2)}) collective-permute-start(f32[128,128]{1,0:T(8,128)S(1)} %add_add_fusion), channel_id=1, source_target_pairs={{0,8},{1,9},{2,10},{3,11},{4,12},{5,13},{6,14},{7,15},{8,0},{9,1},... | collective-permute-start | bytes 196616 | tf_op jit(solution)/shard_map/ppermute | solution.py:423

commit v5 on v4

--- a/solution.py
+++ b/solution.py
@@ -221,7 +221,15 @@
     return [sum(block(i, t - i) for i in range(n) if 0 <= t - i < m) for t in range(n + m - 1)]
 
 
-def factors_kernel(count, g_ref, up_ref, w1_ref, w2_ref, inv2_ref):
+def modes_of(rows, w1, w2):
+    k = rows.shape[1]
+    h, m, l = split3(rows)
+    p = mm(jnp.concatenate([h, m], axis=1), w1)
+    q = mm(jnp.concatenate([h, l], axis=1), w2)
+    return p[:, :k] + (p[:, k:] + q)
+
+
+def factors_kernel(count, g_ref, s_ref, chip_ref, up_ref, w1_ref, w2_ref, modes_ref, low_ref, mb_ref, inv2_ref):
     k = g_ref.shape[1]
     high, low, row = scaled(g_ref[0], g_ref[1])
     inv1 = inverse_factor(0.5 * (high + high.T))
@@ -257,80 +265,38 @@
     w1_ref[...] = jnp.concatenate([hm, hm], axis=0)
     w2_ref[...] = jnp.concatenate([l, h], axis=0)
     up_ref[...] = jnp.where(c >= r, (both[:, k:] * row) / math.sqrt(count), 0.0)
-
-
-def factors(g, count):
-    k = g.shape[1]
+    for at in (slice(i, i + TILE) for i in range(0, s_ref.shape[0], TILE)):
+        modes = modes_of(s_ref[at, :], w1_ref[...], w2_ref[...])
+        modes_ref[at, :] = modes
+        mb_ref[0, at, :], low_ref[at, :] = split2(modes)
+    for at in (slice(i, i + TILE) for i in range(0, s_ref.shape[0], TILE)):
+        mb_ref[1, at, :] = modes_of(chip_ref[at, :], w1_ref[...], w2_ref[...]).astype(BF16)
+
+
+def factors_and_chip_modes(g, s, chip, count):
+    rows, k = s.shape
+    vmem = pl.BlockSpec(memory_space=pltpu.VMEM)
     return pl.pallas_call(
         lambda *refs: factors_kernel(count, *refs),
+        in_specs=[vmem] * 3,
+        out_specs=(vmem,) * 6,
         out_shape=(
             jax.ShapeDtypeStruct((k, k), F32),
-            jax.ShapeDtypeStruct((2 * k, 2 * k), BF16),
-            jax.ShapeDtypeStruct((2 * k, k), BF16),
+            pltpu.VMEM((2 * k, 2 * k), BF16),
+            pltpu.VMEM((2 * k, k), BF16),
+            pltpu.VMEM((rows, k), F32),
+            pltpu.VMEM((rows, k), BF16),
+            pltpu.VMEM((2, rows, k), BF16),
         ),
         scratch_shapes=[pltpu.VMEM((k, k), F32)],
         compiler_params=pltpu.CompilerParams(vmem_limit_bytes=VMEM_LIMIT),
-        name="factors",
-    )(g)
-
-
-def modes_of(rows, w1, w2):
-    k = rows.shape[1]
-    h, m, l = split3(rows)
-    p = mm(jnp.concatenate([h, m], axis=1), w1)
-    q = mm(jnp.concatenate([h, l], axis=1), w2)
-    return p[:, :k] + (p[:, k:] + q)
-
-
-def pieces(source, target, sem):
-    n = target.shape[0] // 4
-    return [
-        pltpu.make_async_copy(source.at[pl.ds(i * n, n)], target.at[pl.ds(i * n, n)], sem.at[i]) for i in range(4)
-    ]
-
-
-def chip_kernel(s_ref, chip_ref, w1_ref, w2_ref, modes_hbm, low_ref, mb_ref, modes_ref, put_sem):
-    rows = s_ref.shape[0]
-    put = pieces(modes_ref, modes_hbm, put_sem)
-    per = rows // TILE // 4
-    for c in range(4 * per):
-        at = slice(c * TILE, (c + 1) * TILE)
-        modes = modes_of(s_ref[at, :], w1_ref[...], w2_ref[...])
-        modes_ref[at, :] = modes
-        mb_ref[0, at, :], low_ref[at, :] = split2(modes)
-        if (c + 1) % per == 0:
-            put[c // per].start()
-    for c in range(4 * per):
-        at = slice(c * TILE, (c + 1) * TILE)
-        mb_ref[1, at, :] = modes_of(chip_ref[at, :], w1_ref[...], w2_ref[...]).astype(BF16)
-    for copy in put:
-        copy.wait()
-
-
-def chip_modes(s, chip, w1, w2):
-    rows, k = s.shape
-    vmem, hbm = pl.BlockSpec(memory_space=pltpu.VMEM), pl.BlockSpec(memory_space=pl.ANY)
-    return pl.pallas_call(
-        chip_kernel,
-        in_specs=[vmem] * 4,
-        out_specs=(hbm, vmem, vmem),
-        out_shape=(
-            jax.ShapeDtypeStruct((rows, k), F32),
-            pltpu.VMEM((rows, k), BF16),
-            pltpu.VMEM((2, rows, k), BF16),
-        ),
-        scratch_shapes=[
-            pltpu.VMEM((rows, k), F32),
-            pltpu.SemaphoreType.DMA((4,)),
-        ],
-        compiler_params=pltpu.CompilerParams(vmem_limit_bytes=VMEM_LIMIT),
-        name="chip_modes",
-    )(in_vmem(s), in_vmem(chip), in_vmem(w1), in_vmem(w2))
+        name="factors_and_chip_modes",
+    )(in_vmem(g), in_vmem(s), in_vmem(chip))
 
 
 def apply_kernel(
-    cols_hbm, low_ref, mb_ref, inner_ref, outer_ref, w1_ref, w2_ref, jb_ref, jm_hbm, red_ref,
-    all_ref, jm_ref, cols_ref, sem, put_sem,
+    cols_hbm, modes_ref, low_ref, mb_ref, inner_ref, outer_ref, w1_ref, w2_ref, jb_ref, modes_hbm, jm_ref, red_ref,
+    all_ref, cols_ref, sem,
 ):
     rows, k = low_ref.shape
     block_rows, slots, blk, _ = jb_ref.shape
@@ -341,10 +307,11 @@
     own = pltpu.make_async_copy(mb_ref.at[0], all_ref.at[at[0]], sem.at[0])
     other = pltpu.make_async_copy(mb_ref.at[1], all_ref.at[at[1]], sem.at[1])
     get_cols = pltpu.make_async_copy(cols_hbm, cols_ref, sem.at[2])
-    put = pieces(jm_ref, jm_hbm, put_sem)
+    put_modes = pltpu.make_async_copy(modes_ref, modes_hbm, sem.at[3])
     get_cols.start()
     own.start()
     other.start()
+    put_modes.start()
 
     def further(ref):
         for c in range(rows // TILE):
@@ -372,8 +339,6 @@
 
     for r in range(block_rows):
         apply(r)
-        if (r + 1) % (block_rows // 4) == 0:
-            put[r // (block_rows // 4)].start()
 
     def project(c, acc):
         at = rows_of(c, TILE)
@@ -381,28 +346,29 @@
 
     acc = lax.fori_loop(0, rows // TILE, project, jnp.zeros((2 * k, k), F32), unroll=True)
     red_ref[...] = acc[:k, :] + acc[k:, :]
-    for copy in put:
-        copy.wait()
-
-
-def apply_and_project(cols, low, mb, inner, outer, w1, w2, jb):
+    put_modes.wait()
+
+
+def apply_and_project(cols, modes, low, mb, inner, outer, w1, w2, jb):
     rows, k = low.shape
     vmem, hbm = pl.BlockSpec(memory_space=pltpu.VMEM), pl.BlockSpec(memory_space=pl.ANY)
     return pl.pallas_call(
         apply_kernel,
-        in_specs=[hbm] + [vmem] * 7,
-        out_specs=(hbm, vmem),
-        out_shape=(jax.ShapeDtypeStruct((rows, k), BF16), jax.ShapeDtypeStruct((k, k), F32)),
+        in_specs=[hbm] + [vmem] * 8,
+        out_specs=(hbm, vmem, vmem),
+        out_shape=(
+            jax.ShapeDtypeStruct((rows, k), F32),
+            pltpu.VMEM((rows, k), BF16),
+            pltpu.VMEM((k, k), F32),
+        ),
         scratch_shapes=[
             pltpu.VMEM((3 * rows, k), BF16),
-            pltpu.VMEM((rows, k), BF16),
             pltpu.SMEM(cols.shape, jnp.int32),
-            pltpu.SemaphoreType.DMA((3,)),
             pltpu.SemaphoreType.DMA((4,)),
         ],
         compiler_params=pltpu.CompilerParams(vmem_limit_bytes=VMEM_LIMIT),
         name="apply_and_project",
-    )(cols, in_vmem(low), in_vmem(mb), in_vmem(inner), in_vmem(outer), in_vmem(w1), in_vmem(w2), in_vmem(jb))
+    )(cols, in_vmem(modes), in_vmem(low), in_vmem(mb), in_vmem(inner), in_vmem(outer), in_vmem(w1), in_vmem(w2), in_vmem(jb))
 
 
 def solution(mesh):
@@ -441,16 +407,14 @@
         mine = add_pairs(jnp.where(even, upper, lower), swap(jnp.where(even, lower, upper), core_mask))
         for phase in masks_far:
             mine = exchange(mine, phase, add_pairs)
-        mine, inner = lax.optimization_barrier((mine, inner))
+        mine, inner, late = lax.optimization_barrier((mine, inner, snapshots))
         mine = exchange(mine, masks_x, add_pairs)
-        mine, late = lax.optimization_barrier((mine, snapshots))
         outer = lax.ppermute(late, "bulk", pairs(3))
         mine = exchange(mine, masks_y, add_pairs)
         other = swap(mine, core_mask)
         gram = jnp.concatenate([jnp.where(even, mine, other), jnp.where(even, other, mine)], axis=1)
-        factor, w1, w2 = factors(gram, rows_total)
-        modes, low, mb = chip_modes(snapshots, chip, w1, w2)
-        jac_modes, reduced = apply_and_project(jac_cols, low, mb, inner, outer, w1, w2, jac_blocks)
+        factor, w1, w2, modes, low, mb = factors_and_chip_modes(gram, snapshots, chip, rows_total)
+        modes, jac_modes, reduced = apply_and_project(jac_cols, modes, low, mb, inner, outer, w1, w2, jac_blocks)
         reduced = reduced + swap(reduced, core_mask)
         for phase in phases:
             reduced = exchange(reduced, phase, jnp.add)

time: 63 us -> 59.2 us (0.940)
  waiting for transfers between devices: 25.1 us -> 20.3 us
  starting transfers between devices: 21.1 us -> 22.3 us
  Pallas kernels: 13.5 us -> 12.5 us
  local copies, waits for them, and re-layouts: 1.32 us -> 2.11 us
    ppermute x15, waiting for transfers between devices: 25.1 us -> 20.3 us  [swap(): return lax.ppermute(value, axes, [(i, i ^ mask) for i in range(count)])]
    ppermute x15, starting transfers between devices: 17.8 us -> 19 us  [swap(): return lax.ppermute(value, axes, [(i, i ^ mask) for i in range(count)])]
    pallas_call x3 -> x2, Pallas kernels: 12.4 us -> 11.4 us  [the longest x1 7.92 us: factors_and_chip_modes(): pl.pallas_call(lambda *refs: factors_kernel(count, *refs), in_specs=[vmem...]
    unnamed x9 -> x10, local copies, waits for them, and re-layouts: 1.32 us -> 2.11 us
  transfers between devices with their start and end apart: 17 -> 17, of which waited for: 14 -> 12; matrix products, arithmetic and copies ran while one was open for 0% -> 2% of each run, Pallas kernels for 15% -> 15%
where the time goes in v5:
time: 59.2 us; the launch traced here: 58.9 us
  starting transfers between devices  22.3 us (38%)
  waiting for transfers between devices  20.3 us (34%)
  Pallas kernels  12.5 us (21%)
  local copies, waits for them, and re-layouts  2.11 us (4%)
  other arithmetic  0.85 us (1%)
  between operations  0.82 us (1%)
    ppermute x15, waiting for transfers between devices, swap(): return lax.ppermute(value, axes, [(i, i ^ mask) for i in range(count)])  20.3 us
    ppermute x15, starting transfers between devices, swap(): return lax.ppermute(value, axes, [(i, i ^ mask) for i in range(count)])  19 us
    pallas_call x1, Pallas kernels, factors_and_chip_modes(): pl.pallas_call(lambda *refs: factors_kernel(count, *refs), in_specs=[vmem...  7.92 us
    pallas_call x1, Pallas kernels, apply_and_project(): pl.pallas_call(apply_kernel, in_specs=[hbm] + [vmem] * 8, out_specs=(hbm,...  3.43 us
    unnamed x10, local copies, waits for them, and re-layouts  2.11 us
    ppermute x1, starting transfers between devices, shards(): inner = lax.ppermute(snapshots, 'bulk', pairs(1))  1.66 us
    ppermute x1, starting transfers between devices, shards(): outer = lax.ppermute(late, 'bulk', pairs(3))  1.61 us
  transfers between devices with their start and end apart: 17, of which 12 were waited for; matrix products, arithmetic and copies ran while one was open for 2% of the time, Pallas kernels for 15%

profile of v5, /device:TPU:0, one launch (start us, length us, event | category | flops | bytes accessed | tf_op | source)
XLA Modules:
  0.0 58.9 jit_solution(4065832735277001459)
XLA Ops:
  0.6 0.0 copy-start.3
  0.6 1.7 %collective-permute-start.4 = (f32[2048,128]{1,0:T(8,128)}, f32[2048,128]{1,0:T(8,128)}, u32[]{:S(2)}, u32[]{:S(2)}) collective-permute-start(f32[2048,128]{1,0:T(8,128)} %refs_1_.1), channel_id=1, source_target_pairs={{2,4},{4,2},{10,12},{12,10},{18,20},{20,18},{26,28},{28,26},{3,5},... | collective-permute-start | bytes 3145736 | tf_op jit(solution)/shard_map/ppermute | solution.py:403
  2.3 0.0 copy-start
  2.3 1.2 %copy-done = f32[2048,128]{1,0:T(8,128)S(1)} copy-done((f32[2048,128]{1,0:T(8,128)S(1)}, f32[2048,128]{1,0:T(8,128)}, u32[]{:S(2)}) %copy-start) | copy-done | bytes 1048600
  3.5 0.0 copy-start.1
  3.5 1.2 %local_gram.1 = f32[2,128,128]{2,1,0:T(8,128)S(1)} custom-call(f32[2048,128]{1,0:T(8,128)S(1)} %copy-done), custom_call_target="tpu_custom_call" | custom-call | tf_op jit(solution)/shard_map/local_gram/pallas_call | solution.py:121
  4.7 3.4 %collective-permute-start = (f32[2,64,128]{2,1,0:T(8,128)S(1)}, f32[2,64,128]{2,1,0:T(8,128)S(1)}, u32[]{:S(2)}, u32[]{:S(2)}) collective-permute-start(f32[2,64,128]{2,1,0:T(8,128)S(1)} %get-tuple-element.41), channel_id=1, source_target_pairs={{0,2},{1,3},{2,0},{3,1},{4,6},{5,7},{6,4},{7,5},{8,10},{9,11},{10,... | collective-permute-start | bytes 196616 | tf_op jit(solution)/shard_map/ppermute | solution.py:389
  8.1 0.9 %collective-permute-done = f32[2,64,128]{2,1,0:T(8,128)S(1)} collective-permute-done((f32[2,64,128]{2,1,0:T(8,128)S(1)}, f32[2,64,128]{2,1,0:T(8,128)S(1)}, u32[]{:S(2)}, u32[]{:S(2)}) %collective-permute-start) | collective-permute-done | bytes 65568 | tf_op jit(solution)/shard_map/ppermute | solution.py:389
  9.1 0.0 copy-start.2
  9.1 3.7 %collective-permute-start.3 = (f32[2,64,128]{2,1,0:T(8,128)S(1)}, f32[2,64,128]{2,1,0:T(8,128)S(1)}, u32[]{:S(2)}, u32[]{:S(2)}) collective-permute-start(f32[2,64,128]{2,1,0:T(8,128)S(1)} %pad_maximum_fusion.1), channel_id=1, source_target_pairs={{0,24},{1,25},{2,26},{3,27},{4,28},{5,29},{6,30},{7,31},{8,16},{9,... | collective-permute-start | bytes 196616 | tf_op jit(solution)/shard_map/ppermute | solution.py:389
  12.8 0.0 collective-permute-start.2
  12.8 0.8 %collective-permute-start.1 = (f32[2,64,128]{2,1,0:T(8,128)S(1)}, f32[2,64,128]{2,1,0:T(8,128)S(1)}, u32[]{:S(2)}, u32[]{:S(2)}) collective-permute-start(f32[2,64,128]{2,1,0:T(8,128)S(1)} %pad_maximum_fusion.1), channel_id=1, source_target_pairs={{0,8},{1,9},{2,10},{3,11},{4,12},{5,13},{6,14},{7,15},{8,0},{9,1},... | collective-permute-start | bytes 196616 | tf_op jit(solution)/shard_map/ppermute | solution.py:389
  13.5 2.1 %collective-permute-done.3 = f32[2,64,128]{2,1,0:T(8,128)S(1)} collective-permute-done((f32[2,64,128]{2,1,0:T(8,128)S(1)}, f32[2,64,128]{2,1,0:T(8,128)S(1)}, u32[]{:S(2)}, u32[]{:S(2)}) %collective-permute-start.3) | collective-permute-done | bytes 65568 | tf_op jit(solution)/shard_map/ppermute | solution.py:389
  15.6 3.1 %collective-permute-done.2 = f32[2,64,128]{2,1,0:T(8,128)S(1)} collective-permute-done((f32[2,64,128]{2,1,0:T(8,128)S(1)}, f32[2,64,128]{2,1,0:T(8,128)S(1)}, u32[]{:S(2)}, u32[]{:S(2)}) %collective-permute-start.2) | collective-permute-done | bytes 65568 | tf_op jit(solution)/shard_map/ppermute | solution.py:389
  18.7 0.0 collective-permute-done.1
  18.8 0.0 collective-permute-done.4.inner_ref
  18.8 1.2 %collective-permute-start.5 = (f32[2,64,128]{2,1,0:T(8,128)S(1)}, f32[2,64,128]{2,1,0:T(8,128)S(1)}, u32[]{:S(2)}, u32[]{:S(2)}) collective-permute-start(f32[2,64,128]{2,1,0:T(8,128)S(1)} %pad_maximum_fusion.2), channel_id=1, source_target_pairs={{0,4},{1,5},{2,6},{3,7},{4,0},{5,1},{6,2},{7,3},{8,12},{9,13},{10,... | collective-permute-start | bytes 196616 | tf_op jit(solution)/shard_map/ppermute | solution.py:389
  20.0 0.0 copy-done.1
  20.0 0.0 collective-permute-start.8
  20.0 1.6 %collective-permute-start.9 = (f32[2048,128]{1,0:T(8,128)S(1)}, f32[2048,128]{1,0:T(8,128)}, u32[]{:S(2)}, u32[]{:S(2)}) collective-permute-start(f32[2048,128]{1,0:T(8,128)S(1)} %copy-done.1), channel_id=1, source_target_pairs={{6,8},{8,6},{14,16},{16,14},{22,24},{24,22},{7,9},{9,7},{15,17},{1... | collective-permute-start | bytes 3145736 | tf_op jit(solution)/shard_map/ppermute | solution.py:412
  21.6 1.5 %collective-permute-done.5 = f32[2,64,128]{2,1,0:T(8,128)S(1)} collective-permute-done((f32[2,64,128]{2,1,0:T(8,128)S(1)}, f32[2,64,128]{2,1,0:T(8,128)S(1)}, u32[]{:S(2)}, u32[]{:S(2)}) %collective-permute-start.5) | collective-permute-done | bytes 65568 | tf_op jit(solution)/shard_map/ppermute | solution.py:389
  23.2 1.6 %collective-permute-start.6 = (f32[2,64,128]{2,1,0:T(8,128)S(1)}, f32[2,64,128]{2,1,0:T(8,128)S(1)}, u32[]{:S(2)}, u32[]{:S(2)}) collective-permute-start(f32[2,64,128]{2,1,0:T(8,128)S(1)} %pad_maximum_fusion.3), channel_id=1, source_target_pairs={{0,1},{1,0},{2,3},{3,2},{4,5},{5,4},{6,7},{7,6},{8,9},{9,8},{10,11... | collective-permute-start | bytes 196616 | tf_op jit(solution)/shard_map/ppermute | solution.py:389
  24.8 2.8 %collective-permute-done.6 = f32[2,64,128]{2,1,0:T(8,128)S(1)} collective-permute-done((f32[2,64,128]{2,1,0:T(8,128)S(1)}, f32[2,64,128]{2,1,0:T(8,128)S(1)}, u32[]{:S(2)}, u32[]{:S(2)}) %collective-permute-start.6) | collective-permute-done | bytes 65568 | tf_op jit(solution)/shard_map/ppermute | solution.py:389
  27.6 0.1 collective-permute-start.7
  27.6 0.0 copy-done.3
  27.6 0.1 copy.7.cols_hbm
  27.7 1.1 %collective-permute-done.7 = f32[2,64,128]{2,1,0:T(8,128)S(1)} collective-permute-done((f32[2,64,128]{2,1,0:T(8,128)S(1)}, f32[2,64,128]{2,1,0:T(8,128)S(1)}, u32[]{:S(2)}, u32[]{:S(2)}) %collective-permute-start.7) | collective-permute-done | bytes 65568 | tf_op jit(solution)/shard_map/ppermute | solution.py:389
  28.9 0.0 collective-permute-done.8.refs_2_
  28.9 7.9 %factors_and_chip_modes.1 = (f32[128,128]{1,0:T(8,128)}, bf16[256,256]{1,0:T(8,128)(2,1)S(1)}, bf16[256,128]{1,0:T(8,128)(2,1)S(1)}, f32[2048,128]{1,0:T(8,128)S...) custom-call(f32[2,128,128]{2,1,0:T(8,128)S(1)} %pad_maximum_fusion.refs_0_, ...), custom_call_target="tpu_custom_call" | custom-call | tf_op jit(solution)/shard_map/factors_and_chip_modes/pallas_call | solution.py:279
  36.9 0.0 collective-permute-done.9.outer_ref
  36.9 0.0 copy-done.2
  36.9 3.4 %apply_and_project.1 = (f32[2048,128]{1,0:T(8,128)}, bf16[2048,128]{1,0:T(8,128)(2,1)S(1)}, f32[128,128]{1,0:T(8,128)S(1)}) custom-call(s32[16,4]{1,0:T(8,128)S(1)} %copy.7.cols_hbm, f32[2048,128]{1,0:T(8,128)S(1)} %get-tuple-element.17.modes_ref, bf16[2048,128]{1,0:T(8,128)(2,1)S(1)} %get-tuple-element.18.low_ref, ...), custom_call_target="tpu_custom_call" | custom-call | tf_op jit(solution)/shard_map/apply_and_project/pallas_call | solution.py:355
  40.3 0.2 collective-permute-start.10
  40.5 1.1 %collective-permute-done.10 = f32[128,128]{1,0:T(8,128)S(1)} collective-permute-done((f32[128,128]{1,0:T(8,128)S(1)}, f32[128,128]{1,0:T(8,128)S(1)}, u32[]{:S(2)}, u32[]{:S(2)}) %collective-permute-start.10) | collective-permute-done | bytes 65568 | tf_op jit(solution)/shard_map/ppermute | solution.py:389
  41.7 2.7 %collective-permute-start.13 = (f32[128,128]{1,0:T(8,128)S(1)}, f32[128,128]{1,0:T(8,128)S(1)}, u32[]{:S(2)}, u32[]{:S(2)}) collective-permute-start(f32[128,128]{1,0:T(8,128)S(1)} %add.226), channel_id=1, source_target_pairs={{0,5},{1,4},{2,7},{3,6},{4,1},{5,0},{6,3},{7,2},{8,13},{9,12},{10,... | collective-permute-start | bytes 196616 | tf_op jit(solution)/shard_map/ppermute | solution.py:389
  44.4 0.4 collective-permute-start.12
  44.7 0.5 collective-permute-start.11
  45.2 1.8 %collective-permute-done.13 = f32[128,128]{1,0:T(8,128)S(1)} collective-permute-done((f32[128,128]{1,0:T(8,128)S(1)}, f32[128,128]{1,0:T(8,128)S(1)}, u32[]{:S(2)}, u32[]{:S(2)}) %collective-permute-start.13) | collective-permute-done | bytes 65568 | tf_op jit(solution)/shard_map/ppermute | solution.py:389
  47.1 1.6 %collective-permute-done.12 = f32[128,128]{1,0:T(8,128)S(1)} collective-permute-done((f32[128,128]{1,0:T(8,128)S(1)}, f32[128,128]{1,0:T(8,128)S(1)}, u32[]{:S(2)}, u32[]{:S(2)}) %collective-permute-start.12) | collective-permute-done | bytes 65568 | tf_op jit(solution)/shard_map/ppermute | solution.py:389
  48.6 0.4 collective-permute-done.11
  49.0 3.9 %collective-permute-start.16 = (f32[128,128]{1,0:T(8,128)S(1)}, f32[128,128]{1,0:T(8,128)S(1)}, u32[]{:S(2)}, u32[]{:S(2)}) collective-permute-start(f32[128,128]{1,0:T(8,128)S(1)} %add_add_fusion), channel_id=1, source_target_pairs={{0,24},{1,25},{2,26},{3,27},{4,28},{5,29},{6,30},{7,31},{8,16},{9,... | collective-permute-start | bytes 196616 | tf_op jit(solution)/shard_map/ppermute | solution.py:389
  52.9 0.0 collective-permute-start.15
  52.9 0.6 %collective-permute-start.14 = (f32[128,128]{1,0:T(8,128)S(1)}, f32[128,128]{1,0:T(8,128)S(1)}, u32[]{:S(2)}, u32[]{:S(2)}) collective-permute-start(f32[128,128]{1,0:T(8,128)S(1)} %add_add_fusion), channel_id=1, source_target_pairs={{0,8},{1,9},{2,10},{3,11},{4,12},{5,13},{6,14},{7,15},{8,0},{9,1},... | collective-permute-start | bytes 196616 | tf_op jit(solution)/shard_map/ppermute | solution.py:389
  53.6 0.8 %copy.8 = bf16[2048,128]{1,0:T(8,128)(2,1)} copy(bf16[2048,128]{1,0:T(8,128)(2,1)S(1)} %get-tuple-element.44) | data formatting | bytes 1048576
  54.3 1.2 %collective-permute-done.16 = f32[128,128]{1,0:T(8,128)S(1)} collective-permute-done((f32[128,128]{1,0:T(8,128)S(1)}, f32[128,128]{1,0:T(8,128)S(1)}, u32[]{:S(2)}, u32[]{:S(2)}) %collective-permute-start.16) | collective-permute-done | bytes 65568 | tf_op jit(solution)/shard_map/ppermute | solution.py:389
  55.6 2.7 %collective-permute-done.15 = f32[128,128]{1,0:T(8,128)S(1)} collective-permute-done((f32[128,128]{1,0:T(8,128)S(1)}, f32[128,128]{1,0:T(8,128)S(1)}, u32[]{:S(2)}, u32[]{:S(2)}) %collective-permute-start.15) | collective-permute-done | bytes 65568 | tf_op jit(solution)/shard_map/ppermute | solution.py:389
  58.3 0.0 collective-permute-done.14
  58.3 0.6 %add_multiply_fusion = f32[128,128]{1,0:T(8,128)} fusion(f32[128,128]{1,0:T(8,128)S(1)} %collective-permute-done.15, f32[128,128]{1,0:T(8,128)S(1)} %collective-permute-done.16, f32[128,128]{1,0:T(8,128)S(1)} %add_add_fusion, f32[128,128]{1,0:T(8,128)S(1)} %collective-permute-done.14), kind=kLoop, calls=%fused_computation.5 | loop fusion | flops 65536 | bytes 327680 | tf_op jit(solution)/shard_map/div | solution.py:421
  (14 shorter events, 0.2 us)
Async XLA Ops:
  0.6 27.0 %copy-start.3 = (s32[16,4]{0,1:T(4,128)S(1)}, s32[16,4]{0,1:T(4,128)}, u32[]{:S(2)}) copy-start(s32[16,4]{0,1:T(4,128)} %param.5) | copy-start | bytes 772
  0.6 18.2 %collective-permute-start.4 = (f32[2048,128]{1,0:T(8,128)}, f32[2048,128]{1,0:T(8,128)}, u32[]{:S(2)}, u32[]{:S(2)}) collective-permute-start(f32[2048,128]{1,0:T(8,128)} %refs_1_.1), channel_id=1, source_target_pairs={{2,4},{4,2},{10,12},{12,10},{18,20},{20,18},{26,28},{28,26},{3,5},... | collective-permute-start | bytes 3145736 | tf_op jit(solution)/shard_map/ppermute | solution.py:403
  2.3 1.2 %copy-start = (f32[2048,128]{1,0:T(8,128)S(1)}, f32[2048,128]{1,0:T(8,128)}, u32[]{:S(2)}) copy-start(f32[2048,128]{1,0:T(8,128)} %refs_1_.1) | copy-start | bytes 3145732
  3.5 16.5 %copy-start.1 = (f32[2048,128]{1,0:T(8,128)S(1)}, f32[2048,128]{1,0:T(8,128)}, u32[]{:S(2)}) copy-start(f32[2048,128]{1,0:T(8,128)} %refs_1_.1) | copy-start | bytes 3145732
  4.7 4.3 %collective-permute-start = (f32[2,64,128]{2,1,0:T(8,128)S(1)}, f32[2,64,128]{2,1,0:T(8,128)S(1)}, u32[]{:S(2)}, u32[]{:S(2)}) collective-permute-start(f32[2,64,128]{2,1,0:T(8,128)S(1)} %get-tuple-element.41), channel_id=1, source_target_pairs={{0,2},{1,3},{2,0},{3,1},{4,6},{5,7},{6,4},{7,5},{8,10},{9,11},{10,... | collective-permute-start | bytes 196616 | tf_op jit(solution)/shard_map/ppermute | solution.py:389
  9.1 27.8 %copy-start.2 = (bf16[16,4,128,128]{3,2,1,0:T(8,128)(2,1)S(1)}, bf16[16,4,128,128]{3,2,1,0:T(8,128)(2,1)}, u32[]{:S(2)}) copy-start(bf16[16,4,128,128]{3,2,1,0:T(8,128)(2,1)} %jb_ref.1) | copy-start | bytes 6291460
  9.1 6.5 %collective-permute-start.3 = (f32[2,64,128]{2,1,0:T(8,128)S(1)}, f32[2,64,128]{2,1,0:T(8,128)S(1)}, u32[]{:S(2)}, u32[]{:S(2)}) collective-permute-start(f32[2,64,128]{2,1,0:T(8,128)S(1)} %pad_maximum_fusion.1), channel_id=1, source_target_pairs={{0,24},{1,25},{2,26},{3,27},{4,28},{5,29},{6,30},{7,31},{8,16},{9,... | collective-permute-start | bytes 196616 | tf_op jit(solution)/shard_map/ppermute | solution.py:389
  12.8 6.0 %collective-permute-start.2 = (f32[2,64,128]{2,1,0:T(8,128)S(1)}, f32[2,64,128]{2,1,0:T(8,128)S(1)}, u32[]{:S(2)}, u32[]{:S(2)}) collective-permute-start(f32[2,64,128]{2,1,0:T(8,128)S(1)} %pad_maximum_fusion.1), channel_id=1, source_target_pairs={{0,16},{1,17},{2,18},{3,19},{4,20},{5,21},{6,22},{7,23},{8,24},{9,... | collective-permute-start | bytes 196616 | tf_op jit(solution)/shard_map/ppermute | solution.py:389
  12.8 6.0 %collective-permute-start.1 = (f32[2,64,128]{2,1,0:T(8,128)S(1)}, f32[2,64,128]{2,1,0:T(8,128)S(1)}, u32[]{:S(2)}, u32[]{:S(2)}) collective-permute-start(f32[2,64,128]{2,1,0:T(8,128)S(1)} %pad_maximum_fusion.1), channel_id=1, source_target_pairs={{0,8},{1,9},{2,10},{3,11},{4,12},{5,13},{6,14},{7,15},{8,0},{9,1},... | collective-permute-start | bytes 196616 | tf_op jit(solution)/shard_map/ppermute | solution.py:389
  18.8 4.3 %collective-permute-start.5 = (f32[2,64,128]{2,1,0:T(8,128)S(1)}, f32[2,64,128]{2,1,0:T(8,128)S(1)}, u32[]{:S(2)}, u32[]{:S(2)}) collective-permute-start(f32[2,64,128]{2,1,0:T(8,128)S(1)} %pad_maximum_fusion.2), channel_id=1, source_target_pairs={{0,4},{1,5},{2,6},{3,7},{4,0},{5,1},{6,2},{7,3},{8,12},{9,13},{10,... | collective-permute-start | bytes 196616 | tf_op jit(solution)/shard_map/ppermute | solution.py:389
  20.0 8.9 %collective-permute-start.8 = (f32[2048,128]{1,0:T(8,128)S(1)}, f32[2048,128]{1,0:T(8,128)}, u32[]{:S(2)}, u32[]{:S(2)}) collective-permute-start(f32[2048,128]{1,0:T(8,128)S(1)} %copy-done.1), channel_id=1, source_target_pairs={{0,2},{1,3},{2,0},{3,1},{4,6},{5,7},{6,4},{7,5},{8,10},{9,11},{10,... | collective-permute-start | bytes 3145736 | tf_op jit(solution)/shard_map/ppermute | solution.py:389
  20.0 16.8 %collective-permute-start.9 = (f32[2048,128]{1,0:T(8,128)S(1)}, f32[2048,128]{1,0:T(8,128)}, u32[]{:S(2)}, u32[]{:S(2)}) collective-permute-start(f32[2048,128]{1,0:T(8,128)S(1)} %copy-done.1), channel_id=1, source_target_pairs={{6,8},{8,6},{14,16},{16,14},{22,24},{24,22},{7,9},{9,7},{15,17},{1... | collective-permute-start | bytes 3145736 | tf_op jit(solution)/shard_map/ppermute | solution.py:412
  23.2 4.3 %collective-permute-start.6 = (f32[2,64,128]{2,1,0:T(8,128)S(1)}, f32[2,64,128]{2,1,0:T(8,128)S(1)}, u32[]{:S(2)}, u32[]{:S(2)}) collective-permute-start(f32[2,64,128]{2,1,0:T(8,128)S(1)} %pad_maximum_fusion.3), channel_id=1, source_target_pairs={{0,1},{1,0},{2,3},{3,2},{4,5},{5,4},{6,7},{7,6},{8,9},{9,8},{10,11... | collective-permute-start | bytes 196616 | tf_op jit(solution)/shard_map/ppermute | solution.py:389
  27.6 1.3 %collective-permute-start.7 = (f32[2,64,128]{2,1,0:T(8,128)S(1)}, f32[2,64,128]{2,1,0:T(8,128)S(1)}, u32[]{:S(2)}, u32[]{:S(2)}) collective-permute-start(f32[2,64,128]{2,1,0:T(8,128)S(1)} %pad_maximum_fusion.4), channel_id=1, source_target_pairs={{0,2},{1,3},{2,0},{3,1},{4,6},{5,7},{6,4},{7,5},{8,10},{9,11},{10,... | collective-permute-start | bytes 196616 | tf_op jit(solution)/shard_map/ppermute | solution.py:389
  40.3 1.3 %collective-permute-start.10 = (f32[128,128]{1,0:T(8,128)S(1)}, f32[128,128]{1,0:T(8,128)S(1)}, u32[]{:S(2)}, u32[]{:S(2)}) collective-permute-start(f32[128,128]{1,0:T(8,128)S(1)} %get-tuple-element.27), channel_id=1, source_target_pairs={{0,2},{1,3},{2,0},{3,1},{4,6},{5,7},{6,4},{7,5},{8,10},{9,11},{10,... | collective-permute-start | bytes 196616 | tf_op jit(solution)/shard_map/ppermute | solution.py:389
  41.7 5.4 %collective-permute-start.13 = (f32[128,128]{1,0:T(8,128)S(1)}, f32[128,128]{1,0:T(8,128)S(1)}, u32[]{:S(2)}, u32[]{:S(2)}) collective-permute-start(f32[128,128]{1,0:T(8,128)S(1)} %add.226), channel_id=1, source_target_pairs={{0,5},{1,4},{2,7},{3,6},{4,1},{5,0},{6,3},{7,2},{8,13},{9,12},{10,... | collective-permute-start | bytes 196616 | tf_op jit(solution)/shard_map/ppermute | solution.py:389
  44.4 4.3 %collective-permute-start.12 = (f32[128,128]{1,0:T(8,128)S(1)}, f32[128,128]{1,0:T(8,128)S(1)}, u32[]{:S(2)}, u32[]{:S(2)}) collective-permute-start(f32[128,128]{1,0:T(8,128)S(1)} %add.226), channel_id=1, source_target_pairs={{0,4},{1,5},{2,6},{3,7},{4,0},{5,1},{6,2},{7,3},{8,12},{9,13},{10,... | collective-permute-start | bytes 196616 | tf_op jit(solution)/shard_map/ppermute | solution.py:389
  44.7 4.3 %collective-permute-start.11 = (f32[128,128]{1,0:T(8,128)S(1)}, f32[128,128]{1,0:T(8,128)S(1)}, u32[]{:S(2)}, u32[]{:S(2)}) collective-permute-start(f32[128,128]{1,0:T(8,128)S(1)} %add.226), channel_id=1, source_target_pairs={{0,1},{1,0},{2,3},{3,2},{4,5},{5,4},{6,7},{7,6},{8,9},{9,8},{10,11... | collective-permute-start | bytes 196616 | tf_op jit(solution)/shard_map/ppermute | solution.py:389
  49.0 6.6 %collective-permute-start.16 = (f32[128,128]{1,0:T(8,128)S(1)}, f32[128,128]{1,0:T(8,128)S(1)}, u32[]{:S(2)}, u32[]{:S(2)}) collective-permute-start(f32[128,128]{1,0:T(8,128)S(1)} %add_add_fusion), channel_id=1, source_target_pairs={{0,24},{1,25},{2,26},{3,27},{4,28},{5,29},{6,30},{7,31},{8,16},{9,... | collective-permute-start | bytes 196616 | tf_op jit(solution)/shard_map/ppermute | solution.py:389
  52.9 5.3 %collective-permute-start.15 = (f32[128,128]{1,0:T(8,128)S(1)}, f32[128,128]{1,0:T(8,128)S(1)}, u32[]{:S(2)}, u32[]{:S(2)}) collective-permute-start(f32[128,128]{1,0:T(8,128)S(1)} %add_add_fusion), channel_id=1, source_target_pairs={{0,16},{1,17},{2,18},{3,19},{4,20},{5,21},{6,22},{7,23},{8,24},{9,... | collective-permute-start | bytes 196616 | tf_op jit(solution)/shard_map/ppermute | solution.py:389
  52.9 5.3 %collective-permute-start.14 = (f32[128,128]{1,0:T(8,128)S(1)}, f32[128,128]{1,0:T(8,128)S(1)}, u32[]{:S(2)}, u32[]{:S(2)}) collective-permute-start(f32[128,128]{1,0:T(8,128)S(1)} %add_add_fusion), channel_id=1, source_target_pairs={{0,8},{1,9},{2,10},{3,11},{4,12},{5,13},{6,14},{7,15},{8,0},{9,1},... | collective-permute-start | bytes 196616 | tf_op jit(solution)/shard_map/ppermute | solution.py:389

commit v6 on v5

--- a/solution.py
+++ b/solution.py
@@ -9,7 +9,6 @@
 
 F32 = jnp.float32
 BF16 = jnp.bfloat16
-HIGH = lax.Precision.HIGHEST
 VMEM_LIMIT = 24 * 1024 * 1024
 CHUNK = 512
 TILE = 256
@@ -198,12 +197,13 @@
     c = lax.broadcasted_iota(jnp.int32, (k, k), 1)
     half = lambda x: jnp.where(c < r, x, jnp.where(c == r, 0.5 * x, 0.0))
     f = half(e)
-    ff = mm3(f, f)
-    n = half(mm3(f, f, (1, 1)) + (ff + ff.T)) - f
+    fb = f.astype(BF16)
+    ff = mm(fb, fb)
+    n = half(mm(fb, fb, (1, 1)) + (ff + ff.T)) - f
     ne = mm3(n, e)
     left = (e + (n + n.T)) + ((ne + ne.T) + mm3(n + ne, n, (1, 1)))
     step = half(left)
-    return jnp.where(c == r, 1.0, 0.0) + (n - (step + mm3(step, n)))
+    return n - (step + mm(step.astype(BF16), n.astype(BF16)))
 
 
 def scaled(high, low):
@@ -213,7 +213,8 @@
     diagonal = jnp.where(r == c, high, 0.0)
     row = power_of_two(jnp.sqrt(jnp.max(diagonal, axis=0, keepdims=True)))
     col = power_of_two(jnp.sqrt(jnp.max(diagonal, axis=1, keepdims=True)))
-    return (high / row) / col, (low / row) / col, row
+    inv_row, inv_col = 1.0 / row, 1.0 / col
+    return (high * inv_row) * inv_col, (low * inv_row) * inv_col, row, inv_row
 
 
 def by_weight(products, k, n, m):
@@ -229,10 +230,10 @@
     return p[:, :k] + (p[:, k:] + q)
 
 
-def factors_kernel(count, g_ref, s_ref, chip_ref, up_ref, w1_ref, w2_ref, modes_ref, low_ref, mb_ref, inv2_ref):
+def factors_kernel(count, g_ref, s_ref, chip_ref, up_ref, w1_ref, w2_ref, modes_ref, low_ref, mb_ref, more_ref):
     k = g_ref.shape[1]
-    high, low, row = scaled(g_ref[0], g_ref[1])
-    inv1 = inverse_factor(0.5 * (high + high.T))
+    high, low, row, inv_row = scaled(g_ref[0], g_ref[1])
+    inv1 = inverse_factor(high)
     size = power_of_two(jnp.max(jnp.abs(inv1), axis=1, keepdims=True))
     p, left = cut(inv1, size, 3)
     inv1 = inv1 - left
@@ -252,19 +253,21 @@
 
     @pl.when(near)
     def _():
-        inv2_ref[...] = inverse_factor_near_one(e)
+        more_ref[...] = inverse_factor_near_one(e)
 
     @pl.when(jnp.logical_not(near))
     def _():
-        inv2_ref[...] = inverse_factor(jnp.where(c == r, 1.0 + e, e))
-
-    both = jnp.dot(inv2_ref[...], jnp.concatenate([inv1, y], axis=1), precision=HIGH, preferred_element_type=F32)
-    inverse = (both[:, :k] / row) * math.sqrt(count)
+        inv2 = inverse_factor(jnp.where(c == r, 1.0 + e, e))
+        more_ref[...] = jnp.where(c == r, inv2 - 1.0, inv2)
+
+    both = jnp.concatenate([inv1, y], axis=1)
+    both = both + mm3(more_ref[...], both)
+    inverse = (both[:, :k] * inv_row) * math.sqrt(count)
     h, m, l = split3(inverse.T)
     hm = jnp.concatenate([h, m], axis=1)
     w1_ref[...] = jnp.concatenate([hm, hm], axis=0)
     w2_ref[...] = jnp.concatenate([l, h], axis=0)
-    up_ref[...] = jnp.where(c >= r, (both[:, k:] * row) / math.sqrt(count), 0.0)
+    up_ref[...] = jnp.where(c >= r, (both[:, k:] * row) * (1.0 / math.sqrt(count)), 0.0)
     for at in (slice(i, i + TILE) for i in range(0, s_ref.shape[0], TILE)):
         modes = modes_of(s_ref[at, :], w1_ref[...], w2_ref[...])
         modes_ref[at, :] = modes
@@ -405,13 +408,14 @@
         half = gram.shape[1] // 2
         upper, lower = gram[:, :half], gram[:, half:]
         mine = add_pairs(jnp.where(even, upper, lower), swap(jnp.where(even, lower, upper), core_mask))
+        mine, chip = lax.optimization_barrier((mine, chip))
         for phase in masks_far:
             mine = exchange(mine, phase, add_pairs)
         mine, inner, late = lax.optimization_barrier((mine, inner, snapshots))
         mine = exchange(mine, masks_x, add_pairs)
         outer = lax.ppermute(late, "bulk", pairs(3))
-        mine = exchange(mine, masks_y, add_pairs)
-        other = swap(mine, core_mask)
+        along_y, other, across = (swap(mine, mask) for mask in (masks_y[0], core_mask, masks_y[0] | core_mask))
+        mine, other = add_pairs(mine, along_y), add_pairs(other, across)
         gram = jnp.concatenate([jnp.where(even, mine, other), jnp.where(even, other, mine)], axis=1)
         factor, w1, w2, modes, low, mb = factors_and_chip_modes(gram, snapshots, chip, rows_total)
         modes, jac_modes, reduced = apply_and_project(jac_cols, modes, low, mb, inner, outer, w1, w2, jac_blocks)

time: 59.2 us -> 59.2 us (level)
  starting transfers between devices: 22.3 us -> 23.2 us
  waiting for transfers between devices: 20.3 us -> 19.5 us
    ppermute x15 -> x16, starting transfers between devices: 19 us -> 20 us  [swap(): return lax.ppermute(value, axes, [(i, i ^ mask) for i in range(count)])]
    ppermute x15 -> x16, waiting for transfers between devices: 20.3 us -> 19.5 us  [swap(): return lax.ppermute(value, axes, [(i, i ^ mask) for i in range(count)])]
  transfers between devices with their start and end apart: 17 -> 18, of which waited for: 12 -> 12; matrix products, arithmetic and copies ran while one was open for 2% -> 2% of each run, Pallas kernels for 15% -> 15%
where the time goes in v6:
time: 59.2 us; the launch traced here: 59 us
  starting transfers between devices  23.2 us (39%)
  waiting for transfers between devices  19.5 us (33%)
  Pallas kernels  12.4 us (21%)
  local copies, waits for them, and re-layouts  2.11 us (4%)
  other arithmetic  0.87 us (1%)
  between operations  0.81 us (1%)
    ppermute x16, starting transfers between devices, swap(): return lax.ppermute(value, axes, [(i, i ^ mask) for i in range(count)])  20 us
    ppermute x16, waiting for transfers between devices, swap(): return lax.ppermute(value, axes, [(i, i ^ mask) for i in range(count)])  19.5 us
    pallas_call x1, Pallas kernels, factors_and_chip_modes(): pl.pallas_call(lambda *refs: factors_kernel(count, *refs), in_specs=[vmem...  7.84 us
    pallas_call x1, Pallas kernels, apply_and_project(): pl.pallas_call(apply_kernel, in_specs=[hbm] + [vmem] * 8, out_specs=(hbm,...  3.43 us
    unnamed x10, local copies, waits for them, and re-layouts  2.11 us
    ppermute x1, starting transfers between devices, shards(): outer = lax.ppermute(late, 'bulk', pairs(3))  1.65 us
    ppermute x1, starting transfers between devices, shards(): inner = lax.ppermute(snapshots, 'bulk', pairs(1))  1.62 us
  transfers between devices with their start and end apart: 18, of which 12 were waited for; matrix products, arithmetic and copies ran while one was open for 2% of the time, Pallas kernels for 15%

profile of v6, /device:TPU:0, one launch (start us, length us, event | category | flops | bytes accessed | tf_op | source)
XLA Modules:
  0.0 59.0 jit_solution(10322887938797304359)
XLA Ops:
  0.6 0.0 copy-start.3
  0.6 0.5 collective-permute-start.1
  1.2 1.6 %collective-permute-start.5 = (f32[2048,128]{1,0:T(8,128)}, f32[2048,128]{1,0:T(8,128)}, u32[]{:S(2)}, u32[]{:S(2)}) collective-permute-start(f32[2048,128]{1,0:T(8,128)} %refs_1_.1), channel_id=1, source_target_pairs={{2,4},{4,2},{10,12},{12,10},{18,20},{20,18},{26,28},{28,26},{3,5},... | collective-permute-start | bytes 3145736 | tf_op jit(solution)/shard_map/ppermute | solution.py:406
  2.8 1.2 %copy-done = f32[2048,128]{1,0:T(8,128)S(1)} copy-done((f32[2048,128]{1,0:T(8,128)S(1)}, f32[2048,128]{1,0:T(8,128)}, u32[]{:S(2)}) %copy-start) | copy-done | bytes 1048600
  4.0 1.2 %local_gram.1 = f32[2,128,128]{2,1,0:T(8,128)S(1)} custom-call(f32[2048,128]{1,0:T(8,128)S(1)} %copy-done), custom_call_target="tpu_custom_call" | custom-call | tf_op jit(solution)/shard_map/local_gram/pallas_call | solution.py:120
  5.2 3.0 %collective-permute-start = (f32[2,64,128]{2,1,0:T(8,128)S(1)}, f32[2,64,128]{2,1,0:T(8,128)S(1)}, u32[]{:S(2)}, u32[]{:S(2)}) collective-permute-start(f32[2,64,128]{2,1,0:T(8,128)S(1)} %get-tuple-element.47), channel_id=1, source_target_pairs={{0,2},{1,3},{2,0},{3,1},{4,6},{5,7},{6,4},{7,5},{8,10},{9,11},{10,... | collective-permute-start | bytes 196616 | tf_op jit(solution)/shard_map/ppermute | solution.py:392
  8.2 0.9 %collective-permute-done = f32[2,64,128]{2,1,0:T(8,128)S(1)} collective-permute-done((f32[2,64,128]{2,1,0:T(8,128)S(1)}, f32[2,64,128]{2,1,0:T(8,128)S(1)}, u32[]{:S(2)}, u32[]{:S(2)}) %collective-permute-start) | collective-permute-done | bytes 65568 | tf_op jit(solution)/shard_map/ppermute | solution.py:392
  9.1 0.0 copy-start.2
  9.2 0.0 collective-permute-done.1.refs_2_
  9.2 2.7 %collective-permute-start.3 = (f32[2,64,128]{2,1,0:T(8,128)S(1)}, f32[2,64,128]{2,1,0:T(8,128)S(1)}, u32[]{:S(2)}, u32[]{:S(2)}) collective-permute-start(f32[2,64,128]{2,1,0:T(8,128)S(1)} %pad_maximum_fusion.1), channel_id=1, source_target_pairs={{0,16},{1,17},{2,18},{3,19},{4,20},{5,21},{6,22},{7,23},{8,24},{9,... | collective-permute-start | bytes 196616 | tf_op jit(solution)/shard_map/ppermute | solution.py:392
  11.8 1.3 %collective-permute-start.4 = (f32[2,64,128]{2,1,0:T(8,128)S(1)}, f32[2,64,128]{2,1,0:T(8,128)S(1)}, u32[]{:S(2)}, u32[]{:S(2)}) collective-permute-start(f32[2,64,128]{2,1,0:T(8,128)S(1)} %pad_maximum_fusion.1), channel_id=1, source_target_pairs={{0,24},{1,25},{2,26},{3,27},{4,28},{5,29},{6,30},{7,31},{8,16},{9,... | collective-permute-start | bytes 196616 | tf_op jit(solution)/shard_map/ppermute | solution.py:392
  13.2 0.2 collective-permute-start.2
  13.4 2.7 %collective-permute-done.3 = f32[2,64,128]{2,1,0:T(8,128)S(1)} collective-permute-done((f32[2,64,128]{2,1,0:T(8,128)S(1)}, f32[2,64,128]{2,1,0:T(8,128)S(1)}, u32[]{:S(2)}, u32[]{:S(2)}) %collective-permute-start.3) | collective-permute-done | bytes 65568 | tf_op jit(solution)/shard_map/ppermute | solution.py:392
  16.1 2.3 %collective-permute-done.4 = f32[2,64,128]{2,1,0:T(8,128)S(1)} collective-permute-done((f32[2,64,128]{2,1,0:T(8,128)S(1)}, f32[2,64,128]{2,1,0:T(8,128)S(1)}, u32[]{:S(2)}, u32[]{:S(2)}) %collective-permute-start.4) | collective-permute-done | bytes 65568 | tf_op jit(solution)/shard_map/ppermute | solution.py:392
  18.4 0.3 collective-permute-done.2
  18.8 0.0 collective-permute-done.5.inner_ref
  18.8 1.3 %collective-permute-start.6 = (f32[2,64,128]{2,1,0:T(8,128)S(1)}, f32[2,64,128]{2,1,0:T(8,128)S(1)}, u32[]{:S(2)}, u32[]{:S(2)}) collective-permute-start(f32[2,64,128]{2,1,0:T(8,128)S(1)} %pad_maximum_fusion.2), channel_id=1, source_target_pairs={{0,4},{1,5},{2,6},{3,7},{4,0},{5,1},{6,2},{7,3},{8,12},{9,13},{10,... | collective-permute-start | bytes 196616 | tf_op jit(solution)/shard_map/ppermute | solution.py:392
  20.1 0.0 copy-done.1
  20.1 1.7 %collective-permute-start.10 = (f32[2048,128]{1,0:T(8,128)S(1)}, f32[2048,128]{1,0:T(8,128)}, u32[]{:S(2)}, u32[]{:S(2)}) collective-permute-start(f32[2048,128]{1,0:T(8,128)S(1)} %copy-done.1), channel_id=1, source_target_pairs={{6,8},{8,6},{14,16},{16,14},{22,24},{24,22},{7,9},{9,7},{15,17},{1... | collective-permute-start | bytes 3145736 | tf_op jit(solution)/shard_map/ppermute | solution.py:416
  21.7 1.4 %collective-permute-done.6 = f32[2,64,128]{2,1,0:T(8,128)S(1)} collective-permute-done((f32[2,64,128]{2,1,0:T(8,128)S(1)}, f32[2,64,128]{2,1,0:T(8,128)S(1)}, u32[]{:S(2)}, u32[]{:S(2)}) %collective-permute-start.6) | collective-permute-done | bytes 65568 | tf_op jit(solution)/shard_map/ppermute | solution.py:392
  23.1 0.3 collective-permute-start.9
  23.4 1.4 %collective-permute-start.8 = (f32[2,64,128]{2,1,0:T(8,128)S(1)}, f32[2,64,128]{2,1,0:T(8,128)S(1)}, u32[]{:S(2)}, u32[]{:S(2)}) collective-permute-start(f32[2,64,128]{2,1,0:T(8,128)S(1)} %pad_maximum_fusion.3), channel_id=1, source_target_pairs={{0,2},{1,3},{2,0},{3,1},{4,6},{5,7},{6,4},{7,5},{8,10},{9,11},{10,... | collective-permute-start | bytes 196616 | tf_op jit(solution)/shard_map/ppermute | solution.py:392
  24.9 0.0 copy-done.3
  24.9 0.1 copy.7.cols_hbm
  24.9 0.5 collective-permute-start.7
  25.4 2.1 %collective-permute-done.9 = f32[2,64,128]{2,1,0:T(8,128)S(1)} collective-permute-done((f32[2,64,128]{2,1,0:T(8,128)S(1)}, f32[2,64,128]{2,1,0:T(8,128)S(1)}, u32[]{:S(2)}, u32[]{:S(2)}) %collective-permute-start.9) | collective-permute-done | bytes 65568 | tf_op jit(solution)/shard_map/ppermute | solution.py:392
  27.5 0.0 collective-permute-done.8
  27.6 1.7 %collective-permute-done.7 = f32[2,64,128]{2,1,0:T(8,128)S(1)} collective-permute-done((f32[2,64,128]{2,1,0:T(8,128)S(1)}, f32[2,64,128]{2,1,0:T(8,128)S(1)}, u32[]{:S(2)}, u32[]{:S(2)}) %collective-permute-start.7) | collective-permute-done | bytes 65568 | tf_op jit(solution)/shard_map/ppermute | solution.py:392
  29.3 7.8 %factors_and_chip_modes.1 = (f32[128,128]{1,0:T(8,128)}, bf16[256,256]{1,0:T(8,128)(2,1)S(1)}, bf16[256,128]{1,0:T(8,128)(2,1)S(1)}, f32[2048,128]{1,0:T(8,128)S...) custom-call(f32[2,128,128]{2,1,0:T(8,128)S(1)} %pad_maximum_fusion.refs_0_, ...), custom_call_target="tpu_custom_call" | custom-call | tf_op jit(solution)/shard_map/factors_and_chip_modes/pallas_call | solution.py:282
  37.1 0.0 collective-permute-done.10.outer_ref
  37.1 0.0 copy-done.2
  37.1 3.4 %apply_and_project.1 = (f32[2048,128]{1,0:T(8,128)}, bf16[2048,128]{1,0:T(8,128)(2,1)S(1)}, f32[128,128]{1,0:T(8,128)S(1)}) custom-call(s32[16,4]{1,0:T(8,128)S(1)} %copy.7.cols_hbm, f32[2048,128]{1,0:T(8,128)S(1)} %get-tuple-element.21.modes_ref, bf16[2048,128]{1,0:T(8,128)(2,1)S(1)} %get-tuple-element.22.low_ref, ...), custom_call_target="tpu_custom_call" | custom-call | tf_op jit(solution)/shard_map/apply_and_project/pallas_call | solution.py:358
  40.6 0.1 collective-permute-start.11
  40.7 1.2 %collective-permute-done.11 = f32[128,128]{1,0:T(8,128)S(1)} collective-permute-done((f32[128,128]{1,0:T(8,128)S(1)}, f32[128,128]{1,0:T(8,128)S(1)}, u32[]{:S(2)}, u32[]{:S(2)}) %collective-permute-start.11) | collective-permute-done | bytes 65568 | tf_op jit(solution)/shard_map/ppermute | solution.py:392
  41.9 2.4 %collective-permute-start.14 = (f32[128,128]{1,0:T(8,128)S(1)}, f32[128,128]{1,0:T(8,128)S(1)}, u32[]{:S(2)}, u32[]{:S(2)}) collective-permute-start(f32[128,128]{1,0:T(8,128)S(1)} %add.246), channel_id=1, source_target_pairs={{0,5},{1,4},{2,7},{3,6},{4,1},{5,0},{6,3},{7,2},{8,13},{9,12},{10,... | collective-permute-start | bytes 196616 | tf_op jit(solution)/shard_map/ppermute | solution.py:392
  44.3 0.0 collective-permute-start.13
  44.3 1.2 %collective-permute-start.12 = (f32[128,128]{1,0:T(8,128)S(1)}, f32[128,128]{1,0:T(8,128)S(1)}, u32[]{:S(2)}, u32[]{:S(2)}) collective-permute-start(f32[128,128]{1,0:T(8,128)S(1)} %add.246), channel_id=1, source_target_pairs={{0,1},{1,0},{2,3},{3,2},{4,5},{5,4},{6,7},{7,6},{8,9},{9,8},{10,11... | collective-permute-start | bytes 196616 | tf_op jit(solution)/shard_map/ppermute | solution.py:392
  45.5 1.7 %collective-permute-done.14 = f32[128,128]{1,0:T(8,128)S(1)} collective-permute-done((f32[128,128]{1,0:T(8,128)S(1)}, f32[128,128]{1,0:T(8,128)S(1)}, u32[]{:S(2)}, u32[]{:S(2)}) %collective-permute-start.14) | collective-permute-done | bytes 65568 | tf_op jit(solution)/shard_map/ppermute | solution.py:392
  47.2 1.4 %collective-permute-done.13 = f32[128,128]{1,0:T(8,128)S(1)} collective-permute-done((f32[128,128]{1,0:T(8,128)S(1)}, f32[128,128]{1,0:T(8,128)S(1)}, u32[]{:S(2)}, u32[]{:S(2)}) %collective-permute-start.13) | collective-permute-done | bytes 65568 | tf_op jit(solution)/shard_map/ppermute | solution.py:392
  48.5 0.0 collective-permute-done.12
  48.6 4.4 %collective-permute-start.17 = (f32[128,128]{1,0:T(8,128)S(1)}, f32[128,128]{1,0:T(8,128)S(1)}, u32[]{:S(2)}, u32[]{:S(2)}) collective-permute-start(f32[128,128]{1,0:T(8,128)S(1)} %add_add_fusion), channel_id=1, source_target_pairs={{0,24},{1,25},{2,26},{3,27},{4,28},{5,29},{6,30},{7,31},{8,16},{9,... | collective-permute-start | bytes 196616 | tf_op jit(solution)/shard_map/ppermute | solution.py:392
  53.0 0.0 collective-permute-start.16
  53.0 0.6 %collective-permute-start.15 = (f32[128,128]{1,0:T(8,128)S(1)}, f32[128,128]{1,0:T(8,128)S(1)}, u32[]{:S(2)}, u32[]{:S(2)}) collective-permute-start(f32[128,128]{1,0:T(8,128)S(1)} %add_add_fusion), channel_id=1, source_target_pairs={{0,8},{1,9},{2,10},{3,11},{4,12},{5,13},{6,14},{7,15},{8,0},{9,1},... | collective-permute-start | bytes 196616 | tf_op jit(solution)/shard_map/ppermute | solution.py:392
  53.6 0.8 %copy.8 = bf16[2048,128]{1,0:T(8,128)(2,1)} copy(bf16[2048,128]{1,0:T(8,128)(2,1)S(1)} %get-tuple-element.50) | data formatting | bytes 1048576
  54.4 1.2 %collective-permute-done.17 = f32[128,128]{1,0:T(8,128)S(1)} collective-permute-done((f32[128,128]{1,0:T(8,128)S(1)}, f32[128,128]{1,0:T(8,128)S(1)}, u32[]{:S(2)}, u32[]{:S(2)}) %collective-permute-start.17) | collective-permute-done | bytes 65568 | tf_op jit(solution)/shard_map/ppermute | solution.py:392
  55.6 2.7 %collective-permute-done.16 = f32[128,128]{1,0:T(8,128)S(1)} collective-permute-done((f32[128,128]{1,0:T(8,128)S(1)}, f32[128,128]{1,0:T(8,128)S(1)}, u32[]{:S(2)}, u32[]{:S(2)}) %collective-permute-start.16) | collective-permute-done | bytes 65568 | tf_op jit(solution)/shard_map/ppermute | solution.py:392
  58.3 0.0 collective-permute-done.15
  58.3 0.6 %add_multiply_fusion = f32[128,128]{1,0:T(8,128)} fusion(f32[128,128]{1,0:T(8,128)S(1)} %collective-permute-done.16, f32[128,128]{1,0:T(8,128)S(1)} %collective-permute-done.17, f32[128,128]{1,0:T(8,128)S(1)} %add_add_fusion, f32[128,128]{1,0:T(8,128)S(1)} %collective-permute-done.15), kind=kLoop, calls=%fused_computation.6 | loop fusion | flops 65536 | bytes 327680 | tf_op jit(solution)/shard_map/div | solution.py:425
  (16 shorter events, 0.2 us)
Async XLA Ops:
  0.6 24.2 %copy-start.3 = (s32[16,4]{0,1:T(4,128)S(1)}, s32[16,4]{0,1:T(4,128)}, u32[]{:S(2)}) copy-start(s32[16,4]{0,1:T(4,128)} %param.5) | copy-start | bytes 772
  0.6 8.5 %collective-permute-start.1 = (f32[2048,128]{1,0:T(8,128)}, f32[2048,128]{1,0:T(8,128)}, u32[]{:S(2)}, u32[]{:S(2)}) collective-permute-start(f32[2048,128]{1,0:T(8,128)} %refs_1_.1), channel_id=1, source_target_pairs={{0,2},{1,3},{2,0},{3,1},{4,6},{5,7},{6,4},{7,5},{8,10},{9,11},{10,... | collective-permute-start | bytes 3145736 | tf_op jit(solution)/shard_map/ppermute | solution.py:392
  1.2 17.6 %collective-permute-start.5 = (f32[2048,128]{1,0:T(8,128)}, f32[2048,128]{1,0:T(8,128)}, u32[]{:S(2)}, u32[]{:S(2)}) collective-permute-start(f32[2048,128]{1,0:T(8,128)} %refs_1_.1), channel_id=1, source_target_pairs={{2,4},{4,2},{10,12},{12,10},{18,20},{20,18},{26,28},{28,26},{3,5},... | collective-permute-start | bytes 3145736 | tf_op jit(solution)/shard_map/ppermute | solution.py:406
  2.8 1.2 %copy-start = (f32[2048,128]{1,0:T(8,128)S(1)}, f32[2048,128]{1,0:T(8,128)}, u32[]{:S(2)}) copy-start(f32[2048,128]{1,0:T(8,128)} %refs_1_.1) | copy-start | bytes 3145732
  4.0 16.1 %copy-start.1 = (f32[2048,128]{1,0:T(8,128)S(1)}, f32[2048,128]{1,0:T(8,128)}, u32[]{:S(2)}) copy-start(f32[2048,128]{1,0:T(8,128)} %refs_1_.1) | copy-start | bytes 3145732
  5.2 3.9 %collective-permute-start = (f32[2,64,128]{2,1,0:T(8,128)S(1)}, f32[2,64,128]{2,1,0:T(8,128)S(1)}, u32[]{:S(2)}, u32[]{:S(2)}) collective-permute-start(f32[2,64,128]{2,1,0:T(8,128)S(1)} %get-tuple-element.47), channel_id=1, source_target_pairs={{0,2},{1,3},{2,0},{3,1},{4,6},{5,7},{6,4},{7,5},{8,10},{9,11},{10,... | collective-permute-start | bytes 196616 | tf_op jit(solution)/shard_map/ppermute | solution.py:392
  9.1 28.0 %copy-start.2 = (bf16[16,4,128,128]{3,2,1,0:T(8,128)(2,1)S(1)}, bf16[16,4,128,128]{3,2,1,0:T(8,128)(2,1)}, u32[]{:S(2)}) copy-start(bf16[16,4,128,128]{3,2,1,0:T(8,128)(2,1)} %jb_ref.1) | copy-start | bytes 6291460
  9.2 6.9 %collective-permute-start.3 = (f32[2,64,128]{2,1,0:T(8,128)S(1)}, f32[2,64,128]{2,1,0:T(8,128)S(1)}, u32[]{:S(2)}, u32[]{:S(2)}) collective-permute-start(f32[2,64,128]{2,1,0:T(8,128)S(1)} %pad_maximum_fusion.1), channel_id=1, source_target_pairs={{0,16},{1,17},{2,18},{3,19},{4,20},{5,21},{6,22},{7,23},{8,24},{9,... | collective-permute-start | bytes 196616 | tf_op jit(solution)/shard_map/ppermute | solution.py:392
  11.8 6.6 %collective-permute-start.4 = (f32[2,64,128]{2,1,0:T(8,128)S(1)}, f32[2,64,128]{2,1,0:T(8,128)S(1)}, u32[]{:S(2)}, u32[]{:S(2)}) collective-permute-start(f32[2,64,128]{2,1,0:T(8,128)S(1)} %pad_maximum_fusion.1), channel_id=1, source_target_pairs={{0,24},{1,25},{2,26},{3,27},{4,28},{5,29},{6,30},{7,31},{8,16},{9,... | collective-permute-start | bytes 196616 | tf_op jit(solution)/shard_map/ppermute | solution.py:392
  13.2 5.5 %collective-permute-start.2 = (f32[2,64,128]{2,1,0:T(8,128)S(1)}, f32[2,64,128]{2,1,0:T(8,128)S(1)}, u32[]{:S(2)}, u32[]{:S(2)}) collective-permute-start(f32[2,64,128]{2,1,0:T(8,128)S(1)} %pad_maximum_fusion.1), channel_id=1, source_target_pairs={{0,8},{1,9},{2,10},{3,11},{4,12},{5,13},{6,14},{7,15},{8,0},{9,1},... | collective-permute-start | bytes 196616 | tf_op jit(solution)/shard_map/ppermute | solution.py:392
  18.8 4.3 %collective-permute-start.6 = (f32[2,64,128]{2,1,0:T(8,128)S(1)}, f32[2,64,128]{2,1,0:T(8,128)S(1)}, u32[]{:S(2)}, u32[]{:S(2)}) collective-permute-start(f32[2,64,128]{2,1,0:T(8,128)S(1)} %pad_maximum_fusion.2), channel_id=1, source_target_pairs={{0,4},{1,5},{2,6},{3,7},{4,0},{5,1},{6,2},{7,3},{8,12},{9,13},{10,... | collective-permute-start | bytes 196616 | tf_op jit(solution)/shard_map/ppermute | solution.py:392
  20.1 17.0 %collective-permute-start.10 = (f32[2048,128]{1,0:T(8,128)S(1)}, f32[2048,128]{1,0:T(8,128)}, u32[]{:S(2)}, u32[]{:S(2)}) collective-permute-start(f32[2048,128]{1,0:T(8,128)S(1)} %copy-done.1), channel_id=1, source_target_pairs={{6,8},{8,6},{14,16},{16,14},{22,24},{24,22},{7,9},{9,7},{15,17},{1... | collective-permute-start | bytes 3145736 | tf_op jit(solution)/shard_map/ppermute | solution.py:416
  23.1 4.4 %collective-permute-start.9 = (f32[2,64,128]{2,1,0:T(8,128)S(1)}, f32[2,64,128]{2,1,0:T(8,128)S(1)}, u32[]{:S(2)}, u32[]{:S(2)}) collective-permute-start(f32[2,64,128]{2,1,0:T(8,128)S(1)} %pad_maximum_fusion.3), channel_id=1, source_target_pairs={{0,3},{1,2},{2,1},{3,0},{4,7},{5,6},{6,5},{7,4},{8,11},{9,10},{10,... | collective-permute-start | bytes 196616 | tf_op jit(solution)/shard_map/ppermute | solution.py:392
  23.4 4.1 %collective-permute-start.8 = (f32[2,64,128]{2,1,0:T(8,128)S(1)}, f32[2,64,128]{2,1,0:T(8,128)S(1)}, u32[]{:S(2)}, u32[]{:S(2)}) collective-permute-start(f32[2,64,128]{2,1,0:T(8,128)S(1)} %pad_maximum_fusion.3), channel_id=1, source_target_pairs={{0,2},{1,3},{2,0},{3,1},{4,6},{5,7},{6,4},{7,5},{8,10},{9,11},{10,... | collective-permute-start | bytes 196616 | tf_op jit(solution)/shard_map/ppermute | solution.py:392
  24.9 4.3 %collective-permute-start.7 = (f32[2,64,128]{2,1,0:T(8,128)S(1)}, f32[2,64,128]{2,1,0:T(8,128)S(1)}, u32[]{:S(2)}, u32[]{:S(2)}) collective-permute-start(f32[2,64,128]{2,1,0:T(8,128)S(1)} %pad_maximum_fusion.3), channel_id=1, source_target_pairs={{0,1},{1,0},{2,3},{3,2},{4,5},{5,4},{6,7},{7,6},{8,9},{9,8},{10,11... | collective-permute-start | bytes 196616 | tf_op jit(solution)/shard_map/ppermute | solution.py:392
  40.6 1.3 %collective-permute-start.11 = (f32[128,128]{1,0:T(8,128)S(1)}, f32[128,128]{1,0:T(8,128)S(1)}, u32[]{:S(2)}, u32[]{:S(2)}) collective-permute-start(f32[128,128]{1,0:T(8,128)S(1)} %get-tuple-element.31), channel_id=1, source_target_pairs={{0,2},{1,3},{2,0},{3,1},{4,6},{5,7},{6,4},{7,5},{8,10},{9,11},{10,... | collective-permute-start | bytes 196616 | tf_op jit(solution)/shard_map/ppermute | solution.py:392
  41.9 5.3 %collective-permute-start.14 = (f32[128,128]{1,0:T(8,128)S(1)}, f32[128,128]{1,0:T(8,128)S(1)}, u32[]{:S(2)}, u32[]{:S(2)}) collective-permute-start(f32[128,128]{1,0:T(8,128)S(1)} %add.246), channel_id=1, source_target_pairs={{0,5},{1,4},{2,7},{3,6},{4,1},{5,0},{6,3},{7,2},{8,13},{9,12},{10,... | collective-permute-start | bytes 196616 | tf_op jit(solution)/shard_map/ppermute | solution.py:392
  44.3 4.3 %collective-permute-start.13 = (f32[128,128]{1,0:T(8,128)S(1)}, f32[128,128]{1,0:T(8,128)S(1)}, u32[]{:S(2)}, u32[]{:S(2)}) collective-permute-start(f32[128,128]{1,0:T(8,128)S(1)} %add.246), channel_id=1, source_target_pairs={{0,4},{1,5},{2,6},{3,7},{4,0},{5,1},{6,2},{7,3},{8,12},{9,13},{10,... | collective-permute-start | bytes 196616 | tf_op jit(solution)/shard_map/ppermute | solution.py:392
  44.3 4.3 %collective-permute-start.12 = (f32[128,128]{1,0:T(8,128)S(1)}, f32[128,128]{1,0:T(8,128)S(1)}, u32[]{:S(2)}, u32[]{:S(2)}) collective-permute-start(f32[128,128]{1,0:T(8,128)S(1)} %add.246), channel_id=1, source_target_pairs={{0,1},{1,0},{2,3},{3,2},{4,5},{5,4},{6,7},{7,6},{8,9},{9,8},{10,11... | collective-permute-start | bytes 196616 | tf_op jit(solution)/shard_map/ppermute | solution.py:392
  48.6 7.1 %collective-permute-start.17 = (f32[128,128]{1,0:T(8,128)S(1)}, f32[128,128]{1,0:T(8,128)S(1)}, u32[]{:S(2)}, u32[]{:S(2)}) collective-permute-start(f32[128,128]{1,0:T(8,128)S(1)} %add_add_fusion), channel_id=1, source_target_pairs={{0,24},{1,25},{2,26},{3,27},{4,28},{5,29},{6,30},{7,31},{8,16},{9,... | collective-permute-start | bytes 196616 | tf_op jit(solution)/shard_map/ppermute | solution.py:392
  53.0 5.4 %collective-permute-start.16 = (f32[128,128]{1,0:T(8,128)S(1)}, f32[128,128]{1,0:T(8,128)S(1)}, u32[]{:S(2)}, u32[]{:S(2)}) collective-permute-start(f32[128,128]{1,0:T(8,128)S(1)} %add_add_fusion), channel_id=1, source_target_pairs={{0,16},{1,17},{2,18},{3,19},{4,20},{5,21},{6,22},{7,23},{8,24},{9,... | collective-permute-start | bytes 196616 | tf_op jit(solution)/shard_map/ppermute | solution.py:392
  53.0 5.4 %collective-permute-start.15 = (f32[128,128]{1,0:T(8,128)S(1)}, f32[128,128]{1,0:T(8,128)S(1)}, u32[]{:S(2)}, u32[]{:S(2)}) collective-permute-start(f32[128,128]{1,0:T(8,128)S(1)} %add_add_fusion), channel_id=1, source_target_pairs={{0,8},{1,9},{2,10},{3,11},{4,12},{5,13},{6,14},{7,15},{8,0},{9,1},... | collective-permute-start | bytes 196616 | tf_op jit(solution)/shard_map/ppermute | solution.py:392

commit v7 on v6

--- a/solution.py
+++ b/solution.py
@@ -73,6 +73,29 @@
         parts.append(part.astype(BF16))
         grid = grid * 2.0**-8
     return parts, x
+
+
+def packed(x):
+    k, n = x.shape[0], 8
+    lane = lax.broadcasted_iota(jnp.int32, (n, k), 1)
+    count = k // n
+    block = lambda b: x[n * b : n * b + n, :]
+    rows = [block(0)]
+    for b in range(1, count // 2):
+        rows.append(jnp.where(lane >= n * b, block(b), pltpu.roll(block(count - b), n * b, 1)))
+    return jnp.concatenate(rows + [block(count // 2)] * 2, axis=0)
+
+
+def unpacked(x):
+    k, n = x.shape[1], 8
+    count = k // n
+    block = lambda b: x[n * b : n * b + n, :]
+    rows = [block(b) for b in range(count // 2 + 1)]
+    rows += [pltpu.roll(block(count - b), k - n * (count - b), 1) for b in range(count // 2 + 1, count)]
+    x = jnp.concatenate(rows, axis=0)
+    r = lax.broadcasted_iota(jnp.int32, (k, k), 0)
+    c = lax.broadcasted_iota(jnp.int32, (k, k), 1)
+    return jnp.where((c >> 3) >= (r >> 3), x, x.T)
 
 
 def gram_kernel(s_hbm, g_ref, s_ref, sem):
@@ -111,8 +134,8 @@
     low = ab_low + (odd + 0.5 * even)
     low = (aa_low + (cross_low + total_low)) + (low + low.T)
     high = total + low
-    g_ref[0] = high
-    g_ref[1] = low - (high - total)
+    g_ref[0] = packed(high)
+    g_ref[1] = packed(low - (high - total))
 
 
 def local_gram(s):
@@ -120,7 +143,7 @@
     return pl.pallas_call(
         gram_kernel,
         in_specs=[pl.BlockSpec(memory_space=pl.ANY)],
-        out_shape=jax.ShapeDtypeStruct((2, k, k), F32),
+        out_shape=jax.ShapeDtypeStruct((2, k // 2 + 16, k), F32),
         scratch_shapes=[pltpu.VMEM((rows, k), F32), pltpu.SemaphoreType.DMA((rows // CHUNK,))],
         compiler_params=pltpu.CompilerParams(vmem_limit_bytes=VMEM_LIMIT),
         name="local_gram",
@@ -231,8 +254,8 @@
 
 
 def factors_kernel(count, g_ref, s_ref, chip_ref, up_ref, w1_ref, w2_ref, modes_ref, low_ref, mb_ref, more_ref):
-    k = g_ref.shape[1]
-    high, low, row, inv_row = scaled(g_ref[0], g_ref[1])
+    k = up_ref.shape[0]
+    high, low, row, inv_row = scaled(unpacked(g_ref[0]), unpacked(g_ref[1]))
     inv1 = inverse_factor(high)
     size = power_of_two(jnp.max(jnp.abs(inv1), axis=1, keepdims=True))
     p, left = cut(inv1, size, 3)

time: 59.2 us -> 59.4 us (level)
  starting transfers between devices: 23.2 us -> 25.3 us
  waiting for transfers between devices: 19.5 us -> 17.6 us
    ppermute x16, starting transfers between devices: 20 us -> 22.1 us  [swap(): return lax.ppermute(value, axes, [(i, i ^ mask) for i in range(count)])]
    ppermute x16, waiting for transfers between devices: 19.5 us -> 17.6 us  [swap(): return lax.ppermute(value, axes, [(i, i ^ mask) for i in range(count)])]
  transfers between devices with their start and end apart: 18 -> 18, of which waited for: 12 -> 11; matrix products, arithmetic and copies ran while one was open for 2% -> 2% of each run, Pallas kernels for 15% -> 15%
where the time goes in v7:
time: 59.4 us; the launch traced here: 59.2 us
  starting transfers between devices  25.3 us (43%)
  waiting for transfers between devices  17.6 us (30%)
  Pallas kernels  12.5 us (21%)
  local copies, waits for them, and re-layouts  2.11 us (4%)
  between operations  0.83 us (1%)
  other arithmetic  0.82 us (1%)
    ppermute x16, starting transfers between devices, swap(): return lax.ppermute(value, axes, [(i, i ^ mask) for i in range(count)])  22.1 us
    ppermute x16, waiting for transfers between devices, swap(): return lax.ppermute(value, axes, [(i, i ^ mask) for i in range(count)])  17.6 us
    pallas_call x1, Pallas kernels, factors_and_chip_modes(): pl.pallas_call(lambda *refs: factors_kernel(count, *refs), in_specs=[vmem...  7.83 us
    pallas_call x1, Pallas kernels, apply_and_project(): pl.pallas_call(apply_kernel, in_specs=[hbm] + [vmem] * 8, out_specs=(hbm,...  3.41 us
    unnamed x10, local copies, waits for them, and re-layouts  2.11 us
    ppermute x1, starting transfers between devices, shards(): outer = lax.ppermute(late, 'bulk', pairs(3))  1.65 us
    ppermute x1, starting transfers between devices, shards(): inner = lax.ppermute(snapshots, 'bulk', pairs(1))  1.62 us
    pallas_call x1, Pallas kernels, local_gram(): pl.pallas_call(gram_kernel, in_specs=[pl.BlockSpec(memory_space=pl.ANY)],...  1.25 us
  transfers between devices with their start and end apart: 18, of which 11 were waited for; matrix products, arithmetic and copies ran while one was open for 2% of the time, Pallas kernels for 15%

profile of v7, /device:TPU:0, one launch (start us, length us, event | category | flops | bytes accessed | tf_op | source)
XLA Modules:
  0.0 59.2 jit_solution(7177169398888309012)
XLA Ops:
  0.6 0.0 copy-start.3
  0.6 0.5 collective-permute-start.1
  1.2 1.6 %collective-permute-start.5 = (f32[2048,128]{1,0:T(8,128)}, f32[2048,128]{1,0:T(8,128)}, u32[]{:S(2)}, u32[]{:S(2)}) collective-permute-start(f32[2048,128]{1,0:T(8,128)} %refs_1_.1), channel_id=1, source_target_pairs={{2,4},{4,2},{10,12},{12,10},{18,20},{20,18},{26,28},{28,26},{3,5},... | collective-permute-start | bytes 3145736 | tf_op jit(solution)/shard_map/ppermute | solution.py:429
  2.8 1.2 %copy-done = f32[2048,128]{1,0:T(8,128)S(1)} copy-done((f32[2048,128]{1,0:T(8,128)S(1)}, f32[2048,128]{1,0:T(8,128)}, u32[]{:S(2)}) %copy-start) | copy-done | bytes 1048600
  4.0 1.2 %local_gram.1 = f32[2,80,128]{2,1,0:T(8,128)S(1)} custom-call(f32[2048,128]{1,0:T(8,128)S(1)} %copy-done), custom_call_target="tpu_custom_call" | custom-call | tf_op jit(solution)/shard_map/local_gram/pallas_call | solution.py:143
  5.3 0.0 copy-start.2
  5.3 3.0 %collective-permute-start = (f32[2,40,128]{2,1,0:T(8,128)S(1)}, f32[2,40,128]{2,1,0:T(8,128)S(1)}, u32[]{:S(2)}, u32[]{:S(2)}) collective-permute-start(f32[2,40,128]{2,1,0:T(8,128)S(1)} %get-tuple-element.47), channel_id=1, source_target_pairs={{0,2},{1,3},{2,0},{3,1},{4,6},{5,7},{6,4},{7,5},{8,10},{9,11},{10,... | collective-permute-start | bytes 122888 | tf_op jit(solution)/shard_map/ppermute | solution.py:415
  8.3 0.9 %collective-permute-done = f32[2,40,128]{2,1,0:T(8,128)S(1)} collective-permute-done((f32[2,40,128]{2,1,0:T(8,128)S(1)}, f32[2,40,128]{2,1,0:T(8,128)S(1)}, u32[]{:S(2)}, u32[]{:S(2)}) %collective-permute-start) | collective-permute-done | bytes 40992 | tf_op jit(solution)/shard_map/ppermute | solution.py:415
  9.2 0.0 collective-permute-done.1.refs_2_
  9.2 2.7 %collective-permute-start.3 = (f32[2,40,128]{2,1,0:T(8,128)S(1)}, f32[2,40,128]{2,1,0:T(8,128)S(1)}, u32[]{:S(2)}, u32[]{:S(2)}) collective-permute-start(f32[2,40,128]{2,1,0:T(8,128)S(1)} %pad_maximum_fusion.1), channel_id=1, source_target_pairs={{0,16},{1,17},{2,18},{3,19},{4,20},{5,21},{6,22},{7,23},{8,24},{9,... | collective-permute-start | bytes 122888 | tf_op jit(solution)/shard_map/ppermute | solution.py:415
  11.9 1.4 %collective-permute-start.4 = (f32[2,40,128]{2,1,0:T(8,128)S(1)}, f32[2,40,128]{2,1,0:T(8,128)S(1)}, u32[]{:S(2)}, u32[]{:S(2)}) collective-permute-start(f32[2,40,128]{2,1,0:T(8,128)S(1)} %pad_maximum_fusion.1), channel_id=1, source_target_pairs={{0,24},{1,25},{2,26},{3,27},{4,28},{5,29},{6,30},{7,31},{8,16},{9,... | collective-permute-start | bytes 122888 | tf_op jit(solution)/shard_map/ppermute | solution.py:415
  13.2 0.2 collective-permute-start.2
  13.4 0.7 %collective-permute-done.3 = f32[2,40,128]{2,1,0:T(8,128)S(1)} collective-permute-done((f32[2,40,128]{2,1,0:T(8,128)S(1)}, f32[2,40,128]{2,1,0:T(8,128)S(1)}, u32[]{:S(2)}, u32[]{:S(2)}) %collective-permute-start.3) | collective-permute-done | bytes 40992 | tf_op jit(solution)/shard_map/ppermute | solution.py:415
  14.2 3.5 %collective-permute-done.4 = f32[2,40,128]{2,1,0:T(8,128)S(1)} collective-permute-done((f32[2,40,128]{2,1,0:T(8,128)S(1)}, f32[2,40,128]{2,1,0:T(8,128)S(1)}, u32[]{:S(2)}, u32[]{:S(2)}) %collective-permute-start.4) | collective-permute-done | bytes 40992 | tf_op jit(solution)/shard_map/ppermute | solution.py:415
  17.7 0.0 collective-permute-done.2
  17.7 0.0 collective-permute-done.5.inner_ref
  17.7 2.4 %collective-permute-start.6 = (f32[2,40,128]{2,1,0:T(8,128)S(1)}, f32[2,40,128]{2,1,0:T(8,128)S(1)}, u32[]{:S(2)}, u32[]{:S(2)}) collective-permute-start(f32[2,40,128]{2,1,0:T(8,128)S(1)} %pad_maximum_fusion.2), channel_id=1, source_target_pairs={{0,4},{1,5},{2,6},{3,7},{4,0},{5,1},{6,2},{7,3},{8,12},{9,13},{10,... | collective-permute-start | bytes 122888 | tf_op jit(solution)/shard_map/ppermute | solution.py:415
  20.1 1.7 %collective-permute-start.10 = (f32[2048,128]{1,0:T(8,128)}, f32[2048,128]{1,0:T(8,128)}, u32[]{:S(2)}, u32[]{:S(2)}) collective-permute-start(f32[2048,128]{1,0:T(8,128)} %refs_1_.1), channel_id=1, source_target_pairs={{6,8},{8,6},{14,16},{16,14},{22,24},{24,22},{7,9},{9,7},{15,17},{1... | collective-permute-start | bytes 3145736 | tf_op jit(solution)/shard_map/ppermute | solution.py:439
  21.8 0.3 collective-permute-done.6
  22.1 1.7 %collective-permute-start.9 = (f32[2,40,128]{2,1,0:T(8,128)S(1)}, f32[2,40,128]{2,1,0:T(8,128)S(1)}, u32[]{:S(2)}, u32[]{:S(2)}) collective-permute-start(f32[2,40,128]{2,1,0:T(8,128)S(1)} %pad_maximum_fusion.3), channel_id=1, source_target_pairs={{0,3},{1,2},{2,1},{3,0},{4,7},{5,6},{6,5},{7,4},{8,11},{9,10},{10,... | collective-permute-start | bytes 122888 | tf_op jit(solution)/shard_map/ppermute | solution.py:415
  23.8 0.4 collective-permute-start.8
  24.2 0.0 copy-done.3
  24.2 0.1 copy.7.cols_hbm
  24.3 0.1 collective-permute-start.7
  24.4 1.3 %collective-permute-done.9 = f32[2,40,128]{2,1,0:T(8,128)S(1)} collective-permute-done((f32[2,40,128]{2,1,0:T(8,128)S(1)}, f32[2,40,128]{2,1,0:T(8,128)S(1)}, u32[]{:S(2)}, u32[]{:S(2)}) %collective-permute-start.9) | collective-permute-done | bytes 40992 | tf_op jit(solution)/shard_map/ppermute | solution.py:415
  25.8 0.0 collective-permute-done.8
  25.8 2.5 %collective-permute-done.7 = f32[2,40,128]{2,1,0:T(8,128)S(1)} collective-permute-done((f32[2,40,128]{2,1,0:T(8,128)S(1)}, f32[2,40,128]{2,1,0:T(8,128)S(1)}, u32[]{:S(2)}, u32[]{:S(2)}) %collective-permute-start.7) | collective-permute-done | bytes 40992 | tf_op jit(solution)/shard_map/ppermute | solution.py:415
  28.3 0.0 copy-done.1
  28.4 7.8 %factors_and_chip_modes.1 = (f32[128,128]{1,0:T(8,128)}, bf16[256,256]{1,0:T(8,128)(2,1)S(1)}, bf16[256,128]{1,0:T(8,128)(2,1)S(1)}, f32[2048,128]{1,0:T(8,128)S...) custom-call(f32[2,80,128]{2,1,0:T(8,128)S(1)} %pad_maximum_fusion.refs_0_, ...), custom_call_target="tpu_custom_call" | custom-call | tf_op jit(solution)/shard_map/factors_and_chip_modes/pallas_call | solution.py:305
  36.2 0.0 collective-permute-done.10.outer_ref
  36.2 0.0 copy-done.2
  36.2 3.4 %apply_and_project.1 = (f32[2048,128]{1,0:T(8,128)}, bf16[2048,128]{1,0:T(8,128)(2,1)S(1)}, f32[128,128]{1,0:T(8,128)S(1)}) custom-call(s32[16,4]{1,0:T(8,128)S(1)} %copy.7.cols_hbm, f32[2048,128]{1,0:T(8,128)S(1)} %get-tuple-element.21.modes_ref, bf16[2048,128]{1,0:T(8,128)(2,1)S(1)} %get-tuple-element.22.low_ref, ...), custom_call_target="tpu_custom_call" | custom-call | tf_op jit(solution)/shard_map/apply_and_project/pallas_call | solution.py:381
  39.6 0.1 collective-permute-start.11
  39.7 1.2 %collective-permute-done.11 = f32[128,128]{1,0:T(8,128)S(1)} collective-permute-done((f32[128,128]{1,0:T(8,128)S(1)}, f32[128,128]{1,0:T(8,128)S(1)}, u32[]{:S(2)}, u32[]{:S(2)}) %collective-permute-start.11) | collective-permute-done | bytes 65568 | tf_op jit(solution)/shard_map/ppermute | solution.py:415
  41.0 2.6 %collective-permute-start.14 = (f32[128,128]{1,0:T(8,128)S(1)}, f32[128,128]{1,0:T(8,128)S(1)}, u32[]{:S(2)}, u32[]{:S(2)}) collective-permute-start(f32[128,128]{1,0:T(8,128)S(1)} %add.246), channel_id=1, source_target_pairs={{0,5},{1,4},{2,7},{3,6},{4,1},{5,0},{6,3},{7,2},{8,13},{9,12},{10,... | collective-permute-start | bytes 196616 | tf_op jit(solution)/shard_map/ppermute | solution.py:415
  43.6 0.0 collective-permute-start.13
  43.6 1.1 %collective-permute-start.12 = (f32[128,128]{1,0:T(8,128)S(1)}, f32[128,128]{1,0:T(8,128)S(1)}, u32[]{:S(2)}, u32[]{:S(2)}) collective-permute-start(f32[128,128]{1,0:T(8,128)S(1)} %add.246), channel_id=1, source_target_pairs={{0,1},{1,0},{2,3},{3,2},{4,5},{5,4},{6,7},{7,6},{8,9},{9,8},{10,11... | collective-permute-start | bytes 196616 | tf_op jit(solution)/shard_map/ppermute | solution.py:415
  44.7 1.5 %collective-permute-done.14 = f32[128,128]{1,0:T(8,128)S(1)} collective-permute-done((f32[128,128]{1,0:T(8,128)S(1)}, f32[128,128]{1,0:T(8,128)S(1)}, u32[]{:S(2)}, u32[]{:S(2)}) %collective-permute-start.14) | collective-permute-done | bytes 65568 | tf_op jit(solution)/shard_map/ppermute | solution.py:415
  46.2 1.6 %collective-permute-done.13 = f32[128,128]{1,0:T(8,128)S(1)} collective-permute-done((f32[128,128]{1,0:T(8,128)S(1)}, f32[128,128]{1,0:T(8,128)S(1)}, u32[]{:S(2)}, u32[]{:S(2)}) %collective-permute-start.13) | collective-permute-done | bytes 65568 | tf_op jit(solution)/shard_map/ppermute | solution.py:415
  47.8 0.0 collective-permute-done.12
  47.9 5.3 %collective-permute-start.17 = (f32[128,128]{1,0:T(8,128)S(1)}, f32[128,128]{1,0:T(8,128)S(1)}, u32[]{:S(2)}, u32[]{:S(2)}) collective-permute-start(f32[128,128]{1,0:T(8,128)S(1)} %add_add_fusion), channel_id=1, source_target_pairs={{0,24},{1,25},{2,26},{3,27},{4,28},{5,29},{6,30},{7,31},{8,16},{9,... | collective-permute-start | bytes 196616 | tf_op jit(solution)/shard_map/ppermute | solution.py:415
  53.2 0.0 collective-permute-start.16
  53.2 0.6 %collective-permute-start.15 = (f32[128,128]{1,0:T(8,128)S(1)}, f32[128,128]{1,0:T(8,128)S(1)}, u32[]{:S(2)}, u32[]{:S(2)}) collective-permute-start(f32[128,128]{1,0:T(8,128)S(1)} %add_add_fusion), channel_id=1, source_target_pairs={{0,8},{1,9},{2,10},{3,11},{4,12},{5,13},{6,14},{7,15},{8,0},{9,1},... | collective-permute-start | bytes 196616 | tf_op jit(solution)/shard_map/ppermute | solution.py:415
  53.8 0.8 %copy.8 = bf16[2048,128]{1,0:T(8,128)(2,1)} copy(bf16[2048,128]{1,0:T(8,128)(2,1)S(1)} %get-tuple-element.50) | data formatting | bytes 1048576
  54.6 1.4 %collective-permute-done.17 = f32[128,128]{1,0:T(8,128)S(1)} collective-permute-done((f32[128,128]{1,0:T(8,128)S(1)}, f32[128,128]{1,0:T(8,128)S(1)}, u32[]{:S(2)}, u32[]{:S(2)}) %collective-permute-start.17) | collective-permute-done | bytes 65568 | tf_op jit(solution)/shard_map/ppermute | solution.py:415
  56.0 2.5 %collective-permute-done.16 = f32[128,128]{1,0:T(8,128)S(1)} collective-permute-done((f32[128,128]{1,0:T(8,128)S(1)}, f32[128,128]{1,0:T(8,128)S(1)}, u32[]{:S(2)}, u32[]{:S(2)}) %collective-permute-start.16) | collective-permute-done | bytes 65568 | tf_op jit(solution)/shard_map/ppermute | solution.py:415
  58.5 0.0 collective-permute-done.15
  58.5 0.6 %add_multiply_fusion = f32[128,128]{1,0:T(8,128)} fusion(f32[128,128]{1,0:T(8,128)S(1)} %collective-permute-done.16, f32[128,128]{1,0:T(8,128)S(1)} %collective-permute-done.17, f32[128,128]{1,0:T(8,128)S(1)} %add_add_fusion, f32[128,128]{1,0:T(8,128)S(1)} %collective-permute-done.15), kind=kLoop, calls=%fused_computation.1 | loop fusion | flops 65536 | bytes 327680 | tf_op jit(solution)/shard_map/div | solution.py:448
  (16 shorter events, 0.2 us)
Async XLA Ops:
  0.6 23.6 %copy-start.3 = (s32[16,4]{0,1:T(4,128)S(1)}, s32[16,4]{0,1:T(4,128)}, u32[]{:S(2)}) copy-start(s32[16,4]{0,1:T(4,128)} %param.5) | copy-start | bytes 772
  0.6 8.6 %collective-permute-start.1 = (f32[2048,128]{1,0:T(8,128)}, f32[2048,128]{1,0:T(8,128)}, u32[]{:S(2)}, u32[]{:S(2)}) collective-permute-start(f32[2048,128]{1,0:T(8,128)} %refs_1_.1), channel_id=1, source_target_pairs={{0,2},{1,3},{2,0},{3,1},{4,6},{5,7},{6,4},{7,5},{8,10},{9,11},{10,... | collective-permute-start | bytes 3145736 | tf_op jit(solution)/shard_map/ppermute | solution.py:415
  1.2 16.6 %collective-permute-start.5 = (f32[2048,128]{1,0:T(8,128)}, f32[2048,128]{1,0:T(8,128)}, u32[]{:S(2)}, u32[]{:S(2)}) collective-permute-start(f32[2048,128]{1,0:T(8,128)} %refs_1_.1), channel_id=1, source_target_pairs={{2,4},{4,2},{10,12},{12,10},{18,20},{20,18},{26,28},{28,26},{3,5},... | collective-permute-start | bytes 3145736 | tf_op jit(solution)/shard_map/ppermute | solution.py:429
  2.8 1.2 %copy-start = (f32[2048,128]{1,0:T(8,128)S(1)}, f32[2048,128]{1,0:T(8,128)}, u32[]{:S(2)}) copy-start(f32[2048,128]{1,0:T(8,128)} %refs_1_.1) | copy-start | bytes 3145732
  4.0 24.3 %copy-start.1 = (f32[2048,128]{1,0:T(8,128)S(1)}, f32[2048,128]{1,0:T(8,128)}, u32[]{:S(2)}) copy-start(f32[2048,128]{1,0:T(8,128)} %refs_1_.1) | copy-start | bytes 3145732
  5.3 30.9 %copy-start.2 = (bf16[16,4,128,128]{3,2,1,0:T(8,128)(2,1)S(1)}, bf16[16,4,128,128]{3,2,1,0:T(8,128)(2,1)}, u32[]{:S(2)}) copy-start(bf16[16,4,128,128]{3,2,1,0:T(8,128)(2,1)} %jb_ref.1) | copy-start | bytes 6291460
  5.3 3.9 %collective-permute-start = (f32[2,40,128]{2,1,0:T(8,128)S(1)}, f32[2,40,128]{2,1,0:T(8,128)S(1)}, u32[]{:S(2)}, u32[]{:S(2)}) collective-permute-start(f32[2,40,128]{2,1,0:T(8,128)S(1)} %get-tuple-element.47), channel_id=1, source_target_pairs={{0,2},{1,3},{2,0},{3,1},{4,6},{5,7},{6,4},{7,5},{8,10},{9,11},{10,... | collective-permute-start | bytes 122888 | tf_op jit(solution)/shard_map/ppermute | solution.py:415
  9.2 5.0 %collective-permute-start.3 = (f32[2,40,128]{2,1,0:T(8,128)S(1)}, f32[2,40,128]{2,1,0:T(8,128)S(1)}, u32[]{:S(2)}, u32[]{:S(2)}) collective-permute-start(f32[2,40,128]{2,1,0:T(8,128)S(1)} %pad_maximum_fusion.1), channel_id=1, source_target_pairs={{0,16},{1,17},{2,18},{3,19},{4,20},{5,21},{6,22},{7,23},{8,24},{9,... | collective-permute-start | bytes 122888 | tf_op jit(solution)/shard_map/ppermute | solution.py:415
  11.9 5.8 %collective-permute-start.4 = (f32[2,40,128]{2,1,0:T(8,128)S(1)}, f32[2,40,128]{2,1,0:T(8,128)S(1)}, u32[]{:S(2)}, u32[]{:S(2)}) collective-permute-start(f32[2,40,128]{2,1,0:T(8,128)S(1)} %pad_maximum_fusion.1), channel_id=1, source_target_pairs={{0,24},{1,25},{2,26},{3,27},{4,28},{5,29},{6,30},{7,31},{8,16},{9,... | collective-permute-start | bytes 122888 | tf_op jit(solution)/shard_map/ppermute | solution.py:415
  13.2 4.5 %collective-permute-start.2 = (f32[2,40,128]{2,1,0:T(8,128)S(1)}, f32[2,40,128]{2,1,0:T(8,128)S(1)}, u32[]{:S(2)}, u32[]{:S(2)}) collective-permute-start(f32[2,40,128]{2,1,0:T(8,128)S(1)} %pad_maximum_fusion.1), channel_id=1, source_target_pairs={{0,8},{1,9},{2,10},{3,11},{4,12},{5,13},{6,14},{7,15},{8,0},{9,1},... | collective-permute-start | bytes 122888 | tf_op jit(solution)/shard_map/ppermute | solution.py:415
  17.7 4.3 %collective-permute-start.6 = (f32[2,40,128]{2,1,0:T(8,128)S(1)}, f32[2,40,128]{2,1,0:T(8,128)S(1)}, u32[]{:S(2)}, u32[]{:S(2)}) collective-permute-start(f32[2,40,128]{2,1,0:T(8,128)S(1)} %pad_maximum_fusion.2), channel_id=1, source_target_pairs={{0,4},{1,5},{2,6},{3,7},{4,0},{5,1},{6,2},{7,3},{8,12},{9,13},{10,... | collective-permute-start | bytes 122888 | tf_op jit(solution)/shard_map/ppermute | solution.py:415
  20.1 16.1 %collective-permute-start.10 = (f32[2048,128]{1,0:T(8,128)}, f32[2048,128]{1,0:T(8,128)}, u32[]{:S(2)}, u32[]{:S(2)}) collective-permute-start(f32[2048,128]{1,0:T(8,128)} %refs_1_.1), channel_id=1, source_target_pairs={{6,8},{8,6},{14,16},{16,14},{22,24},{24,22},{7,9},{9,7},{15,17},{1... | collective-permute-start | bytes 3145736 | tf_op jit(solution)/shard_map/ppermute | solution.py:439
  22.1 3.7 %collective-permute-start.9 = (f32[2,40,128]{2,1,0:T(8,128)S(1)}, f32[2,40,128]{2,1,0:T(8,128)S(1)}, u32[]{:S(2)}, u32[]{:S(2)}) collective-permute-start(f32[2,40,128]{2,1,0:T(8,128)S(1)} %pad_maximum_fusion.3), channel_id=1, source_target_pairs={{0,3},{1,2},{2,1},{3,0},{4,7},{5,6},{6,5},{7,4},{8,11},{9,10},{10,... | collective-permute-start | bytes 122888 | tf_op jit(solution)/shard_map/ppermute | solution.py:415
  23.8 2.0 %collective-permute-start.8 = (f32[2,40,128]{2,1,0:T(8,128)S(1)}, f32[2,40,128]{2,1,0:T(8,128)S(1)}, u32[]{:S(2)}, u32[]{:S(2)}) collective-permute-start(f32[2,40,128]{2,1,0:T(8,128)S(1)} %pad_maximum_fusion.3), channel_id=1, source_target_pairs={{0,2},{1,3},{2,0},{3,1},{4,6},{5,7},{6,4},{7,5},{8,10},{9,11},{10,... | collective-permute-start | bytes 122888 | tf_op jit(solution)/shard_map/ppermute | solution.py:415
  24.3 4.0 %collective-permute-start.7 = (f32[2,40,128]{2,1,0:T(8,128)S(1)}, f32[2,40,128]{2,1,0:T(8,128)S(1)}, u32[]{:S(2)}, u32[]{:S(2)}) collective-permute-start(f32[2,40,128]{2,1,0:T(8,128)S(1)} %pad_maximum_fusion.3), channel_id=1, source_target_pairs={{0,1},{1,0},{2,3},{3,2},{4,5},{5,4},{6,7},{7,6},{8,9},{9,8},{10,11... | collective-permute-start | bytes 122888 | tf_op jit(solution)/shard_map/ppermute | solution.py:415
  39.6 1.3 %collective-permute-start.11 = (f32[128,128]{1,0:T(8,128)S(1)}, f32[128,128]{1,0:T(8,128)S(1)}, u32[]{:S(2)}, u32[]{:S(2)}) collective-permute-start(f32[128,128]{1,0:T(8,128)S(1)} %get-tuple-element.31), channel_id=1, source_target_pairs={{0,2},{1,3},{2,0},{3,1},{4,6},{5,7},{6,4},{7,5},{8,10},{9,11},{10,... | collective-permute-start | bytes 196616 | tf_op jit(solution)/shard_map/ppermute | solution.py:415
  41.0 5.2 %collective-permute-start.14 = (f32[128,128]{1,0:T(8,128)S(1)}, f32[128,128]{1,0:T(8,128)S(1)}, u32[]{:S(2)}, u32[]{:S(2)}) collective-permute-start(f32[128,128]{1,0:T(8,128)S(1)} %add.246), channel_id=1, source_target_pairs={{0,5},{1,4},{2,7},{3,6},{4,1},{5,0},{6,3},{7,2},{8,13},{9,12},{10,... | collective-permute-start | bytes 196616 | tf_op jit(solution)/shard_map/ppermute | solution.py:415
  43.6 4.3 %collective-permute-start.13 = (f32[128,128]{1,0:T(8,128)S(1)}, f32[128,128]{1,0:T(8,128)S(1)}, u32[]{:S(2)}, u32[]{:S(2)}) collective-permute-start(f32[128,128]{1,0:T(8,128)S(1)} %add.246), channel_id=1, source_target_pairs={{0,4},{1,5},{2,6},{3,7},{4,0},{5,1},{6,2},{7,3},{8,12},{9,13},{10,... | collective-permute-start | bytes 196616 | tf_op jit(solution)/shard_map/ppermute | solution.py:415
  43.6 4.3 %collective-permute-start.12 = (f32[128,128]{1,0:T(8,128)S(1)}, f32[128,128]{1,0:T(8,128)S(1)}, u32[]{:S(2)}, u32[]{:S(2)}) collective-permute-start(f32[128,128]{1,0:T(8,128)S(1)} %add.246), channel_id=1, source_target_pairs={{0,1},{1,0},{2,3},{3,2},{4,5},{5,4},{6,7},{7,6},{8,9},{9,8},{10,11... | collective-permute-start | bytes 196616 | tf_op jit(solution)/shard_map/ppermute | solution.py:415
  47.9 8.1 %collective-permute-start.17 = (f32[128,128]{1,0:T(8,128)S(1)}, f32[128,128]{1,0:T(8,128)S(1)}, u32[]{:S(2)}, u32[]{:S(2)}) collective-permute-start(f32[128,128]{1,0:T(8,128)S(1)} %add_add_fusion), channel_id=1, source_target_pairs={{0,24},{1,25},{2,26},{3,27},{4,28},{5,29},{6,30},{7,31},{8,16},{9,... | collective-permute-start | bytes 196616 | tf_op jit(solution)/shard_map/ppermute | solution.py:415
  53.2 5.3 %collective-permute-start.16 = (f32[128,128]{1,0:T(8,128)S(1)}, f32[128,128]{1,0:T(8,128)S(1)}, u32[]{:S(2)}, u32[]{:S(2)}) collective-permute-start(f32[128,128]{1,0:T(8,128)S(1)} %add_add_fusion), channel_id=1, source_target_pairs={{0,16},{1,17},{2,18},{3,19},{4,20},{5,21},{6,22},{7,23},{8,24},{9,... | collective-permute-start | bytes 196616 | tf_op jit(solution)/shard_map/ppermute | solution.py:415
  53.2 5.3 %collective-permute-start.15 = (f32[128,128]{1,0:T(8,128)S(1)}, f32[128,128]{1,0:T(8,128)S(1)}, u32[]{:S(2)}, u32[]{:S(2)}) collective-permute-start(f32[128,128]{1,0:T(8,128)S(1)} %add_add_fusion), channel_id=1, source_target_pairs={{0,8},{1,9},{2,10},{3,11},{4,12},{5,13},{6,14},{7,15},{8,0},{9,1},... | collective-permute-start | bytes 196616 | tf_op jit(solution)/shard_map/ppermute | solution.py:415

commit v8 on v6

--- a/solution.py
+++ b/solution.py
@@ -402,9 +402,9 @@
         rows_total = snapshots.shape[0] * count
         even = lax.axis_index("bulk") % 2 == 0
         pairs = lambda first: [p for i in range(first, n_bulk - 1, 4) for p in ((i, i + 1), (i + 1, i))]
-        chip = swap(snapshots, core_mask)
         inner = lax.ppermute(snapshots, "bulk", pairs(1))
-        gram = local_gram(snapshots)
+        gram, early = lax.optimization_barrier((local_gram(snapshots), snapshots))
+        chip = swap(early, core_mask)
         half = gram.shape[1] // 2
         upper, lower = gram[:, :half], gram[:, half:]
         mine = add_pairs(jnp.where(even, upper, lower), swap(jnp.where(even, lower, upper), core_mask))

time: 59.2 us -> 61.7 us (1.042)
  starting transfers between devices: 23.2 us -> 25.6 us
  local copies, waits for them, and re-layouts: 2.11 us -> 0.89 us
  Pallas kernels: 12.4 us -> 13.5 us
    ppermute x16, starting transfers between devices: 20 us -> 22.3 us  [swap(): return lax.ppermute(value, axes, [(i, i ^ mask) for i in range(count)])]
    unnamed x10 -> x6, local copies, waits for them, and re-layouts: 2.11 us -> 0.89 us
    pallas_call x1, Pallas kernels: 1.18 us -> 2.25 us  [local_gram(): pl.pallas_call(gram_kernel, in_specs=[pl.BlockSpec(memory_space=pl.ANY)],...]
  transfers between devices with their start and end apart: 18 -> 18, of which waited for: 12 -> 13; matrix products, arithmetic and copies ran while one was open for 2% -> 2% of each run, Pallas kernels for 15% -> 13%
where the time goes in v8:
time: 61.7 us; the launch traced here: 61.5 us
  starting transfers between devices  25.6 us (41%)
  waiting for transfers between devices  19.8 us (32%)
  Pallas kernels  13.5 us (22%)
  local copies, waits for them, and re-layouts  0.89 us (1%)
  other arithmetic  0.87 us (1%)
  between operations  0.79 us (1%)
    ppermute x16, starting transfers between devices, swap(): return lax.ppermute(value, axes, [(i, i ^ mask) for i in range(count)])  22.3 us
    ppermute x16, waiting for transfers between devices, swap(): return lax.ppermute(value, axes, [(i, i ^ mask) for i in range(count)])  19.8 us
    pallas_call x1, Pallas kernels, factors_and_chip_modes(): pl.pallas_call(lambda *refs: factors_kernel(count, *refs), in_specs=[vmem...  7.85 us
    pallas_call x1, Pallas kernels, apply_and_project(): pl.pallas_call(apply_kernel, in_specs=[hbm] + [vmem] * 8, out_specs=(hbm,...  3.43 us
    pallas_call x1, Pallas kernels, local_gram(): pl.pallas_call(gram_kernel, in_specs=[pl.BlockSpec(memory_space=pl.ANY)],...  2.25 us
    ppermute x1, starting transfers between devices, shards(): inner = lax.ppermute(snapshots, 'bulk', pairs(1))  1.65 us
    ppermute x1, starting transfers between devices, shards(): outer = lax.ppermute(late, 'bulk', pairs(3))  1.61 us
  transfers between devices with their start and end apart: 18, of which 13 were waited for; matrix products, arithmetic and copies ran while one was open for 2% of the time, Pallas kernels for 13%

profile of v8, /device:TPU:0, one launch (start us, length us, event | category | flops | bytes accessed | tf_op | source)
XLA Modules:
  0.0 61.5 jit_solution(13242566594062309417)
XLA Ops:
  0.6 0.0 copy-start.1
  0.6 2.2 %local_gram.1 = f32[2,128,128]{2,1,0:T(8,128)S(1)} custom-call(f32[2048,128]{1,0:T(8,128)} %refs_1_.1), custom_call_target="tpu_custom_call" | custom-call | tf_op jit(solution)/shard_map/local_gram/pallas_call | solution.py:120
  2.9 0.5 collective-permute-start.1
  3.4 1.6 %collective-permute-start.5 = (f32[2048,128]{1,0:T(8,128)}, f32[2048,128]{1,0:T(8,128)}, u32[]{:S(2)}, u32[]{:S(2)}) collective-permute-start(f32[2048,128]{1,0:T(8,128)} %refs_1_.1), channel_id=1, source_target_pairs={{2,4},{4,2},{10,12},{12,10},{18,20},{20,18},{26,28},{28,26},{3,5},... | collective-permute-start | bytes 3145736 | tf_op jit(solution)/shard_map/ppermute | solution.py:405
  5.1 3.0 %collective-permute-start = (f32[2,64,128]{2,1,0:T(8,128)S(1)}, f32[2,64,128]{2,1,0:T(8,128)S(1)}, u32[]{:S(2)}, u32[]{:S(2)}) collective-permute-start(f32[2,64,128]{2,1,0:T(8,128)S(1)} %get-tuple-element.51), channel_id=1, source_target_pairs={{0,2},{1,3},{2,0},{3,1},{4,6},{5,7},{6,4},{7,5},{8,10},{9,11},{10,... | collective-permute-start | bytes 196616 | tf_op jit(solution)/shard_map/ppermute | solution.py:392
  8.0 0.9 %collective-permute-done = f32[2,64,128]{2,1,0:T(8,128)S(1)} collective-permute-done((f32[2,64,128]{2,1,0:T(8,128)S(1)}, f32[2,64,128]{2,1,0:T(8,128)S(1)}, u32[]{:S(2)}, u32[]{:S(2)}) %collective-permute-start) | collective-permute-done | bytes 65568 | tf_op jit(solution)/shard_map/ppermute | solution.py:392
  9.0 0.0 copy-start
  9.0 0.0 collective-permute-done.1.refs_2_
  9.0 2.7 %collective-permute-start.3 = (f32[2,64,128]{2,1,0:T(8,128)S(1)}, f32[2,64,128]{2,1,0:T(8,128)S(1)}, u32[]{:S(2)}, u32[]{:S(2)}) collective-permute-start(f32[2,64,128]{2,1,0:T(8,128)S(1)} %pad_maximum_fusion.1), channel_id=1, source_target_pairs={{0,16},{1,17},{2,18},{3,19},{4,20},{5,21},{6,22},{7,23},{8,24},{9,... | collective-permute-start | bytes 196616 | tf_op jit(solution)/shard_map/ppermute | solution.py:392
  11.7 1.4 %collective-permute-start.4 = (f32[2,64,128]{2,1,0:T(8,128)S(1)}, f32[2,64,128]{2,1,0:T(8,128)S(1)}, u32[]{:S(2)}, u32[]{:S(2)}) collective-permute-start(f32[2,64,128]{2,1,0:T(8,128)S(1)} %pad_maximum_fusion.1), channel_id=1, source_target_pairs={{0,24},{1,25},{2,26},{3,27},{4,28},{5,29},{6,30},{7,31},{8,16},{9,... | collective-permute-start | bytes 196616 | tf_op jit(solution)/shard_map/ppermute | solution.py:392
  13.0 0.2 collective-permute-start.2
  13.2 2.7 %collective-permute-done.3 = f32[2,64,128]{2,1,0:T(8,128)S(1)} collective-permute-done((f32[2,64,128]{2,1,0:T(8,128)S(1)}, f32[2,64,128]{2,1,0:T(8,128)S(1)}, u32[]{:S(2)}, u32[]{:S(2)}) %collective-permute-start.3) | collective-permute-done | bytes 65568 | tf_op jit(solution)/shard_map/ppermute | solution.py:392
  16.0 2.3 %collective-permute-done.4 = f32[2,64,128]{2,1,0:T(8,128)S(1)} collective-permute-done((f32[2,64,128]{2,1,0:T(8,128)S(1)}, f32[2,64,128]{2,1,0:T(8,128)S(1)}, u32[]{:S(2)}, u32[]{:S(2)}) %collective-permute-start.4) | collective-permute-done | bytes 65568 | tf_op jit(solution)/shard_map/ppermute | solution.py:392
  18.3 0.3 collective-permute-done.2
  18.6 0.0 collective-permute-done.5.inner_ref
  18.6 3.7 %collective-permute-start.6 = (f32[2,64,128]{2,1,0:T(8,128)S(1)}, f32[2,64,128]{2,1,0:T(8,128)S(1)}, u32[]{:S(2)}, u32[]{:S(2)}) collective-permute-start(f32[2,64,128]{2,1,0:T(8,128)S(1)} %pad_maximum_fusion.2), channel_id=1, source_target_pairs={{0,4},{1,5},{2,6},{3,7},{4,0},{5,1},{6,2},{7,3},{8,12},{9,13},{10,... | collective-permute-start | bytes 196616 | tf_op jit(solution)/shard_map/ppermute | solution.py:392
  22.4 1.6 %collective-permute-start.10 = (f32[2048,128]{1,0:T(8,128)}, f32[2048,128]{1,0:T(8,128)}, u32[]{:S(2)}, u32[]{:S(2)}) collective-permute-start(f32[2048,128]{1,0:T(8,128)} %refs_1_.1), channel_id=1, source_target_pairs={{6,8},{8,6},{14,16},{16,14},{22,24},{24,22},{7,9},{9,7},{15,17},{1... | collective-permute-start | bytes 3145736 | tf_op jit(solution)/shard_map/ppermute | solution.py:416
  24.0 0.8 %collective-permute-done.6 = f32[2,64,128]{2,1,0:T(8,128)S(1)} collective-permute-done((f32[2,64,128]{2,1,0:T(8,128)S(1)}, f32[2,64,128]{2,1,0:T(8,128)S(1)}, u32[]{:S(2)}, u32[]{:S(2)}) %collective-permute-start.6) | collective-permute-done | bytes 65568 | tf_op jit(solution)/shard_map/ppermute | solution.py:392
  24.8 1.8 %collective-permute-start.9 = (f32[2,64,128]{2,1,0:T(8,128)S(1)}, f32[2,64,128]{2,1,0:T(8,128)S(1)}, u32[]{:S(2)}, u32[]{:S(2)}) collective-permute-start(f32[2,64,128]{2,1,0:T(8,128)S(1)} %pad_maximum_fusion.3), channel_id=1, source_target_pairs={{0,3},{1,2},{2,1},{3,0},{4,7},{5,6},{6,5},{7,4},{8,11},{9,10},{10,... | collective-permute-start | bytes 196616 | tf_op jit(solution)/shard_map/ppermute | solution.py:392
  26.6 0.4 collective-permute-start.8
  27.0 0.0 copy-done.1
  27.0 0.1 copy.7.cols_hbm
  27.1 0.1 collective-permute-start.7
  27.2 1.9 %collective-permute-done.9 = f32[2,64,128]{2,1,0:T(8,128)S(1)} collective-permute-done((f32[2,64,128]{2,1,0:T(8,128)S(1)}, f32[2,64,128]{2,1,0:T(8,128)S(1)}, u32[]{:S(2)}, u32[]{:S(2)}) %collective-permute-start.9) | collective-permute-done | bytes 65568 | tf_op jit(solution)/shard_map/ppermute | solution.py:392
  29.1 0.0 collective-permute-done.8
  29.1 2.2 %collective-permute-done.7 = f32[2,64,128]{2,1,0:T(8,128)S(1)} collective-permute-done((f32[2,64,128]{2,1,0:T(8,128)S(1)}, f32[2,64,128]{2,1,0:T(8,128)S(1)}, u32[]{:S(2)}, u32[]{:S(2)}) %collective-permute-start.7) | collective-permute-done | bytes 65568 | tf_op jit(solution)/shard_map/ppermute | solution.py:392
  31.4 7.8 %factors_and_chip_modes.1 = (f32[128,128]{1,0:T(8,128)}, bf16[256,256]{1,0:T(8,128)(2,1)S(1)}, bf16[256,128]{1,0:T(8,128)(2,1)S(1)}, f32[2048,128]{1,0:T(8,128)S...) custom-call(f32[2,128,128]{2,1,0:T(8,128)S(1)} %pad_maximum_fusion.refs_0_, f32[2048,128]{1,0:T(8,128)} %refs_1_.1, ...), custom_call_target="tpu_custom_call" | custom-call | tf_op jit(solution)/shard_map/factors_and_chip_modes/pallas_call | solution.py:282
  39.3 0.0 collective-permute-done.10.outer_ref
  39.3 0.0 copy-done
  39.3 3.4 %apply_and_project.1 = (f32[2048,128]{1,0:T(8,128)}, bf16[2048,128]{1,0:T(8,128)(2,1)S(1)}, f32[128,128]{1,0:T(8,128)S(1)}) custom-call(s32[16,4]{1,0:T(8,128)S(1)} %copy.7.cols_hbm, f32[2048,128]{1,0:T(8,128)S(1)} %get-tuple-element.25.modes_ref, bf16[2048,128]{1,0:T(8,128)(2,1)S(1)} %get-tuple-element.26.low_ref, ...), custom_call_target="tpu_custom_call" | custom-call | tf_op jit(solution)/shard_map/apply_and_project/pallas_call | solution.py:358
  42.7 0.1 collective-permute-start.11
  42.8 1.2 %collective-permute-done.11 = f32[128,128]{1,0:T(8,128)S(1)} collective-permute-done((f32[128,128]{1,0:T(8,128)S(1)}, f32[128,128]{1,0:T(8,128)S(1)}, u32[]{:S(2)}, u32[]{:S(2)}) %collective-permute-start.11) | collective-permute-done | bytes 65568 | tf_op jit(solution)/shard_map/ppermute | solution.py:392
  44.1 2.5 %collective-permute-start.14 = (f32[128,128]{1,0:T(8,128)S(1)}, f32[128,128]{1,0:T(8,128)S(1)}, u32[]{:S(2)}, u32[]{:S(2)}) collective-permute-start(f32[128,128]{1,0:T(8,128)S(1)} %add.246), channel_id=1, source_target_pairs={{0,5},{1,4},{2,7},{3,6},{4,1},{5,0},{6,3},{7,2},{8,13},{9,12},{10,... | collective-permute-start | bytes 196616 | tf_op jit(solution)/shard_map/ppermute | solution.py:392
  46.5 0.4 collective-permute-start.13
  46.9 0.7 %collective-permute-start.12 = (f32[128,128]{1,0:T(8,128)S(1)}, f32[128,128]{1,0:T(8,128)S(1)}, u32[]{:S(2)}, u32[]{:S(2)}) collective-permute-start(f32[128,128]{1,0:T(8,128)S(1)} %add.246), channel_id=1, source_target_pairs={{0,1},{1,0},{2,3},{3,2},{4,5},{5,4},{6,7},{7,6},{8,9},{9,8},{10,11... | collective-permute-start | bytes 196616 | tf_op jit(solution)/shard_map/ppermute | solution.py:392
  47.6 1.7 %collective-permute-done.14 = f32[128,128]{1,0:T(8,128)S(1)} collective-permute-done((f32[128,128]{1,0:T(8,128)S(1)}, f32[128,128]{1,0:T(8,128)S(1)}, u32[]{:S(2)}, u32[]{:S(2)}) %collective-permute-start.14) | collective-permute-done | bytes 65568 | tf_op jit(solution)/shard_map/ppermute | solution.py:392
  49.3 1.5 %collective-permute-done.13 = f32[128,128]{1,0:T(8,128)S(1)} collective-permute-done((f32[128,128]{1,0:T(8,128)S(1)}, f32[128,128]{1,0:T(8,128)S(1)}, u32[]{:S(2)}, u32[]{:S(2)}) %collective-permute-start.13) | collective-permute-done | bytes 65568 | tf_op jit(solution)/shard_map/ppermute | solution.py:392
  50.8 0.4 collective-permute-done.12
  51.2 4.3 %collective-permute-start.17 = (f32[128,128]{1,0:T(8,128)S(1)}, f32[128,128]{1,0:T(8,128)S(1)}, u32[]{:S(2)}, u32[]{:S(2)}) collective-permute-start(f32[128,128]{1,0:T(8,128)S(1)} %add_add_fusion), channel_id=1, source_target_pairs={{0,24},{1,25},{2,26},{3,27},{4,28},{5,29},{6,30},{7,31},{8,16},{9,... | collective-permute-start | bytes 196616 | tf_op jit(solution)/shard_map/ppermute | solution.py:392
  55.5 0.0 collective-permute-start.16
  55.5 0.6 %collective-permute-start.15 = (f32[128,128]{1,0:T(8,128)S(1)}, f32[128,128]{1,0:T(8,128)S(1)}, u32[]{:S(2)}, u32[]{:S(2)}) collective-permute-start(f32[128,128]{1,0:T(8,128)S(1)} %add_add_fusion), channel_id=1, source_target_pairs={{0,8},{1,9},{2,10},{3,11},{4,12},{5,13},{6,14},{7,15},{8,0},{9,1},... | collective-permute-start | bytes 196616 | tf_op jit(solution)/shard_map/ppermute | solution.py:392
  56.1 0.8 %copy.8 = bf16[2048,128]{1,0:T(8,128)(2,1)} copy(bf16[2048,128]{1,0:T(8,128)(2,1)S(1)} %get-tuple-element.54) | data formatting | bytes 1048576
  56.9 1.2 %collective-permute-done.17 = f32[128,128]{1,0:T(8,128)S(1)} collective-permute-done((f32[128,128]{1,0:T(8,128)S(1)}, f32[128,128]{1,0:T(8,128)S(1)}, u32[]{:S(2)}, u32[]{:S(2)}) %collective-permute-start.17) | collective-permute-done | bytes 65568 | tf_op jit(solution)/shard_map/ppermute | solution.py:392
  58.1 2.7 %collective-permute-done.16 = f32[128,128]{1,0:T(8,128)S(1)} collective-permute-done((f32[128,128]{1,0:T(8,128)S(1)}, f32[128,128]{1,0:T(8,128)S(1)}, u32[]{:S(2)}, u32[]{:S(2)}) %collective-permute-start.16) | collective-permute-done | bytes 65568 | tf_op jit(solution)/shard_map/ppermute | solution.py:392
  60.8 0.0 collective-permute-done.15
  60.8 0.6 %add_multiply_fusion = f32[128,128]{1,0:T(8,128)} fusion(f32[128,128]{1,0:T(8,128)S(1)} %collective-permute-done.16, f32[128,128]{1,0:T(8,128)S(1)} %collective-permute-done.17, f32[128,128]{1,0:T(8,128)S(1)} %add_add_fusion, f32[128,128]{1,0:T(8,128)S(1)} %collective-permute-done.15), kind=kLoop, calls=%fused_computation.6 | loop fusion | flops 65536 | bytes 327680 | tf_op jit(solution)/shard_map/div | solution.py:425
  (14 shorter events, 0.2 us)
Async XLA Ops:
  0.6 26.4 %copy-start.1 = (s32[16,4]{0,1:T(4,128)S(1)}, s32[16,4]{0,1:T(4,128)}, u32[]{:S(2)}) copy-start(s32[16,4]{0,1:T(4,128)} %param.5) | copy-start | bytes 772
  2.9 6.1 %collective-permute-start.1 = (f32[2048,128]{1,0:T(8,128)}, f32[2048,128]{1,0:T(8,128)S(1)}, u32[]{:S(2)}, u32[]{:S(2)}) collective-permute-start(f32[2048,128]{1,0:T(8,128)} %refs_1_.1), channel_id=1, source_target_pairs={{0,2},{1,3},{2,0},{3,1},{4,6},{5,7},{6,4},{7,5},{8,10},{9,11},{10,... | collective-permute-start | bytes 3145736 | tf_op jit(solution)/shard_map/ppermute | solution.py:392
  3.4 15.2 %collective-permute-start.5 = (f32[2048,128]{1,0:T(8,128)}, f32[2048,128]{1,0:T(8,128)}, u32[]{:S(2)}, u32[]{:S(2)}) collective-permute-start(f32[2048,128]{1,0:T(8,128)} %refs_1_.1), channel_id=1, source_target_pairs={{2,4},{4,2},{10,12},{12,10},{18,20},{20,18},{26,28},{28,26},{3,5},... | collective-permute-start | bytes 3145736 | tf_op jit(solution)/shard_map/ppermute | solution.py:405
  5.1 3.9 %collective-permute-start = (f32[2,64,128]{2,1,0:T(8,128)S(1)}, f32[2,64,128]{2,1,0:T(8,128)S(1)}, u32[]{:S(2)}, u32[]{:S(2)}) collective-permute-start(f32[2,64,128]{2,1,0:T(8,128)S(1)} %get-tuple-element.51), channel_id=1, source_target_pairs={{0,2},{1,3},{2,0},{3,1},{4,6},{5,7},{6,4},{7,5},{8,10},{9,11},{10,... | collective-permute-start | bytes 196616 | tf_op jit(solution)/shard_map/ppermute | solution.py:392
  9.0 30.3 %copy-start = (bf16[16,4,128,128]{3,2,1,0:T(8,128)(2,1)S(1)}, bf16[16,4,128,128]{3,2,1,0:T(8,128)(2,1)}, u32[]{:S(2)}) copy-start(bf16[16,4,128,128]{3,2,1,0:T(8,128)(2,1)} %jb_ref.1) | copy-start | bytes 6291460
  9.0 6.9 %collective-permute-start.3 = (f32[2,64,128]{2,1,0:T(8,128)S(1)}, f32[2,64,128]{2,1,0:T(8,128)S(1)}, u32[]{:S(2)}, u32[]{:S(2)}) collective-permute-start(f32[2,64,128]{2,1,0:T(8,128)S(1)} %pad_maximum_fusion.1), channel_id=1, source_target_pairs={{0,16},{1,17},{2,18},{3,19},{4,20},{5,21},{6,22},{7,23},{8,24},{9,... | collective-permute-start | bytes 196616 | tf_op jit(solution)/shard_map/ppermute | solution.py:392
  11.7 6.6 %collective-permute-start.4 = (f32[2,64,128]{2,1,0:T(8,128)S(1)}, f32[2,64,128]{2,1,0:T(8,128)S(1)}, u32[]{:S(2)}, u32[]{:S(2)}) collective-permute-start(f32[2,64,128]{2,1,0:T(8,128)S(1)} %pad_maximum_fusion.1), channel_id=1, source_target_pairs={{0,24},{1,25},{2,26},{3,27},{4,28},{5,29},{6,30},{7,31},{8,16},{9,... | collective-permute-start | bytes 196616 | tf_op jit(solution)/shard_map/ppermute | solution.py:392
  13.0 5.5 %collective-permute-start.2 = (f32[2,64,128]{2,1,0:T(8,128)S(1)}, f32[2,64,128]{2,1,0:T(8,128)S(1)}, u32[]{:S(2)}, u32[]{:S(2)}) collective-permute-start(f32[2,64,128]{2,1,0:T(8,128)S(1)} %pad_maximum_fusion.1), channel_id=1, source_target_pairs={{0,8},{1,9},{2,10},{3,11},{4,12},{5,13},{6,14},{7,15},{8,0},{9,1},... | collective-permute-start | bytes 196616 | tf_op jit(solution)/shard_map/ppermute | solution.py:392
  18.6 6.1 %collective-permute-start.6 = (f32[2,64,128]{2,1,0:T(8,128)S(1)}, f32[2,64,128]{2,1,0:T(8,128)S(1)}, u32[]{:S(2)}, u32[]{:S(2)}) collective-permute-start(f32[2,64,128]{2,1,0:T(8,128)S(1)} %pad_maximum_fusion.2), channel_id=1, source_target_pairs={{0,4},{1,5},{2,6},{3,7},{4,0},{5,1},{6,2},{7,3},{8,12},{9,13},{10,... | collective-permute-start | bytes 196616 | tf_op jit(solution)/shard_map/ppermute | solution.py:392
  22.4 16.9 %collective-permute-start.10 = (f32[2048,128]{1,0:T(8,128)}, f32[2048,128]{1,0:T(8,128)}, u32[]{:S(2)}, u32[]{:S(2)}) collective-permute-start(f32[2048,128]{1,0:T(8,128)} %refs_1_.1), channel_id=1, source_target_pairs={{6,8},{8,6},{14,16},{16,14},{22,24},{24,22},{7,9},{9,7},{15,17},{1... | collective-permute-start | bytes 3145736 | tf_op jit(solution)/shard_map/ppermute | solution.py:416
  24.8 4.3 %collective-permute-start.9 = (f32[2,64,128]{2,1,0:T(8,128)S(1)}, f32[2,64,128]{2,1,0:T(8,128)S(1)}, u32[]{:S(2)}, u32[]{:S(2)}) collective-permute-start(f32[2,64,128]{2,1,0:T(8,128)S(1)} %pad_maximum_fusion.3), channel_id=1, source_target_pairs={{0,3},{1,2},{2,1},{3,0},{4,7},{5,6},{6,5},{7,4},{8,11},{9,10},{10,... | collective-permute-start | bytes 196616 | tf_op jit(solution)/shard_map/ppermute | solution.py:392
  26.6 2.5 %collective-permute-start.8 = (f32[2,64,128]{2,1,0:T(8,128)S(1)}, f32[2,64,128]{2,1,0:T(8,128)S(1)}, u32[]{:S(2)}, u32[]{:S(2)}) collective-permute-start(f32[2,64,128]{2,1,0:T(8,128)S(1)} %pad_maximum_fusion.3), channel_id=1, source_target_pairs={{0,2},{1,3},{2,0},{3,1},{4,6},{5,7},{6,4},{7,5},{8,10},{9,11},{10,... | collective-permute-start | bytes 196616 | tf_op jit(solution)/shard_map/ppermute | solution.py:392
  27.1 4.3 %collective-permute-start.7 = (f32[2,64,128]{2,1,0:T(8,128)S(1)}, f32[2,64,128]{2,1,0:T(8,128)S(1)}, u32[]{:S(2)}, u32[]{:S(2)}) collective-permute-start(f32[2,64,128]{2,1,0:T(8,128)S(1)} %pad_maximum_fusion.3), channel_id=1, source_target_pairs={{0,1},{1,0},{2,3},{3,2},{4,5},{5,4},{6,7},{7,6},{8,9},{9,8},{10,11... | collective-permute-start | bytes 196616 | tf_op jit(solution)/shard_map/ppermute | solution.py:392
  42.7 1.3 %collective-permute-start.11 = (f32[128,128]{1,0:T(8,128)S(1)}, f32[128,128]{1,0:T(8,128)S(1)}, u32[]{:S(2)}, u32[]{:S(2)}) collective-permute-start(f32[128,128]{1,0:T(8,128)S(1)} %get-tuple-element.35), channel_id=1, source_target_pairs={{0,2},{1,3},{2,0},{3,1},{4,6},{5,7},{6,4},{7,5},{8,10},{9,11},{10,... | collective-permute-start | bytes 196616 | tf_op jit(solution)/shard_map/ppermute | solution.py:392
  44.1 5.2 %collective-permute-start.14 = (f32[128,128]{1,0:T(8,128)S(1)}, f32[128,128]{1,0:T(8,128)S(1)}, u32[]{:S(2)}, u32[]{:S(2)}) collective-permute-start(f32[128,128]{1,0:T(8,128)S(1)} %add.246), channel_id=1, source_target_pairs={{0,5},{1,4},{2,7},{3,6},{4,1},{5,0},{6,3},{7,2},{8,13},{9,12},{10,... | collective-permute-start | bytes 196616 | tf_op jit(solution)/shard_map/ppermute | solution.py:392
  46.5 4.3 %collective-permute-start.13 = (f32[128,128]{1,0:T(8,128)S(1)}, f32[128,128]{1,0:T(8,128)S(1)}, u32[]{:S(2)}, u32[]{:S(2)}) collective-permute-start(f32[128,128]{1,0:T(8,128)S(1)} %add.246), channel_id=1, source_target_pairs={{0,4},{1,5},{2,6},{3,7},{4,0},{5,1},{6,2},{7,3},{8,12},{9,13},{10,... | collective-permute-start | bytes 196616 | tf_op jit(solution)/shard_map/ppermute | solution.py:392
  46.9 4.3 %collective-permute-start.12 = (f32[128,128]{1,0:T(8,128)S(1)}, f32[128,128]{1,0:T(8,128)S(1)}, u32[]{:S(2)}, u32[]{:S(2)}) collective-permute-start(f32[128,128]{1,0:T(8,128)S(1)} %add.246), channel_id=1, source_target_pairs={{0,1},{1,0},{2,3},{3,2},{4,5},{5,4},{6,7},{7,6},{8,9},{9,8},{10,11... | collective-permute-start | bytes 196616 | tf_op jit(solution)/shard_map/ppermute | solution.py:392
  51.2 6.9 %collective-permute-start.17 = (f32[128,128]{1,0:T(8,128)S(1)}, f32[128,128]{1,0:T(8,128)S(1)}, u32[]{:S(2)}, u32[]{:S(2)}) collective-permute-start(f32[128,128]{1,0:T(8,128)S(1)} %add_add_fusion), channel_id=1, source_target_pairs={{0,24},{1,25},{2,26},{3,27},{4,28},{5,29},{6,30},{7,31},{8,16},{9,... | collective-permute-start | bytes 196616 | tf_op jit(solution)/shard_map/ppermute | solution.py:392
  55.5 5.4 %collective-permute-start.16 = (f32[128,128]{1,0:T(8,128)S(1)}, f32[128,128]{1,0:T(8,128)S(1)}, u32[]{:S(2)}, u32[]{:S(2)}) collective-permute-start(f32[128,128]{1,0:T(8,128)S(1)} %add_add_fusion), channel_id=1, source_target_pairs={{0,16},{1,17},{2,18},{3,19},{4,20},{5,21},{6,22},{7,23},{8,24},{9,... | collective-permute-start | bytes 196616 | tf_op jit(solution)/shard_map/ppermute | solution.py:392
  55.5 5.4 %collective-permute-start.15 = (f32[128,128]{1,0:T(8,128)S(1)}, f32[128,128]{1,0:T(8,128)S(1)}, u32[]{:S(2)}, u32[]{:S(2)}) collective-permute-start(f32[128,128]{1,0:T(8,128)S(1)} %add_add_fusion), channel_id=1, source_target_pairs={{0,8},{1,9},{2,10},{3,11},{4,12},{5,13},{6,14},{7,15},{8,0},{9,1},... | collective-permute-start | bytes 196616 | tf_op jit(solution)/shard_map/ppermute | solution.py:392
